TPU v7x, 128 devices: a whole 4x4x4 slice. The times are simulated.
128 devices in a mesh: ctx: 16 (over y, x), head: 8 (over z, core).
Axes of the slice: x: 4, y: 4, z: 4, core: 2. Of those that a mesh axis runs over, the one named last changes fastest.
Arguments:
- queries: bfloat16 [1024, 64, 192], P(('ctx', 'head')), may hold values from -24 to 24
- latent_cache: bfloat16 [8192, 576], P('ctx'), may hold values from -8 to 8
- absorb_key: bfloat16 [64, 128, 512], P('head'), may hold values from -0.5 to 0.5
- absorb_value: bfloat16 [64, 512, 128], P('head'), may hold values from -6 to 6
- out_proj: bfloat16 [8192, 7168], P('head'), may hold values from -0.009765625 to 0.009765625
- residual: bfloat16 [1024, 7168], P(('ctx', 'head')), may hold values from -0.8984375 to 0.8984375
- norm_gain: float32 [7168], replicated, may hold values from 0.25 to 1.75
- routes: int32 [1024, 8], P(('ctx', 'head')), may hold values from 0 to 15, all different within a row; in each aligned block of 8 rows (0 to 7, 8 to 15, ...) at most 6 rows name the same one
- route_score: float32 [1024, 8], P(('ctx', 'head')), may hold values from 0.5 to 1
- response_doc: int32 [1024], replicated, may hold values from 0 to 7, never falling along the last dimension, each value on 1 to 512 neighbouring positions
- expert_gate: bfloat16 [16, 7168, 1024], P('ctx', None, 'head'), may hold values from -0.0625 to 0.0625
- expert_up: bfloat16 [16, 7168, 1024], P('ctx', None, 'head'), may hold values from -0.0625 to 0.0625
- expert_down: bfloat16 [16, 1024, 7168], P('ctx', 'head'), may hold values from -0.75 to 0.75
Outputs:
- layer_out: bfloat16 [1024, 7168], P(('ctx', 'head'))
Inputs may be any that keep to these rules, and one draw needn't show every extreme that they name: `routes`: each row names 8 different experts. In the rows of one device (8 aligned rows) no expert is named by more than 6 rows, a bound that some block reaches. `response_doc`: never falling; each response has 1 to 512 tokens, one exactly 512.
All inputs are finite; a program needn't handle non-finite values.
Results may differ from a plain program's by a relative error of at most 0.03.
Values may be sent and summed in bfloat16 or wider, within the bound.
No kernel may reach another device: no remote copies, remote signals or barrier semaphores. Data moves between devices by JAX's collectives and lax.ppermute only.
A program may use at most 128 MiB of HBM per device.

v0:
```python
import jax
import jax.numpy as jnp
from jax import lax
from jax.sharding import PartitionSpec as P

D = 7168
NOPE = 128
ROPE = 64
LAT = 512
VDIM = 128
EXPERTS = 16
TOP = 8
RESP = 1024
PROMPT = 7168


def visible_mask(row_pos, row_doc, key_pos, response_doc):
    key_doc = jnp.take(response_doc, jnp.clip(key_pos - PROMPT, 0, RESP - 1))
    inside = (key_doc[None, :] == row_doc[:, None]) & (key_pos[None, :] <= row_pos[:, None])
    return (key_pos[None, :] < PROMPT) | inside


def shards(
    queries,
    latent_cache,
    absorb_key,
    absorb_value,
    out_proj,
    residual,
    norm_gain,
    routes,
    route_score,
    response_doc,
    expert_gate,
    expert_up,
    expert_down,
):
    score_scale = (NOPE + ROPE) ** (-0.5)
    head_major = lax.all_to_all(queries, "head", split_axis=1, concat_axis=0, tiled=True)
    tok_rows = head_major.shape[0]
    local_heads = head_major.shape[1]
    query_rows_count = tok_rows * local_heads
    query_latent = jnp.einsum(
        "thn,hnl->thl", head_major[:, :, :NOPE], absorb_key, preferred_element_type=jnp.float32
    ).astype(jnp.bfloat16)
    query_rows = jnp.concatenate([query_latent, head_major[:, :, NOPE:]], axis=2).reshape(
        query_rows_count, LAT + ROPE
    )
    first_tok = lax.axis_index("ctx") * tok_rows
    token_ids = first_tok + jnp.arange(query_rows_count, dtype=jnp.int32) // local_heads
    row_pos = PROMPT + token_ids
    row_doc = jnp.take(response_doc, token_ids)
    key_block = lax.all_gather(latent_cache, "ctx", axis=0, tiled=True)
    run_max = jnp.full((query_rows_count,), -1e30, jnp.float32)
    key_pos = jnp.arange(key_block.shape[0], dtype=jnp.int32)
    visible = visible_mask(row_pos, row_doc, key_pos, response_doc)
    scores = (
        lax.dot_general(
            query_rows, key_block, (((1,), (1,)), ((), ())), preferred_element_type=jnp.float32
        )
        * score_scale
    )
    scores = jnp.where(visible, scores, -1e30)
    new_max = jnp.maximum(run_max, jnp.max(scores, axis=1))
    exp_scores = jnp.where(visible, jnp.exp(scores - new_max[:, None]), 0.0)
    run_sum = jnp.sum(exp_scores, axis=1)
    run_acc = jnp.dot(
        exp_scores.astype(jnp.bfloat16), key_block[:, :LAT], preferred_element_type=jnp.float32
    )
    run_max, run_sum, run_acc = (new_max, run_sum, run_acc)
    out_latent = (
        (run_acc / run_sum[:, None]).astype(jnp.bfloat16).reshape(tok_rows, local_heads, LAT)
    )
    head_out = jnp.einsum(
        "thl,hlv->thv", out_latent, absorb_value, preferred_element_type=jnp.float32
    ).astype(jnp.bfloat16)
    head_out = head_out.reshape(tok_rows, local_heads * VDIM)
    attended = lax.psum_scatter(
        jnp.dot(head_out, out_proj, preferred_element_type=jnp.float32).astype(jnp.bfloat16),
        "head",
        scatter_dimension=0,
        tiled=True,
    ).astype(jnp.float32)
    hidden_state = residual.astype(jnp.float32) + attended
    mean_square = jnp.mean(hidden_state * hidden_state, axis=1, keepdims=True)
    normed = (hidden_state * lax.rsqrt(mean_square + 1e-06) * norm_gain).astype(jnp.bfloat16)
    n_ctx = lax.axis_size("ctx")
    n_head = lax.axis_size("head")
    devices = n_ctx * n_head
    local_exp = expert_gate.shape[0]
    tok_dev = routes.shape[0]
    capacity = max(2, tok_dev * 3 // 4)
    flat_exp = routes.reshape(-1)
    onehot = (flat_exp[:, None] == jnp.arange(EXPERTS, dtype=jnp.int32)[None, :]).astype(jnp.int32)
    before = jnp.cumsum(onehot, axis=0) - onehot
    slot_index = jnp.sum(before * onehot, axis=1)
    dest_row = flat_exp * capacity + slot_index
    source = jnp.repeat(normed, TOP, axis=0)
    outgoing = jnp.zeros((EXPERTS * capacity, D), jnp.bfloat16).at[dest_row].set(source)
    outgoing = outgoing.reshape(n_ctx, local_exp, capacity, D)
    copies = jnp.broadcast_to(outgoing[:, None], (n_ctx, n_head, local_exp, capacity, D))
    arrived = lax.all_to_all(
        copies.reshape(devices, local_exp, capacity, D),
        ("ctx", "head"),
        split_axis=0,
        concat_axis=0,
        tiled=True,
    )
    gate_act = jnp.einsum(
        "slcd,ldf->slcf", arrived, expert_gate, preferred_element_type=jnp.float32
    )
    up_act = jnp.einsum("slcd,ldf->slcf", arrived, expert_up, preferred_element_type=jnp.float32)
    inner_act = (jax.nn.silu(gate_act) * up_act).astype(jnp.bfloat16)
    result = jnp.einsum(
        "slcf,lfd->slcd", inner_act, expert_down, preferred_element_type=jnp.float32
    ).astype(jnp.bfloat16)
    returned = lax.all_to_all(
        result, ("ctx", "head"), split_axis=0, concat_axis=0, tiled=True
    ).reshape(n_ctx, n_head, local_exp, capacity, D)
    combined = jnp.sum(returned.astype(jnp.float32), axis=1).reshape(EXPERTS * capacity, D)
    picked = jnp.take(combined, dest_row, axis=0).reshape(tok_dev, TOP, D)
    weight = 2.5 * route_score / jnp.sum(route_score, axis=1, keepdims=True)
    expert_mix = jnp.sum(weight[:, :, None] * picked, axis=1)
    return (hidden_state + expert_mix).astype(jnp.bfloat16)


def solution(mesh):
    in_specs = (
        P(("ctx", "head"), None, None),
        P("ctx", None),
        P("head", None, None),
        P("head", None, None),
        P("head", None),
        P(("ctx", "head"), None),
        P(),
        P(("ctx", "head"), None),
        P(("ctx", "head"), None),
        P(),
        P("ctx", None, "head"),
        P("ctx", None, "head"),
        P("ctx", "head", None),
    )
    out_specs = P(("ctx", "head"), None)
    return jax.shard_map(shards, mesh=mesh, in_specs=in_specs, out_specs=out_specs, check_vma=False)
```

profile of v0, /device:TPU:40, one launch (start us, length us, event | category | flops | bytes accessed | tf_op | source)
XLA Modules:
  0.0 639.0 jit_solution(15235417583545967726)
XLA Ops:
  6.5 0.7 all-gather.2.cloned.1.call-update
  7.3 1.8 copy.21
  9.1 5.4 all-to-all-start
  14.5 3.4 gather_fusion.1
  17.9 0.0 copy-start.3
  17.9 32.9 %gather_fusion = s32[8192]{0:T(1024)S(1)} fusion(s32[1024]{0:T(1024)S(1)} %copy-done.1, s32[8192]{0:T(1024)S(1)} %broadcast_clamp_fusion), kind=kCustom, calls=%fused_computation | custom fusion | bytes 98304 | tf_op jit(solution)/shard_map/jit(_take)/gather | solution.py:18
  50.9 0.0 all-to-all-done
  50.9 0.3 fusion.33
  51.2 0.1 pad_maximum_fusion
  51.3 43.3 %all-gather.2.cloned.1.call-done = bf16[8192,576]{0,1:T(8,128)(2,1)} async-done(((bf16[512,576]{0,1:T(8,128)(2,1)}), bf16[8192,576]{0,1:T(8,128)(2,1)}) %all-gather.2.cloned.1.call-update) | async-done | bytes 9437200 | tf_op jit(solution)/shard_map/all_gather | solution.py:53
  94.6 12.1 %fusion.2 = (f32[512]{0:T(512)S(1)}, f32[512,8192]{1,0:T(8,128)S(1)}) fusion(s32[512]{0:T(512)S(1)} %get-tuple-element.8, s32[512]{0:T(512)S(1)} %get-tuple-element.7, s32[8192]{0:T(1024)S(1)} %fusion.80, pred[8192]{0:T(1024)(128)(4,1)S(1)} %iota_compare_fusion.2, bf16[8192,576]{0,1:T(8,128)(2,1)} %all-gather.2.cloned.1.call-done, ...), kind=kOutput, calls=%fused_computation.10 | convolution fusion | flops 4861197824 | bytes 26851328 | tf_op jit(solution)/shard_map/dot_general | solution.py:58
  106.8 5.7 copy-done.2
  112.5 9.3 %fusion.8 = f32[512]{0:T(512)S(1)} fusion(f32[512,8192]{1,0:T(8,128)S(1)} %get-tuple-element.6, f32[512]{0:T(512)S(1)} %broadcast_maximum_fusion, s32[512]{0:T(512)S(1)} %get-tuple-element.8, s32[512]{0:T(512)S(1)} %get-tuple-element.7, s32[8192]{0:T(1024)S(1)} %fusion.80, pred[8192]{0:T(1024)(128)(4,1)S(1)} %iota_compare_fusion.2), kind=kLoop, calls=%fused_computation.17 | loop fusion | flops 37748224 | bytes 16826368 | tf_op jit(solution)/shard_map/reduce_sum | solution.py:66
  121.8 0.0 copy-start.4
  121.8 13.9 %fusion.34 = bf16[64,8,512]{2,1,0:T(8,128)(2,1)S(1)} fusion(bf16[8192,576]{0,1:T(8,128)(2,1)} %all-gather.2.cloned.1.call-done, f32[512,8192]{1,0:T(8,128)} %copy-done.2, f32[512]{0:T(512)S(1)} %broadcast_maximum_fusion, f32[512]{0:T(512)S(1)} %fusion.8, s32[512]{0:T(512)S(1)} %get-tuple-element.8, s32[8192]{0:T(1024)S(1)} %fusion.80, ...), kind=kOutput, calls=%fused_computation.37 | convolution fusion | flops 4333240320 | bytes 25739264 | tf_op jit(solution)/shard_map/dot_general | solution.py:67
  135.7 0.0 copy-done.4
  135.7 0.4 fusion.64
  136.1 0.0 copy-start.5
  136.1 0.0 copy-start.8
  136.1 8.9 %convolution_convert_fusion.1 = bf16[64,7168]{1,0:T(8,128)(2,1)} fusion(bf16[1024,7168]{1,0:T(8,128)(2,1)} %param.17, bf16[8,8,8,128]{3,2,1,0:T(8,128)(2,1)S(1)} %fusion.64), kind=kOutput, calls=%fused_computation.24 | convolution fusion | flops 939982848 | bytes 15728640 | tf_op jit(solution)/shard_map/dot_general | solution.py:79
  145.0 0.0 reduce-scatter.2.cloned.1.call-update
  145.1 0.1 reshape.229
  145.1 0.1 mul.80
  145.2 0.1 fusion.76
  145.3 0.1 reduce_window_sum.11
  145.4 0.2 select_reduce_fusion
  145.6 28.0 %reduce-scatter.2.cloned.1.call-done = bf16[8,7168]{1,0:T(8,128)(2,1)} async-done(((bf16[64,7168]{1,0:T(8,128)(2,1)}), bf16[8,7168]{1,0:T(8,128)(2,1)}) %reduce-scatter.2.cloned.1.call-update) | async-done | bytes 114704 | tf_op jit(solution)/shard_map/reduce_scatter | solution.py:78
  173.6 1.1 multiply_reduce_fusion
  174.7 1.0 multiply_convert_fusion
  175.7 2.3 scatter_custom_fusion
  177.9 1.5 broadcast_in_dim.68
  179.5 3.7 broadcast_in_dim.69
  183.2 0.0 copy-start.10
  183.2 172.8 %all_to_all.28 = bf16[128,1,6,7168]{3,2,1,0:T(8,128)(2,1)S(1)} all-to-all(bf16[128,1,6,7168]{3,2,1,0:T(8,128)(2,1)S(1)} %bitcast.111), channel_id=1, replica_groups=mesh['ctx'=16,'head'=8] {'ctx','head'}, dimensions={0} | all-to-all | bytes 22020096 | tf_op jit(solution)/shard_map/all_to_all | solution.py:102
  356.0 12.0 %fusion.39 = f32[128,1,6,128]{3,0,2,1:T(8,128)S(1)} fusion(bf16[1,7168,128]{2,1,0:T(8,128)(2,1)S(1)} %copy-done.10, bf16[128,1,6,7168]{3,2,1,0:T(8,128)(2,1)S(1)} %all_to_all.28), kind=kOutput, calls=%fused_computation.38 | convolution fusion | flops 1409286144 | bytes 13238272 | tf_op jit(solution)/shard_map/slcd,ldf->slcf/dot_general | solution.py:109
  368.0 11.9 %fusion.59 = bf16[128,6,128]{2,0,1:T(8,128)(2,1)S(1)} fusion(bf16[1,7168,128]{2,1,0:T(8,128)(2,1)S(1)} %copy-done.11, bf16[128,1,6,7168]{3,2,1,0:T(8,128)(2,1)S(1)} %all_to_all.28, f32[128,1,6,128]{3,0,2,1:T(8,128)S(1)} %fusion.39), kind=kOutput, calls=%fused_computation.42 | convolution fusion | flops 1409875968 | bytes 13434880 | tf_op jit(solution)/shard_map/slcd,ldf->slcf/dot_general | solution.py:112
  379.9 3.2 fusion.7
  383.1 10.2 %copy.27 = bf16[128,1,6,7168]{3,2,1,0:T(8,128)(2,1)} copy(bf16[128,1,6,7168]{3,0,2,1:T(8,128)(2,1)S(1)} %fusion.7) | data formatting | bytes 22020096 | tf_op jit(solution)/shard_map/convert_element_type | solution.py:116
  393.3 11.9 %all-to-all-start.2 = ((bf16[128,1,6,7168]{3,2,1,0:T(8,128)(2,1)}), bf16[128,1,6,7168]{3,2,1,0:T(8,128)(2,1)}, u32[]{:S(2)}, u32[]{:S(2)}) async-start(bf16[128,1,6,7168]{3,2,1,0:T(8,128)(2,1)} %copy.27), calls=%async_computation.3 | async-start | bytes 29360128 | tf_op jit(solution)/shard_map/all_to_all | solution.py:117
  405.2 0.1 reduce_sum.61
  405.3 0.1 reduce_sum.59
  405.4 0.1 multiply_divide_fusion
  405.5 204.7 %all-to-all-done.2 = bf16[128,1,6,7168]{3,2,1,0:T(8,128)(2,1)} async-done(((bf16[128,1,6,7168]{3,2,1,0:T(8,128)(2,1)}), bf16[128,1,6,7168]{3,2,1,0:T(8,128)(2,1)}, u32[]{:S(2)}, u32[]{:S(2)}) %all-to-all-start.2) | async-done | bytes 11010080 | tf_op jit(solution)/shard_map/all_to_all | solution.py:117
  610.2 10.7 %convert_reduce_fusion = f32[16,6,7168]{2,1,0:T(8,128)} fusion(bf16[16,8,6,7168]{3,2,1,0:T(8,128)(2,1)} %bitcast.110), kind=kLoop, calls=%fused_computation.4 | loop fusion | flops 10321920 | bytes 13762560 | tf_op jit(solution)/shard_map/reduce_sum | solution.py:120
  620.9 3.4 reshape.236
  624.3 4.9 gather_fusion.2
  629.2 2.1 fusion.19
  631.3 0.7 add_convert_fusion
  (34 shorter events, 0.2 us)
Async XLA Ops:
  6.5 373.3 %copy-start = (bf16[1,128,7168]{2,1,0:T(8,128)(2,1)S(1)}, bf16[1,128,7168]{2,1,0:T(8,128)(2,1)}, u32[]{:S(2)}) copy-start(bf16[1,128,7168]{2,1,0:T(8,128)(2,1)} %param.25) | copy-start | bytes 5505028
  6.5 11.4 %copy-start.1 = (s32[1024]{0:T(1024)S(1)}, s32[1024]{0:T(1024)}, u32[]{:S(2)}) copy-start(s32[1024]{0:T(1024)} %param.22) | copy-start | bytes 12292
  6.5 88.1 %all-gather.2.cloned.1.call-start = ((), (), s32[]{:S(2)}) async-start(), calls=%async_computation.4 | async-start | bytes 10027008 | tf_op jit(solution)/shard_map/all_gather | solution.py:53
  9.1 41.8 %all-to-all-start = ((bf16[8,64,192]{2,0,1:T(8,128)(2,1)}), bf16[8,64,192]{2,0,1:T(8,128)(2,1)S(1)}, u32[]{:S(2)}, u32[]{:S(2)}) async-start(bf16[8,64,192]{2,0,1:T(8,128)(2,1)} %copy.21), calls=%async_computation | async-start | bytes 524288 | tf_op jit(solution)/shard_map/all_to_all | solution.py:39
  14.5 159.1 %reduce-scatter.2.cloned.1.call-start = ((), (), s32[]{:S(2)}) async-start(), calls=%async_computation.5 | async-start | bytes 1032192 | tf_op jit(solution)/shard_map/reduce_scatter | solution.py:78
  17.9 33.0 %copy-start.3 = (bf16[8,128,512]{2,1,0:T(8,128)(2,1)S(1)}, bf16[8,128,512]{2,1,0:T(8,128)(2,1)}, u32[]{:S(2)}) copy-start(bf16[8,128,512]{2,1,0:T(8,128)(2,1)} %param.15) | copy-start | bytes 3145732
  106.8 5.7 copy-start.2
  121.8 13.9 %copy-start.4 = (bf16[8,512,128]{2,1,0:T(8,128)(2,1)S(1)}, bf16[8,512,128]{2,1,0:T(8,128)(2,1)}, u32[]{:S(2)}) copy-start(bf16[8,512,128]{2,1,0:T(8,128)(2,1)} %param.16) | copy-start | bytes 3145732
  136.1 8.9 %copy-start.7 = (s32[8,8]{1,0:T(8,128)S(1)}, s32[8,8]{1,0:T(8,128)}, u32[]{:S(2)}) copy-start(s32[8,8]{1,0:T(8,128)} %param.20) | copy-start | bytes 772
  136.1 37.5 %copy-start.5 = (bf16[8,7168]{1,0:T(8,128)(2,1)S(1)}, bf16[8,7168]{1,0:T(8,128)(2,1)}, u32[]{:S(2)}) copy-start(bf16[8,7168]{1,0:T(8,128)(2,1)} %param.18) | copy-start | bytes 344068
  136.1 38.6 %copy-start.8 = (f32[7168]{0:T(1024)S(1)}, f32[7168]{0:T(1024)}, u32[]{:S(2)}) copy-start(f32[7168]{0:T(1024)} %param.19) | copy-start | bytes 86020
  183.2 172.8 %copy-start.10 = (bf16[1,7168,128]{2,1,0:T(8,128)(2,1)S(1)}, bf16[1,7168,128]{2,1,0:T(8,128)(2,1)}, u32[]{:S(2)}) copy-start(bf16[1,7168,128]{2,1,0:T(8,128)(2,1)} %param.23) | copy-start | bytes 5505028
  356.0 12.0 %copy-start.11 = (bf16[1,7168,128]{2,1,0:T(8,128)(2,1)S(1)}, bf16[1,7168,128]{2,1,0:T(8,128)(2,1)}, u32[]{:S(2)}) copy-start(bf16[1,7168,128]{2,1,0:T(8,128)(2,1)} %param.24) | copy-start | bytes 5505028
  393.3 12.0 %copy-start.9 = (f32[8,8]{1,0:T(8,128)S(1)}, f32[8,8]{1,0:T(8,128)}, u32[]{:S(2)}) copy-start(f32[8,8]{1,0:T(8,128)} %param.21) | copy-start | bytes 772
  393.3 216.9 %all-to-all-start.2 = ((bf16[128,1,6,7168]{3,2,1,0:T(8,128)(2,1)}), bf16[128,1,6,7168]{3,2,1,0:T(8,128)(2,1)}, u32[]{:S(2)}, u32[]{:S(2)}) async-start(bf16[128,1,6,7168]{3,2,1,0:T(8,128)(2,1)} %copy.27), calls=%async_computation.3 | async-start | bytes 29360128 | tf_op jit(solution)/shard_map/all_to_all | solution.py:117
  624.3 7.0 %copy-start.6 = (bf16[8,7168]{1,0:T(8,128)(2,1)S(1)}, bf16[8,7168]{1,0:T(8,128)(2,1)}, u32[]{:S(2)}) copy-start(bf16[8,7168]{1,0:T(8,128)(2,1)} %reduce-scatter.2.cloned.1.call-done) | copy-start | bytes 344068
Sparse Core Ops, SparseCore 0:
  9.5 85.1 all-gather.1
  145.2 28.3 reduce-scatter.1
where the time goes:
time: 646 us; the launch traced here: 639 us
  waiting for transfers between devices  277 us (43%)
  blocking collectives  173 us (27%)
  local copies, waits for them, and re-layouts  70 us (11%)
  matrix products  62.7 us (10%)
  other arithmetic  25.6 us (4%)
  starting transfers between devices  17.4 us (3%)
  between operations  13.9 us (2%)
    all_to_all x1, waiting for transfers between devices, shards(): lax.all_to_all(result, ('ctx', 'head'), split_axis=0, concat_axis=0, tile...  205 us
    all_to_all x1, blocking collectives, shards(): lax.all_to_all(copies.reshape(devices, local_exp, capacity, D), ('ctx', '...  173 us
    all_gather x1, waiting for transfers between devices, shards(): key_block = lax.all_gather(latent_cache, 'ctx', axis=0, tiled=True)  43.3 us
    gather x1, local copies, waits for them, and re-layouts, visible_mask(): key_doc = jnp.take(response_doc, jnp.clip(key_pos - PROMPT, 0, RESP - 1))  32.9 us
    reduce_scatter x1, waiting for transfers between devices, shards(): lax.psum_scatter(jnp.dot(head_out, out_proj, preferred_element_type=jnp.f...  28 us
    dot_general x1, matrix products, shards(): jnp.dot(exp_scores.astype(jnp.bfloat16), key_block[:, :LAT], preferred_el...  13.9 us
  transfers between devices with their start and end apart: 4, of which 3 were waited for; matrix products, arithmetic and copies ran while one was open for 6% of the time, Pallas kernels for 0%

commit v1 on v0

v1 whole, which is shorter than its diff:
```python
import functools

import jax
import jax.numpy as jnp
from jax import lax
from jax.experimental import pallas as pl
from jax.experimental.pallas import tpu as pltpu
from jax.sharding import Mesh
from jax.sharding import PartitionSpec as P

D = 7168
NOPE = 128
ROPE = 64
LAT = 512
VDIM = 128
EXPERTS = 16
TOP = 8
RESP = 1024
PROMPT = 7168
NX = 4
NY = 4
NZ = 4
GRP = 8
BLK = 8
CAP = 6
KEYS = 2048
HALF = 256
ROWS = 256
CHUNK = D // NZ
SLOTS = NZ * CAP
EROWS = 16 * SLOTS
LOG2E = 1.4426950408889634
BF = jnp.bfloat16
F32 = jnp.float32
HIDE = -1e30


def shift(a, axis, n, d):
    return lax.ppermute(a, axis, [(i, (i + d) % n) for i in range(n)])


def split3(v):
    hi = v.astype(BF).astype(F32)
    mid = (v - hi).astype(BF).astype(F32)
    low = (v - hi - mid).astype(BF).astype(F32)
    return hi, mid, low


def attention_kernel(
    pos_ref, q_ref, first_ref, last_ref, c0, c1, c2, c3, s1, s2, s3, ak_ref, av_ref, o_ref, kv, rp, st
):
    h = pl.program_id(0)

    @pl.when(h == 0)
    def _():
        kv[pl.ds(pl.multiple_of(pos_ref[0], HALF), 2 * HALF), :] = c0[...]
        for i, piece in enumerate((c1, c2, c3, s1, s2, s3)):
            kv[pl.ds(pl.multiple_of(pos_ref[1 + i], HALF), HALF), :] = piece[...]
        r = kv[:, LAT:]
        rp[...] = jnp.concatenate([r, r], axis=1)
        st[...] = jnp.zeros_like(st)

    nope = q_ref[:, pl.ds(pl.multiple_of(h * NOPE, NOPE), NOPE)]
    q_lat = jnp.dot(nope, ak_ref[0], preferred_element_type=F32).astype(BF)
    pair = q_ref[:, pl.ds(pl.multiple_of(GRP * NOPE + (h // 2) * 128, 128), 128)].astype(F32)
    lane = lax.broadcasted_iota(jnp.int32, (ROWS, 128), 1)
    rope = jnp.where(lane // ROPE == h % 2, pair, 0.0).astype(BF)
    nt = (((1,), (1,)), ((), ()))
    step = 512
    parts = []
    for j in range(0, KEYS, step):
        s = lax.dot_general(q_lat, kv[j : j + step, :LAT], nt, preferred_element_type=F32)
        s = s + lax.dot_general(rope, rp[j : j + step, :], nt, preferred_element_type=F32)
        if j >= KEYS // 2:
            col = lax.broadcasted_iota(jnp.int32, (ROWS, step), 1) + (j - KEYS // 2)
            s = jnp.where((col >= first_ref[...]) & (col <= last_ref[...]), s, HIDE)
        parts.append(s)
    top = jnp.max(parts[0], axis=1, keepdims=True)
    for s in parts[1:]:
        top = jnp.maximum(top, jnp.max(s, axis=1, keepdims=True))
    scale = LOG2E * (NOPE + ROPE) ** (-0.5)
    total = jnp.zeros((ROWS, 1), F32)
    acc = jnp.zeros((ROWS, LAT), F32)
    for i, s in enumerate(parts):
        p = jnp.exp2((s - top) * scale)
        total = total + jnp.sum(p, axis=1, keepdims=True)
        acc = acc + jnp.dot(p.astype(BF), kv[i * step : (i + 1) * step, :LAT], preferred_element_type=F32)
    lat = (acc / total).astype(BF)
    o_ref[:, pl.ds(pl.multiple_of(h * VDIM, VDIM), VDIM)] = jnp.dot(
        lat, av_ref[0], preferred_element_type=F32
    ).astype(BF)
    add = jnp.zeros((ROWS, 128), F32)
    for i, v in enumerate(split3(top) + split3(total)):
        add = add + jnp.where(lane == i * GRP + h, v, 0.0)
    st[...] += add

    @pl.when(h == GRP - 1)
    def _():
        o_ref[:, GRP * VDIM :] = st[...].astype(BF)


def attention(place, q, first, last, pieces, absorb_key, absorb_value):
    whole = lambda a: pl.BlockSpec(a.shape, lambda h: (0,) * a.ndim)
    return pl.pallas_call(
        attention_kernel,
        grid=(GRP,),
        out_shape=jax.ShapeDtypeStruct((ROWS, GRP * VDIM + 128), BF),
        in_specs=[pl.BlockSpec(memory_space=pltpu.SMEM), whole(q), whole(first), whole(last)]
        + [whole(p) for p in pieces]
        + [
            pl.BlockSpec((1, NOPE, LAT), lambda h: (h, 0, 0)),
            pl.BlockSpec((1, LAT, VDIM), lambda h: (h, 0, 0)),
        ],
        out_specs=pl.BlockSpec((ROWS, GRP * VDIM + 128), lambda h: (0, 0)),
        scratch_shapes=[
            pltpu.VMEM((KEYS, LAT + ROPE), BF),
            pltpu.VMEM((KEYS, 2 * ROPE), BF),
            pltpu.VMEM((ROWS, 128), F32),
        ],
        compiler_params=pltpu.CompilerParams(vmem_limit_bytes=40 * 2**20),
        cost_estimate=pl.CostEstimate(flops=9 * 10**9, bytes_accessed=6 * 10**6, transcendentals=4 * 10**6),
        name="attention",
    )(place, q, first, last, *pieces, absorb_key, absorb_value)


def gate_up_kernel(z_ref, x_ref, *refs):
    pieces, (o_ref, w, sem) = refs[:8], refs[8:]
    copies = [pltpu.make_async_copy(p, w.at[i], sem.at[i]) for i, p in enumerate(pieces)]
    for c in copies:
        c.start()
    for i, c in enumerate(copies):
        c.wait()
        d, k = i // 2, i % 2
        part = jnp.dot(x_ref[...], w[i], preferred_element_type=F32).astype(BF)
        o_ref[lax.rem(z_ref[0] + NZ - d, NZ), :, k * 256 : (k + 1) * 256] = part


def gate_up(z, x, pieces):
    return pl.pallas_call(
        gate_up_kernel,
        out_shape=jax.ShapeDtypeStruct((NZ, EROWS, 512), BF),
        in_specs=[pl.BlockSpec(memory_space=pltpu.SMEM), pl.BlockSpec(memory_space=pltpu.VMEM)]
        + [pl.BlockSpec(memory_space=pl.ANY)] * 8,
        out_specs=pl.BlockSpec(memory_space=pltpu.VMEM),
        scratch_shapes=[pltpu.VMEM((8, CHUNK, 256), BF), pltpu.SemaphoreType.DMA((8,))],
        compiler_params=pltpu.CompilerParams(vmem_limit_bytes=40 * 2**20),
        cost_estimate=pl.CostEstimate(flops=3 * 10**9, bytes_accessed=10 * 10**6, transcendentals=0),
        name="gate_up",
    )(z, x, *pieces)


def down_kernel(i0, i1, i2, i3, *refs):
    pieces, (o_ref, w, sem) = refs[:8], refs[8:]
    copies = [
        pltpu.make_async_copy(p, w.at[pl.ds(i * 128, 128)], sem.at[i]) for i, p in enumerate(pieces)
    ]
    for c in copies:
        c.start()
    inner = jnp.concatenate([i0[...], i1[...], i2[...], i3[...]], axis=1)
    for c in copies:
        c.wait()
    for j in range(0, CHUNK, 256):
        o_ref[:, j : j + 256] = jnp.dot(inner, w[:, j : j + 256], preferred_element_type=F32).astype(BF)


def down(inners, pieces):
    return pl.pallas_call(
        down_kernel,
        out_shape=jax.ShapeDtypeStruct((EROWS, CHUNK), BF),
        in_specs=[pl.BlockSpec(memory_space=pltpu.VMEM)] * 4 + [pl.BlockSpec(memory_space=pl.ANY)] * 8,
        out_specs=pl.BlockSpec(memory_space=pltpu.VMEM),
        scratch_shapes=[pltpu.VMEM((1024, CHUNK), BF), pltpu.SemaphoreType.DMA((8,))],
        compiler_params=pltpu.CompilerParams(vmem_limit_bytes=40 * 2**20),
        cost_estimate=pl.CostEstimate(flops=14 * 10**8, bytes_accessed=6 * 10**6, transcendentals=0),
        name="down",
    )(*inners, *pieces)


def after(arrays, token):
    out = lax.optimization_barrier(tuple(arrays) + (token,))
    return out[:-1]


def absolute(rel, z):
    line = jnp.stack([rel[3], rel[2], rel[1], rel[0], rel[3], rel[2], rel[1]])
    return lax.dynamic_slice_in_dim(line, 3 - z, NZ, axis=0)


def shards(
    queries,
    latent_cache,
    absorb_key,
    absorb_value,
    out_proj,
    residual,
    norm_gain,
    routes,
    route_score,
    response_doc,
    expert_gate,
    expert_up,
    expert_down,
):
    x, y, z, k = (lax.axis_index(a) for a in ("x", "y", "z", "core"))

    with jax.named_scope("cache_gather"):
        half = lax.dynamic_slice_in_dim(latent_cache, k * HALF, HALF, axis=0)
        mine = [shift(half, "x", NX, d) for d in range(1, NX)]
        other = [shift(m, "core", 2, 1) for m in mine]

    with jax.named_scope("query_exchange"):
        nope = queries[:, :, :NOPE].reshape(BLK, NZ, 2, GRP * NOPE)
        rope = queries[:, :, NOPE:].reshape(BLK, NZ, 2, GRP * ROPE)
        q = jnp.concatenate([nope, rope], axis=3).transpose(2, 1, 0, 3)
        q = jnp.broadcast_to(q[None], (NY, 2, NZ, BLK, GRP * (NOPE + ROPE)))
        q = q.reshape(NY * 2 * NZ, BLK, GRP * (NOPE + ROPE))
        q = lax.all_to_all(q, ("y", "core", "z"), split_axis=0, concat_axis=0, tiled=True)
        q = q.reshape(ROWS, GRP * (NOPE + ROPE))

    with jax.named_scope("gate_up_weights"):
        gates = expert_gate[0].reshape(NZ, CHUNK, 128)
        ups = expert_up[0].reshape(NZ, CHUNK, 128)
        downs = expert_down[0]
        gu_out, dn_out = [], []
        for d in range(NZ):
            to = (z + d) % NZ
            g = lax.dynamic_index_in_dim(gates, to, 0, keepdims=False)
            u = lax.dynamic_index_in_dim(ups, to, 0, keepdims=False)
            gu_out.append(jnp.concatenate([g, u], axis=1))
            dn_out.append(lax.dynamic_slice_in_dim(downs, to * CHUNK, CHUNK, axis=1))
        sent = after(gu_out[1:], q)
        gu = [gu_out[0]] + [shift(w, "z", NZ, d + 1) for d, w in enumerate(sent)]

    with jax.named_scope("residual_exchange"):
        score_hi = lax.reduce_precision(route_score, 8, 7)
        score_mid = lax.reduce_precision(route_score - score_hi, 8, 7)
        score_low = route_score - score_hi - score_mid
        info = jnp.concatenate(
            [routes.astype(BF)]
            + [s.astype(BF) for s in (score_hi, score_mid, score_low)]
            + [jnp.zeros((BLK, 128 - 4 * TOP), BF)],
            axis=1,
        )
        rel = []
        for d in range(NZ):
            part = lax.dynamic_slice_in_dim(residual, ((z + d) % NZ) * CHUNK, CHUNK, axis=1)
            part = jnp.concatenate([part, info], axis=1)
            rel.append(shift(part, "z", NZ, d) if d else part)
        owned = absolute(rel, z).reshape(NZ * BLK, CHUNK + 128)
        res = owned[:, :CHUNK].astype(F32)

    with jax.named_scope("routing"):
        tokens = NZ * BLK
        route = owned[:, CHUNK : CHUNK + TOP].astype(jnp.int32)
        score = owned[:, CHUNK + TOP : CHUNK + 4 * TOP].astype(F32).reshape(tokens, 3, TOP)
        score = score[:, 0] + score[:, 1] + score[:, 2]
        weight = 2.5 * score / jnp.sum(score, axis=1, keepdims=True)
        experts = jnp.arange(EXPERTS, dtype=jnp.int32)
        hit = route[:, :, None] == experts
        named = jnp.any(hit, axis=1).astype(jnp.int32).reshape(NZ, BLK, EXPERTS)
        mix = jnp.sum(jnp.where(hit, weight[:, :, None], 0.0), axis=1)
        rank = jnp.cumsum(named, axis=1) - named
        slot = jnp.arange(NZ, dtype=jnp.int32)[:, None, None] * CAP + rank
        slot = jnp.where(named > 0, slot, -1).reshape(tokens, EXPERTS)
        place = slot[:, :, None] == jnp.arange(SLOTS, dtype=jnp.int32)
        pick = place.reshape(tokens, EROWS).astype(BF)
        blend = jnp.where(place, mix[:, :, None], 0.0).reshape(tokens, EROWS)

    with jax.named_scope("attention"):
        doc = lax.dynamic_index_in_dim(response_doc.reshape(NY, NX, NZ, 2, BLK), x, 1, keepdims=False)
        doc = doc.transpose(0, 2, 1, 3).reshape(ROWS)
        ids = jnp.arange(RESP, dtype=jnp.int32).reshape(NY, NX, NZ, 2, BLK)
        ids = lax.dynamic_index_in_dim(ids, x, 1, keepdims=False).transpose(0, 2, 1, 3).reshape(ROWS)
        start = jnp.sum((response_doc[None, :] < doc[:, None]).astype(jnp.int32), axis=1)
        far = jnp.int32(1 << 20)
        first = jnp.where(y == NY - 1, start, -far)[:, None]
        last = jnp.where(y == NY - 1, ids, far)[:, None]
        at = [x * 512]
        for core in (k, 1 - k):
            at += [((x - d) % NX) * 512 + core * HALF for d in range(1, NX)]
        place_of = jnp.stack(at).astype(jnp.int32)
        out = attention(place_of, q, first, last, [latent_cache] + mine + other, absorb_key, absorb_value)

    with jax.named_scope("combine"):
        out = out.reshape(NY, 64, GRP * VDIM + 128)
        out = lax.all_to_all(out, "y", split_axis=0, concat_axis=0, tiled=True)
        stat = out[:, :, GRP * VDIM : GRP * VDIM + 6 * GRP].astype(F32).reshape(NY, 64, 6, GRP)
        top = stat[:, :, 0] + stat[:, :, 1] + stat[:, :, 2]
        total = stat[:, :, 3] + stat[:, :, 4] + stat[:, :, 5]
        scale = LOG2E * (NOPE + ROPE) ** (-0.5)
        share = total * jnp.exp2((top - jnp.max(top, axis=0, keepdims=True)) * scale)
        share = share / jnp.sum(share, axis=0, keepdims=True)
        heads = out[:, :, : GRP * VDIM].astype(F32).reshape(NY, 64, GRP, VDIM)
        head_out = jnp.sum(heads * share[..., None], axis=0).astype(BF).reshape(64, GRP * VDIM)

    with jax.named_scope("out_projection"):
        part = jnp.dot(head_out, out_proj, preferred_element_type=F32).astype(BF)
        part = part.reshape(2, NZ * BLK, NZ, CHUNK).transpose(0, 2, 1, 3).reshape(8, NZ * BLK, CHUNK)
        part = lax.all_to_all(part, ("core", "z"), split_axis=0, concat_axis=0, tiled=True)
        hidden = res + jnp.sum(part.astype(F32), axis=0)

    with jax.named_scope("down_weights"):
        sent = after(dn_out[1:], hidden)
        dn = [dn_out[0]] + [shift(w, "z", NZ, d + 1) for d, w in enumerate(sent)]
        gu = [gu[0]] + list(after(gu[1:], hidden))
        gu_other = [shift(w, "core", 2, 1) for w in gu]

    with jax.named_scope("norm"):
        square = jnp.sum(hidden * hidden, axis=1, keepdims=True)
        square = square + sum(shift(square, "z", NZ, d) for d in range(1, NZ))
        normed = (hidden * lax.rsqrt(square / D + 1e-6) * lax.dynamic_slice_in_dim(norm_gain, z * CHUNK, CHUNK)).astype(BF)

    with jax.named_scope("dispatch"):
        rows = lax.dot_general(pick, normed, (((0,), (0,)), ((), ())), preferred_element_type=F32).astype(BF)
        rows = rows.reshape(EXPERTS, SLOTS, CHUNK)
        rows = lax.all_to_all(rows, ("y", "x"), split_axis=0, concat_axis=0, tiled=True)
        rows = rows.reshape(EROWS, CHUNK)

    with jax.named_scope("experts"):
        dn = [dn[0]] + list(after(dn[1:], rows))
        dn_other = [shift(w, "core", 2, 1) for w in dn]
        gu_pieces = [w for pair in zip(gu, gu_other) for w in pair]
        part = gate_up(z.reshape(1), rows, gu_pieces)
        part = lax.all_to_all(part, "z", split_axis=0, concat_axis=0, tiled=True)
        act = jnp.sum(part.astype(F32), axis=0).reshape(EROWS, 2, 2, 128)
        inner = (jax.nn.silu(act[:, :, 0]) * act[:, :, 1]).astype(BF).reshape(EROWS, 256)
        inners = [inner] + [shift(inner, "z", NZ, d) for d in range(1, NZ)]
        result = down(inners, [w for pair in zip(dn, dn_other) for w in pair])

    with jax.named_scope("return"):
        back = lax.all_to_all(
            result.reshape(EXPERTS, SLOTS, CHUNK), ("y", "x"), split_axis=0, concat_axis=0, tiled=True
        ).reshape(EROWS, CHUNK)
        mixed = jnp.dot(blend, back.astype(F32), precision=lax.Precision.HIGHEST, preferred_element_type=F32)
        done = (hidden + mixed).astype(BF).reshape(NZ, BLK, CHUNK)
        done = lax.all_to_all(done, "z", split_axis=0, concat_axis=0, tiled=True)
        return done.transpose(1, 0, 2).reshape(BLK, D)


def solution(mesh):
    fine = Mesh(mesh.devices.reshape(NY, NX, NZ, 2), ("y", "x", "z", "core"))
    ctx, head = ("y", "x"), ("z", "core")
    both = ctx + head
    in_specs = (
        P(both, None, None),
        P(ctx, None),
        P(head, None, None),
        P(head, None, None),
        P(head, None),
        P(both, None),
        P(),
        P(both, None),
        P(both, None),
        P(),
        P(ctx, None, head),
        P(ctx, None, head),
        P(ctx, head, None),
    )
    return jax.shard_map(shards, mesh=fine, in_specs=in_specs, out_specs=P(both, None), check_vma=False)
```

time: 646 us -> 308 us (0.48)
  blocking collectives: 173 us -> 9.62 us
  waiting for transfers between devices: 277 us -> 130 us
  matrix products: 62.7 us -> 10.3 us
  starting transfers between devices: 17.4 us -> 65.6 us
  Pallas kernels: 0 us -> 34.6 us
  local copies, waits for them, and re-layouts: 70 us -> 42.4 us
  other arithmetic: 25.6 us -> 9.87 us
  between operations: 13.9 us -> 0.68 us
    all_to_all x1, blocking collectives: 173 us -> 9.62 us  [shards(): done = lax.all_to_all(done, 'z', split_axis=0, concat_axis=0, tiled=True)]
    all_to_all x2 -> x6, waiting for transfers between devices: 205 us -> 42.6 us  [the longest x1 18.7 us: shards(): lax.all_to_all(result.reshape(EXPERTS, SLOTS, CHUNK), ('y', 'x'), split_a...]
    ppermute x0 -> x29, waiting for transfers between devices: none -> 87.3 us  [shift(): return lax.ppermute(a, axis, [(i, (i + d) % n) for i in range(n)])]
    dot_general x8 -> x3, matrix products: 62.7 us -> 10.3 us  [the longest x1 7.89 us: shards(): part = jnp.dot(head_out, out_proj, preferred_element_type=F32).astype(BF)]
    all_gather x1 -> x0, waiting for transfers between devices: 43.3 us -> none  [shards(): key_block = lax.all_gather(latent_cache, 'ctx', axis=0, tiled=True)]
    gather x3 -> x0, local copies, waits for them, and re-layouts: 41.1 us -> none  [the longest x1 32.9 us: visible_mask(): key_doc = jnp.take(response_doc, jnp.clip(key_pos - PROMPT, 0, RESP - 1))]
    pallas_call x0 -> x3, Pallas kernels: none -> 34.6 us  [the longest x1 19.5 us: attention(): pl.pallas_call(attention_kernel, grid=(GRP,), out_shape=jax.ShapeDtypeStr...]
    ppermute x0 -> x29, starting transfers between devices: none -> 30 us  [shift(): return lax.ppermute(a, axis, [(i, (i + d) % n) for i in range(n)])]
  transfers between devices with their start and end apart: 4 -> 35, of which waited for: 3 -> 16; matrix products, arithmetic and copies ran while one was open for 6% -> 11% of each run, Pallas kernels for 0% -> 0%
where the time goes in v1:
time: 308 us; the launch traced here: 303 us
  waiting for transfers between devices  130 us (42%)
  starting transfers between devices  65.6 us (21%)
  local copies, waits for them, and re-layouts  42.4 us (14%)
  Pallas kernels  34.6 us (11%)
  matrix products  10.3 us (3%)
  other arithmetic  9.87 us (3%)
  blocking collectives  9.62 us (3%)
    ppermute x29, waiting for transfers between devices, shift(): return lax.ppermute(a, axis, [(i, (i + d) % n) for i in range(n)])  87.3 us
    ppermute x29, starting transfers between devices, shift(): return lax.ppermute(a, axis, [(i, (i + d) % n) for i in range(n)])  30 us
    pallas_call x1, Pallas kernels, attention(): pl.pallas_call(attention_kernel, grid=(GRP,), out_shape=jax.ShapeDtypeStr...  19.5 us
    all_to_all x1, waiting for transfers between devices, shards(): lax.all_to_all(result.reshape(EXPERTS, SLOTS, CHUNK), ('y', 'x'), split_a...  18.7 us
    unnamed x70, local copies, waits for them, and re-layouts  18 us
    all_to_all x1, blocking collectives, shards(): done = lax.all_to_all(done, 'z', split_axis=0, concat_axis=0, tiled=True)  9.62 us
    pallas_call x1, Pallas kernels, gate_up(): pl.pallas_call(gate_up_kernel, out_shape=jax.ShapeDtypeStruct((NZ, EROWS,...  9.44 us
    all_to_all x1, waiting for transfers between devices, shards(): out = lax.all_to_all(out, 'y', split_axis=0, concat_axis=0, tiled=True)  8.41 us
  transfers between devices with their start and end apart: 35, of which 16 were waited for; matrix products, arithmetic and copies ran while one was open for 11% of the time, Pallas kernels for 0%

profile of v1, /device:TPU:40, one launch (start us, length us, event | category | flops | bytes accessed | tf_op | source)
XLA Modules:
  0.0 303.0 jit_solution(13737752135179573726)
XLA Ops:
  0.0 1.4 copy.131.c0
  2.2 1.5 collective-permute-start.3
  3.7 2.7 collective-permute-start.4
  6.4 1.4 collective-permute-start.5
  9.3 8.1 %all-to-all-start = ((bf16[32,8,1536]{2,1,0:T(8,128)(2,1)}), bf16[32,8,1536]{2,1,0:T(8,128)(2,1)S(1)}, u32[]{:S(2)}, u32[]{:S(2)}) async-start(bf16[32,8,1536]{2,1,0:T(8,128)(2,1)} %bitcast.13), calls=%async_computation | async-start | bytes 1572864 | tf_op jit(solution)/shard_map/query_exchange/all_to_all | solution.py:217
  19.6 2.4 collective-permute-start.1
  22.6 3.2 %dynamic-slice_bitcast_fusion.4 = (bf16[1792,128]{1,0:T(8,128)(2,1)S(1)}, bf16[1792,128]{1,0:T(8,128)(2,1)S(1)}, bf16[1792,128]{1,0:T(8,128)(2,1)S(1)}, bf16[179...) fusion(bf16[4,1792,128]{2,1,0:T(8,128)(2,1)} %bitcast.144, ...), kind=kLoop, calls=%fused_computation.18 | loop fusion | bytes 7340048 | tf_op jit(solution)/shard_map/gate_up_weights/jit(dynamic_index_in_dim)/squeeze | solution.py:228
  29.6 1.4 concatenate.34
  33.9 1.8 collective-permute-start.2
  35.8 2.3 collective-permute-done.2
  46.2 19.5 %attention.1 = bf16[256,1152]{1,0:T(8,128)(2,1)} custom-call(s32[7]{0:T(128)S(1)} %stack.54.pos_ref, bf16[256,1536]{1,0:T(8,128)(2,1)S(1)} %bitcast.141, s32[256,1]{1,0:T(8,128)S(1)} %copy.129.first_ref, s32[256,1]{1,0:T(8,128)S(1)} %select_n.178.last_ref, bf16[512,576]{1,0:T(8,128)(2,1)S(1)} %copy.131.c0, bf16[256,576]{1,0:T(8,128)(2,1)S(1)} %collective-permute-done.3.c1, ...), custom_call_target="tpu_custom_call" | custom-call | flops 8999999488 | bytes 6000000 | tf_op jit(solution)/shard_map/attention/attention/pallas_call | solution.py:104
  65.7 4.8 %all-to-all-start.1 = ((bf16[4,64,1152]{2,1,0:T(8,128)(2,1)}), bf16[4,64,1152]{2,1,0:T(8,128)(2,1)S(1)}, u32[]{:S(2)}, u32[]{:S(2)}) async-start(bf16[4,64,1152]{2,1,0:T(8,128)(2,1)} %bitcast.20), calls=%async_computation.1 | async-start | bytes 1179648 | tf_op jit(solution)/shard_map/combine/all_to_all | solution.py:286
  71.1 8.4 %all-to-all-done.1 = bf16[4,64,1152]{2,1,0:T(8,128)(2,1)S(1)} async-done(((bf16[4,64,1152]{2,1,0:T(8,128)(2,1)}), bf16[4,64,1152]{2,1,0:T(8,128)(2,1)S(1)}, u32[]{:S(2)}, u32[]{:S(2)}) %all-to-all-start.1) | async-done | bytes 589856 | tf_op jit(solution)/shard_map/combine/all_to_all | solution.py:286
  80.6 7.9 %convolution_convert_fusion = bf16[64,7168]{1,0:T(8,128)(2,1)S(1)} fusion(bf16[1024,7168]{1,0:T(8,128)(2,1)} %param.17, bf16[64,1024]{0,1:T(8,128)(2,1)S(1)} %copy.148), kind=kOutput, calls=%fused_computation | convolution fusion | flops 939982848 | bytes 15728640 | tf_op jit(solution)/shard_map/out_projection/dot_general | solution.py:297
  90.2 6.0 %all-to-all-start.2 = ((bf16[8,32,1792]{2,1,0:T(8,128)(2,1)}), bf16[8,32,1792]{2,1,0:T(8,128)(2,1)S(1)}, u32[]{:S(2)}, u32[]{:S(2)}) async-start(bf16[8,32,1792]{2,1,0:T(8,128)(2,1)} %bitcast.26), calls=%async_computation.2 | async-start | bytes 1835008 | tf_op jit(solution)/shard_map/out_projection/all_to_all | solution.py:299
  96.6 1.5 collective-permute-start.13
  98.9 2.3 collective-permute-start.15
  101.3 7.7 %all-to-all-done.2 = bf16[8,32,1792]{2,1,0:T(8,128)(2,1)S(1)} async-done(((bf16[8,32,1792]{2,1,0:T(8,128)(2,1)}), bf16[8,32,1792]{2,1,0:T(8,128)(2,1)S(1)}, u32[]{:S(2)}, u32[]{:S(2)}) %all-to-all-start.2) | async-done | bytes 917536 | tf_op jit(solution)/shard_map/out_projection/all_to_all | solution.py:299
  109.2 1.3 collective-permute-start.11
  111.3 36.8 %collective-permute-done.11 = f32[32,1]{0,1:T(1,128)S(1)} collective-permute-done((f32[32,1]{0,1:T(1,128)S(1)}, f32[32,1]{0,1:T(1,128)S(1)}, u32[]{:S(2)}, u32[]{:S(2)}) %collective-permute-start.11) | collective-permute-done | bytes 160 | tf_op jit(solution)/shard_map/norm/ppermute | solution.py:39
  148.1 1.4 collective-permute-start.10
  149.7 3.5 %collective-permute-done.10 = f32[32,1]{0,1:T(1,128)S(1)} collective-permute-done((f32[32,1]{0,1:T(1,128)S(1)}, f32[32,1]{0,1:T(1,128)S(1)}, u32[]{:S(2)}, u32[]{:S(2)}) %collective-permute-start.10) | collective-permute-done | bytes 160 | tf_op jit(solution)/shard_map/norm/ppermute | solution.py:39
  153.2 1.7 convolution_convert_fusion.1
  154.9 5.0 %all-to-all-start.3 = ((bf16[16,24,1792]{2,1,0:T(8,128)(2,1)}), bf16[16,24,1792]{2,1,0:T(8,128)(2,1)S(1)}, u32[]{:S(2)}, u32[]{:S(2)}) async-start(bf16[16,24,1792]{2,1,0:T(8,128)(2,1)} %bitcast.142), calls=%async_computation.3 | async-start | bytes 2752512 | tf_op jit(solution)/shard_map/dispatch/all_to_all | solution.py:316
  162.3 1.4 collective-permute-done.12.refs_1_
  164.6 1.7 collective-permute-done.16.refs_3_
  169.1 7.8 %all-to-all-done.3 = bf16[16,24,1792]{2,1,0:T(8,128)(2,1)S(1)} async-done(((bf16[16,24,1792]{2,1,0:T(8,128)(2,1)}), bf16[16,24,1792]{2,1,0:T(8,128)(2,1)S(1)}, u32[]{:S(2)}, u32[]{:S(2)}) %all-to-all-start.3) | async-done | bytes 1376288 | tf_op jit(solution)/shard_map/dispatch/all_to_all | solution.py:316
  181.6 9.4 %gate_up.1 = bf16[4,384,512]{2,1,0:T(8,128)(2,1)} custom-call(s32[1]{0:T(128)} %bitcast.32.z_ref, bf16[384,1792]{1,0:T(8,128)(2,1)S(1)} %bitcast.140, bf16[1792,256]{1,0:T(8,128)(2,1)S(1)} %pad_maximum_fusion.refs_0_, bf16[1792,256]{1,0:T(8,128)(2,1)S(1)} %copy-done.3, bf16[1792,256]{1,0:T(8,128)(2,1)S(1)} %collective-permute-done.13.refs_2_, ...), custom_call_target="tpu_custom_call" | custom-call | flops 3000000000 | bytes 10000000 | tf_op jit(solution)/shard_map/experts/gate_up/pallas_call | solution.py:139
  191.0 4.9 %all-to-all-start.4 = ((bf16[4,384,512]{2,1,0:T(8,128)(2,1)}), bf16[4,384,512]{2,1,0:T(8,128)(2,1)}, u32[]{:S(2)}, u32[]{:S(2)}) async-start(bf16[4,384,512]{2,1,0:T(8,128)(2,1)} %gate_up.1), calls=%async_computation.4 | async-start | bytes 3145728 | tf_op jit(solution)/shard_map/experts/all_to_all | solution.py:324
  195.9 1.6 dynamic-slice_bitcast_fusion
  197.5 1.5 collective-permute-start.23
  199.7 2.5 collective-permute-start.25
  202.3 22.2 %collective-permute-done.23.refs_2_ = bf16[128,1792]{1,0:T(8,128)(2,1)S(1)} collective-permute-done((bf16[128,1792]{1,0:T(8,128)(2,1)S(1)}, bf16[128,1792]{1,0:T(8,128)(2,1)S(1)}, u32[]{:S(2)}, u32[]{:S(2)}) %collective-permute-start.23) | collective-permute-done | bytes 458784 | tf_op jit(solution)/shard_map/down_weights/ppermute | solution.py:39
  224.5 2.0 collective-permute-done.24.refs_4_
  226.5 6.6 %collective-permute-done.25.refs_6_ = bf16[128,1792]{1,0:T(8,128)(2,1)S(1)} collective-permute-done((bf16[128,1792]{1,0:T(8,128)(2,1)S(1)}, bf16[128,1792]{1,0:T(8,128)(2,1)S(1)}, u32[]{:S(2)}, u32[]{:S(2)}) %collective-permute-start.25) | collective-permute-done | bytes 458784 | tf_op jit(solution)/shard_map/down_weights/ppermute | solution.py:39
  233.7 2.6 convert_reduce_fusion
  236.3 2.3 copy.143
  238.6 2.1 fusion.28
  240.6 1.9 copy.147
  242.5 1.9 copy.146
  247.0 3.0 collective-permute-start.20
  250.0 3.7 %collective-permute-done.19.i1 = bf16[384,256]{1,0:T(8,128)(2,1)S(1)} collective-permute-done((bf16[384,256]{1,0:T(8,128)(2,1)S(1)}, bf16[384,256]{1,0:T(8,128)(2,1)S(1)}, u32[]{:S(2)}, u32[]{:S(2)}) %collective-permute-start.19) | collective-permute-done | bytes 196640 | tf_op jit(solution)/shard_map/experts/ppermute | solution.py:39
  253.7 2.6 collective-permute-done.20.i2
  256.3 3.5 %collective-permute-done.21.i3 = bf16[384,256]{1,0:T(8,128)(2,1)S(1)} collective-permute-done((bf16[384,256]{1,0:T(8,128)(2,1)S(1)}, bf16[384,256]{1,0:T(8,128)(2,1)S(1)}, u32[]{:S(2)}, u32[]{:S(2)}) %collective-permute-start.21) | collective-permute-done | bytes 196640 | tf_op jit(solution)/shard_map/experts/ppermute | solution.py:39
  259.8 5.7 %down.1 = bf16[384,1792]{1,0:T(8,128)(2,1)} custom-call(bf16[384,256]{1,0:T(8,128)(2,1)S(1)} %multiply_convert_fusion.i0, bf16[384,256]{1,0:T(8,128)(2,1)S(1)} %collective-permute-done.19.i1, bf16[384,256]{1,0:T(8,128)(2,1)S(1)} %collective-permute-done.20.i2, bf16[384,256]{1,0:T(8,128)(2,1)S(1)} %collective-permute-done.21.i3, ...), custom_call_target="tpu_custom_call" | custom-call | flops 1400000000 | bytes 6000000 | tf_op jit(solution)/shard_map/experts/down/pallas_call | solution.py:167
  265.4 6.8 %all-to-all-start.5 = ((bf16[16,24,1792]{2,1,0:T(8,128)(2,1)}), bf16[16,24,1792]{2,1,0:T(8,128)(2,1)S(1)}, u32[]{:S(2)}, u32[]{:S(2)}) async-start(bf16[16,24,1792]{2,1,0:T(8,128)(2,1)} %bitcast.55), calls=%async_computation.5 | async-start | bytes 2752512 | tf_op jit(solution)/shard_map/return/all_to_all | solution.py:331
  273.2 18.7 %all-to-all-done.5 = bf16[16,24,1792]{2,1,0:T(8,128)(2,1)S(1)} async-done(((bf16[16,24,1792]{2,1,0:T(8,128)(2,1)}), bf16[16,24,1792]{2,1,0:T(8,128)(2,1)S(1)}, u32[]{:S(2)}, u32[]{:S(2)}) %all-to-all-start.5) | async-done | bytes 1376288 | tf_op jit(solution)/shard_map/return/all_to_all | solution.py:331
  292.7 9.6 %all_to_all.35 = bf16[4,8,1792]{2,1,0:T(8,128)(2,1)S(1)} all-to-all(bf16[4,8,1792]{2,1,0:T(8,128)(2,1)S(1)} %fusion.2), channel_id=1, replica_groups=mesh['y'=4,'x'=4,'z'=4,'core'=2] {'z'}, dimensions={0} | all-to-all | bytes 229376 | tf_op jit(solution)/shard_map/return/all_to_all | solution.py:336
  (175 shorter events, 42.3 us)
Async XLA Ops:
  0.0 7.8 %slice-start = ((bf16[8,64,192]{2,1,0:T(8,128)(2,1)}), bf16[8,64,64]{2,1,0:T(8,128)(2,1)S(1)}, s32[]{:S(2)}) async-start(bf16[8,64,192]{2,1,0:T(8,128)(2,1)} %param.13), calls=%async_computation.7 | async-start | bytes 262144 | tf_op jit(solution)/shard_map/query_exchange/slice | solution.py:213
  0.0 8.0 %slice-start.1 = ((bf16[8,64,192]{2,1,0:T(8,128)(2,1)}), bf16[8,64,128]{2,1,0:T(8,128)(2,1)S(1)}, s32[]{:S(2)}) async-start(bf16[8,64,192]{2,1,0:T(8,128)(2,1)} %param.13), calls=%async_computation.8 | async-start | bytes 262144 | tf_op jit(solution)/shard_map/query_exchange/slice | solution.py:212
  2.2 35.9 %collective-permute-start.3 = (bf16[256,576]{1,0:T(8,128)(2,1)}, bf16[256,576]{1,0:T(8,128)(2,1)S(1)}, u32[]{:S(2)}, u32[]{:S(2)}) collective-permute-start(bf16[256,576]{1,0:T(8,128)(2,1)} %constant_dynamic-slice_fusion), channel_id=1, source_target_pairs={{0,8},{8,16},{16,24},{24,0},{1,9},{9,17},{17,25},{25,1},{2,10},{10... | collective-permute-start | bytes 884744 | tf_op jit(solution)/shard_map/cache_gather/ppermute | solution.py:39
  3.7 34.5 %collective-permute-start.4 = (bf16[256,576]{1,0:T(8,128)(2,1)}, bf16[256,576]{1,0:T(8,128)(2,1)S(1)}, u32[]{:S(2)}, u32[]{:S(2)}) collective-permute-start(bf16[256,576]{1,0:T(8,128)(2,1)} %constant_dynamic-slice_fusion), channel_id=1, source_target_pairs={{0,16},{8,24},{16,0},{24,8},{1,17},{9,25},{17,1},{25,9},{2,18},{10... | collective-permute-start | bytes 884744 | tf_op jit(solution)/shard_map/cache_gather/ppermute | solution.py:39
  6.4 32.3 %collective-permute-start.5 = (bf16[256,576]{1,0:T(8,128)(2,1)}, bf16[256,576]{1,0:T(8,128)(2,1)}, u32[]{:S(2)}, u32[]{:S(2)}) collective-permute-start(bf16[256,576]{1,0:T(8,128)(2,1)} %constant_dynamic-slice_fusion), channel_id=1, source_target_pairs={{0,24},{8,0},{16,8},{24,16},{1,25},{9,1},{17,9},{25,17},{2,26},{10... | collective-permute-start | bytes 884744 | tf_op jit(solution)/shard_map/cache_gather/ppermute | solution.py:39
  8.0 9.5 %copy-start.26 = (s32[8,8]{1,0:T(8,128)S(1)}, s32[8,8]{1,0:T(8,128)}, u32[]{:S(2)}) copy-start(s32[8,8]{1,0:T(8,128)} %param.20) | copy-start | bytes 772
  8.0 9.5 %copy-start.27 = (f32[8,8]{1,0:T(8,128)S(1)}, f32[8,8]{1,0:T(8,128)}, u32[]{:S(2)}) copy-start(f32[8,8]{1,0:T(8,128)} %param.21) | copy-start | bytes 772
  8.0 9.5 %copy-start.19 = (bf16[8,7168]{1,0:T(8,128)(2,1)S(1)}, bf16[8,7168]{1,0:T(8,128)(2,1)}, u32[]{:S(2)}) copy-start(bf16[8,7168]{1,0:T(8,128)(2,1)} %param.18) | copy-start | bytes 344068
  8.2 13.7 %copy-start.25 = (s32[1024]{0:T(1024)S(1)}, s32[1024]{0:T(1024)}, u32[]{:S(2)}) copy-start(s32[1024]{0:T(1024)} %param.22) | copy-start | bytes 12292
  9.3 32.7 %all-to-all-start = ((bf16[32,8,1536]{2,1,0:T(8,128)(2,1)}), bf16[32,8,1536]{2,1,0:T(8,128)(2,1)S(1)}, u32[]{:S(2)}, u32[]{:S(2)}) async-start(bf16[32,8,1536]{2,1,0:T(8,128)(2,1)} %bitcast.13), calls=%async_computation | async-start | bytes 1572864 | tf_op jit(solution)/shard_map/query_exchange/all_to_all | solution.py:217
  17.5 5.0 %copy-start.22 = (bf16[8,8]{1,0:T(8,128)(2,1)}, bf16[8,8]{1,0:T(8,128)(2,1)S(1)}, u32[]{:S(2)}) copy-start(bf16[8,8]{1,0:T(8,128)(2,1)S(1)} %get-tuple-element.52) | copy-start | bytes 388
  18.3 15.6 %collective-permute-start = (bf16[8,1920]{1,0:T(8,128)(2,1)}, bf16[8,1920]{1,0:T(8,128)(2,1)S(1)}, u32[]{:S(2)}, u32[]{:S(2)}) collective-permute-start(bf16[8,1920]{1,0:T(8,128)(2,1)} %concatenate.32), channel_id=1, source_target_pairs={{0,6},{2,0},{4,2},{6,4},{1,7},{3,1},{5,3},{7,5},{8,14},{10,8},{12,... | collective-permute-start | bytes 92168 | tf_op jit(solution)/shard_map/residual_exchange/ppermute | solution.py:39
  19.6 16.2 %collective-permute-start.1 = (bf16[8,1920]{1,0:T(8,128)(2,1)}, bf16[8,1920]{1,0:T(8,128)(2,1)S(1)}, u32[]{:S(2)}, u32[]{:S(2)}) collective-permute-start(bf16[8,1920]{1,0:T(8,128)(2,1)} %concatenate.33), channel_id=1, source_target_pairs={{0,4},{2,6},{4,0},{6,2},{1,5},{3,7},{5,1},{7,3},{8,12},{10,14},{12... | collective-permute-start | bytes 92168 | tf_op jit(solution)/shard_map/residual_exchange/ppermute | solution.py:39
  26.8 15.3 %copy-start = (bf16[8,128,512]{2,1,0:T(8,128)(2,1)S(1)}, bf16[8,128,512]{2,1,0:T(8,128)(2,1)}, u32[]{:S(2)}) copy-start(bf16[8,128,512]{2,1,0:T(8,128)(2,1)} %ak_ref.1) | copy-start | bytes 3145732
  33.9 4.2 %collective-permute-start.2 = (bf16[8,1920]{1,0:T(8,128)(2,1)}, bf16[8,1920]{1,0:T(8,128)(2,1)S(1)}, u32[]{:S(2)}, u32[]{:S(2)}) collective-permute-start(bf16[8,1920]{1,0:T(8,128)(2,1)} %concatenate.34), channel_id=1, source_target_pairs={{0,2},{2,4},{4,6},{6,0},{1,3},{3,5},{5,7},{7,1},{8,10},{10,12},{12... | collective-permute-start | bytes 92168 | tf_op jit(solution)/shard_map/residual_exchange/ppermute | solution.py:39
  38.1 1.7 collective-permute-start.6
  38.2 2.4 collective-permute-start.7
  38.7 2.6 collective-permute-start.8
  65.7 13.8 %all-to-all-start.1 = ((bf16[4,64,1152]{2,1,0:T(8,128)(2,1)}), bf16[4,64,1152]{2,1,0:T(8,128)(2,1)S(1)}, u32[]{:S(2)}, u32[]{:S(2)}) async-start(bf16[4,64,1152]{2,1,0:T(8,128)(2,1)} %bitcast.20), calls=%async_computation.1 | async-start | bytes 1179648 | tf_op jit(solution)/shard_map/combine/all_to_all | solution.py:286
  89.2 7.0 %copy-start.21 = (bf16[7,8,1920]{2,1,0:T(8,128)(2,1)S(1)}, bf16[7,8,1920]{2,1,0:T(8,128)(2,1)}, u32[]{:S(2)}) copy-start(bf16[7,8,1920]{2,1,0:T(8,128)(2,1)} %bitcast_dynamic-update-slice_fusion.6) | copy-start | bytes 645124
  90.2 20.3 %copy-start.28 = (s32[32]{0:T(128)S(1)}, s32[32]{0:T(128)}, u32[]{:S(2)}) copy-start(s32[32]{0:T(128)} %add.239) | copy-start | bytes 388
  90.2 18.7 %all-to-all-start.2 = ((bf16[8,32,1792]{2,1,0:T(8,128)(2,1)}), bf16[8,32,1792]{2,1,0:T(8,128)(2,1)S(1)}, u32[]{:S(2)}, u32[]{:S(2)}) async-start(bf16[8,32,1792]{2,1,0:T(8,128)(2,1)} %bitcast.26), calls=%async_computation.2 | async-start | bytes 1835008 | tf_op jit(solution)/shard_map/out_projection/all_to_all | solution.py:299
  96.2 58.6 %copy-start.18 = (bf16[32,1920]{1,0:T(8,128)(2,1)}, bf16[32,1920]{1,0:T(8,128)(2,1)S(1)}, u32[]{:S(2)}) copy-start(bf16[32,1920]{1,0:T(8,128)(2,1)S(1)} %dynamic-slice_bitcast_fusion.12) | copy-start | bytes 368644
  96.6 64.7 %collective-permute-start.13 = (bf16[1792,256]{1,0:T(8,128)(2,1)}, bf16[1792,256]{1,0:T(8,128)(2,1)S(1)}, u32[]{:S(2)}, u32[]{:S(2)}) collective-permute-start(bf16[1792,256]{1,0:T(8,128)(2,1)} %pad_maximum_fusion.1), channel_id=1, source_target_pairs={{0,2},{2,4},{4,6},{6,0},{1,3},{3,5},{5,7},{7,1},{8,10},{10,12},{12... | collective-permute-start | bytes 2752520 | tf_op jit(solution)/shard_map/gate_up_weights/ppermute | solution.py:39
  98.0 63.2 %collective-permute-start.14 = (bf16[1792,256]{1,0:T(8,128)(2,1)}, bf16[1792,256]{1,0:T(8,128)(2,1)}, u32[]{:S(2)}, u32[]{:S(2)}) collective-permute-start(bf16[1792,256]{1,0:T(8,128)(2,1)} %pad_maximum_fusion.2), channel_id=1, source_target_pairs={{0,4},{2,6},{4,0},{6,2},{1,5},{3,7},{5,1},{7,3},{8,12},{10,14},{12... | collective-permute-start | bytes 2752520 | tf_op jit(solution)/shard_map/gate_up_weights/ppermute | solution.py:39
  98.9 62.3 %collective-permute-start.15 = (bf16[1792,256]{1,0:T(8,128)(2,1)}, bf16[1792,256]{1,0:T(8,128)(2,1)}, u32[]{:S(2)}, u32[]{:S(2)}) collective-permute-start(bf16[1792,256]{1,0:T(8,128)(2,1)} %pad_maximum_fusion.3), channel_id=1, source_target_pairs={{0,6},{2,0},{4,2},{6,4},{1,7},{3,1},{5,3},{7,5},{8,14},{10,8},{12,... | collective-permute-start | bytes 2752520 | tf_op jit(solution)/shard_map/gate_up_weights/ppermute | solution.py:39
  109.2 45.7 %copy-start.16 = (f32[32,1792]{1,0:T(8,128)}, f32[32,1792]{1,0:T(8,128)S(1)}, u32[]{:S(2)}) copy-start(f32[32,1792]{1,0:T(8,128)S(1)} %get-tuple-element.30) | copy-start | bytes 688132
  109.2 38.9 %collective-permute-start.11 = (f32[32,1]{0,1:T(1,128)S(1)}, f32[32,1]{0,1:T(1,128)S(1)}, u32[]{:S(2)}, u32[]{:S(2)}) collective-permute-start(f32[32,1]{0,1:T(1,128)S(1)} %bitcast.152), channel_id=1, source_target_pairs={{0,6},{2,0},{4,2},{6,4},{1,7},{3,1},{5,3},{7,5},{8,14},{10,8},{12,... | collective-permute-start | bytes 392 | tf_op jit(solution)/shard_map/norm/ppermute | solution.py:39
  110.5 39.2 %collective-permute-start.9 = (f32[32,1]{0,1:T(1,128)S(1)}, f32[32,1]{0,1:T(1,128)S(1)}, u32[]{:S(2)}, u32[]{:S(2)}) collective-permute-start(f32[32,1]{0,1:T(1,128)S(1)} %bitcast.153), channel_id=1, source_target_pairs={{0,2},{2,4},{4,6},{6,0},{1,3},{3,5},{5,7},{7,1},{8,10},{10,12},{12... | collective-permute-start | bytes 392 | tf_op jit(solution)/shard_map/norm/ppermute | solution.py:39
  148.1 5.0 %collective-permute-start.10 = (f32[32,1]{0,1:T(1,128)S(1)}, f32[32,1]{0,1:T(1,128)S(1)}, u32[]{:S(2)}, u32[]{:S(2)}) collective-permute-start(f32[32,1]{0,1:T(1,128)S(1)} %bitcast.154), channel_id=1, source_target_pairs={{0,4},{2,6},{4,0},{6,2},{1,5},{3,7},{5,1},{7,3},{8,12},{10,14},{12... | collective-permute-start | bytes 392 | tf_op jit(solution)/shard_map/norm/ppermute | solution.py:39
  154.9 22.0 %all-to-all-start.3 = ((bf16[16,24,1792]{2,1,0:T(8,128)(2,1)}), bf16[16,24,1792]{2,1,0:T(8,128)(2,1)S(1)}, u32[]{:S(2)}, u32[]{:S(2)}) async-start(bf16[16,24,1792]{2,1,0:T(8,128)(2,1)} %bitcast.142), calls=%async_computation.3 | async-start | bytes 2752512 | tf_op jit(solution)/shard_map/dispatch/all_to_all | solution.py:316
  161.1 2.6 collective-permute-start.12
  161.2 5.1 %collective-permute-start.16 = (bf16[1792,256]{1,0:T(8,128)(2,1)S(1)}, bf16[1792,256]{1,0:T(8,128)(2,1)S(1)}, u32[]{:S(2)}, u32[]{:S(2)}) collective-permute-start(bf16[1792,256]{1,0:T(8,128)(2,1)S(1)} %collective-permute-done.13.refs_2_), channel_id=1, source_target_pairs={{0,1},{1,0},{2,3},{3,2},{4,5},{5,4},{6,7},{7,6},{8,9},{9,8},{10,11... | collective-permute-start | bytes 2752520 | tf_op jit(solution)/shard_map/down_weights/ppermute | solution.py:39
  161.8 5.4 %collective-permute-start.17 = (bf16[1792,256]{1,0:T(8,128)(2,1)}, bf16[1792,256]{1,0:T(8,128)(2,1)S(1)}, u32[]{:S(2)}, u32[]{:S(2)}) collective-permute-start(bf16[1792,256]{1,0:T(8,128)(2,1)} %collective-permute-done.14.refs_4_), channel_id=1, source_target_pairs={{0,1},{1,0},{2,3},{3,2},{4,5},{5,4},{6,7},{7,6},{8,9},{9,8},{10,11... | collective-permute-start | bytes 2752520 | tf_op jit(solution)/shard_map/down_weights/ppermute | solution.py:39
  161.9 6.3 %collective-permute-start.18 = (bf16[1792,256]{1,0:T(8,128)(2,1)}, bf16[1792,256]{1,0:T(8,128)(2,1)S(1)}, u32[]{:S(2)}, u32[]{:S(2)}) collective-permute-start(bf16[1792,256]{1,0:T(8,128)(2,1)} %collective-permute-done.15.refs_6_), channel_id=1, source_target_pairs={{0,1},{1,0},{2,3},{3,2},{4,5},{5,4},{6,7},{7,6},{8,9},{9,8},{10,11... | collective-permute-start | bytes 2752520 | tf_op jit(solution)/shard_map/down_weights/ppermute | solution.py:39
  191.0 42.6 %all-to-all-start.4 = ((bf16[4,384,512]{2,1,0:T(8,128)(2,1)}), bf16[4,384,512]{2,1,0:T(8,128)(2,1)}, u32[]{:S(2)}, u32[]{:S(2)}) async-start(bf16[4,384,512]{2,1,0:T(8,128)(2,1)} %gate_up.1), calls=%async_computation.4 | async-start | bytes 3145728 | tf_op jit(solution)/shard_map/experts/all_to_all | solution.py:324
  197.5 27.0 %collective-permute-start.23 = (bf16[128,1792]{1,0:T(8,128)(2,1)S(1)}, bf16[128,1792]{1,0:T(8,128)(2,1)S(1)}, u32[]{:S(2)}, u32[]{:S(2)}) collective-permute-start(bf16[128,1792]{1,0:T(8,128)(2,1)S(1)} %get-tuple-element.23), channel_id=1, source_target_pairs={{0,2},{2,4},{4,6},{6,0},{1,3},{3,5},{5,7},{7,1},{8,10},{10,12},{12... | collective-permute-start | bytes 1376264 | tf_op jit(solution)/shard_map/down_weights/ppermute | solution.py:39
  199.0 27.5 %collective-permute-start.24 = (bf16[128,1792]{1,0:T(8,128)(2,1)S(1)}, bf16[128,1792]{1,0:T(8,128)(2,1)S(1)}, u32[]{:S(2)}, u32[]{:S(2)}) collective-permute-start(bf16[128,1792]{1,0:T(8,128)(2,1)S(1)} %get-tuple-element.24), channel_id=1, source_target_pairs={{0,4},{2,6},{4,0},{6,2},{1,5},{3,7},{5,1},{7,3},{8,12},{10,14},{12... | collective-permute-start | bytes 1376264 | tf_op jit(solution)/shard_map/down_weights/ppermute | solution.py:39
  199.7 33.4 %collective-permute-start.25 = (bf16[128,1792]{1,0:T(8,128)(2,1)S(1)}, bf16[128,1792]{1,0:T(8,128)(2,1)S(1)}, u32[]{:S(2)}, u32[]{:S(2)}) collective-permute-start(bf16[128,1792]{1,0:T(8,128)(2,1)S(1)} %get-tuple-element.25), channel_id=1, source_target_pairs={{0,6},{2,0},{4,2},{6,4},{1,7},{3,1},{5,3},{7,5},{8,14},{10,8},{12,... | collective-permute-start | bytes 1376264 | tf_op jit(solution)/shard_map/down_weights/ppermute | solution.py:39
  202.3 44.7 %collective-permute-start.22 = (bf16[128,1792]{1,0:T(8,128)(2,1)S(1)}, bf16[128,1792]{1,0:T(8,128)(2,1)S(1)}, u32[]{:S(2)}, u32[]{:S(2)}) collective-permute-start(bf16[128,1792]{1,0:T(8,128)(2,1)S(1)} %get-tuple-element.35.refs_0_), channel_id=1, source_target_pairs={{0,1},{1,0},{2,3},{3,2},{4,5},{5,4},{6,7},{7,6},{8,9},{9,8},{10,11... | collective-permute-start | bytes 1376264 | tf_op jit(solution)/shard_map/experts/ppermute | solution.py:39
  233.1 16.8 %collective-permute-start.26 = (bf16[128,1792]{1,0:T(8,128)(2,1)S(1)}, bf16[128,1792]{1,0:T(8,128)(2,1)S(1)}, u32[]{:S(2)}, u32[]{:S(2)}) collective-permute-start(bf16[128,1792]{1,0:T(8,128)(2,1)S(1)} %collective-permute-done.23.refs_2_), channel_id=1, source_target_pairs={{0,1},{1,0},{2,3},{3,2},{4,5},{5,4},{6,7},{7,6},{8,9},{9,8},{10,11... | collective-permute-start | bytes 1376264 | tf_op jit(solution)/shard_map/experts/ppermute | solution.py:39
  233.1 16.8 %collective-permute-start.27 = (bf16[128,1792]{1,0:T(8,128)(2,1)S(1)}, bf16[128,1792]{1,0:T(8,128)(2,1)S(1)}, u32[]{:S(2)}, u32[]{:S(2)}) collective-permute-start(bf16[128,1792]{1,0:T(8,128)(2,1)S(1)} %collective-permute-done.24.refs_4_), channel_id=1, source_target_pairs={{0,1},{1,0},{2,3},{3,2},{4,5},{5,4},{6,7},{7,6},{8,9},{9,8},{10,11... | collective-permute-start | bytes 1376264 | tf_op jit(solution)/shard_map/experts/ppermute | solution.py:39
  233.6 16.3 %collective-permute-start.28 = (bf16[128,1792]{1,0:T(8,128)(2,1)S(1)}, bf16[128,1792]{1,0:T(8,128)(2,1)}, u32[]{:S(2)}, u32[]{:S(2)}) collective-permute-start(bf16[128,1792]{1,0:T(8,128)(2,1)S(1)} %collective-permute-done.25.refs_6_), channel_id=1, source_target_pairs={{0,1},{1,0},{2,3},{3,2},{4,5},{5,4},{6,7},{7,6},{8,9},{9,8},{10,11... | collective-permute-start | bytes 1376264 | tf_op jit(solution)/shard_map/experts/ppermute | solution.py:39
  245.7 7.9 %collective-permute-start.19 = (bf16[384,256]{1,0:T(8,128)(2,1)S(1)}, bf16[384,256]{1,0:T(8,128)(2,1)S(1)}, u32[]{:S(2)}, u32[]{:S(2)}) collective-permute-start(bf16[384,256]{1,0:T(8,128)(2,1)S(1)} %multiply_convert_fusion.i0), channel_id=1, source_target_pairs={{0,2},{2,4},{4,6},{6,0},{1,3},{3,5},{5,7},{7,1},{8,10},{10,12},{12... | collective-permute-start | bytes 589832 | tf_op jit(solution)/shard_map/experts/ppermute | solution.py:39
  247.0 9.3 %collective-permute-start.20 = (bf16[384,256]{1,0:T(8,128)(2,1)S(1)}, bf16[384,256]{1,0:T(8,128)(2,1)S(1)}, u32[]{:S(2)}, u32[]{:S(2)}) collective-permute-start(bf16[384,256]{1,0:T(8,128)(2,1)S(1)} %multiply_convert_fusion.i0), channel_id=1, source_target_pairs={{0,4},{2,6},{4,0},{6,2},{1,5},{3,7},{5,1},{7,3},{8,12},{10,14},{12... | collective-permute-start | bytes 589832 | tf_op jit(solution)/shard_map/experts/ppermute | solution.py:39
  250.0 9.8 %collective-permute-start.21 = (bf16[384,256]{1,0:T(8,128)(2,1)S(1)}, bf16[384,256]{1,0:T(8,128)(2,1)S(1)}, u32[]{:S(2)}, u32[]{:S(2)}) collective-permute-start(bf16[384,256]{1,0:T(8,128)(2,1)S(1)} %multiply_convert_fusion.i0), channel_id=1, source_target_pairs={{0,6},{2,0},{4,2},{6,4},{1,7},{3,1},{5,3},{7,5},{8,14},{10,8},{12,... | collective-permute-start | bytes 589832 | tf_op jit(solution)/shard_map/experts/ppermute | solution.py:39
  265.4 26.5 %copy-start.17 = (f32[32,1792]{1,0:T(8,128)S(1)}, f32[32,1792]{1,0:T(8,128)}, u32[]{:S(2)}) copy-start(f32[32,1792]{1,0:T(8,128)} %copy-done.16) | copy-start | bytes 688132
  265.4 26.5 %all-to-all-start.5 = ((bf16[16,24,1792]{2,1,0:T(8,128)(2,1)}), bf16[16,24,1792]{2,1,0:T(8,128)(2,1)S(1)}, u32[]{:S(2)}, u32[]{:S(2)}) async-start(bf16[16,24,1792]{2,1,0:T(8,128)(2,1)} %bitcast.55), calls=%async_computation.5 | async-start | bytes 2752512 | tf_op jit(solution)/shard_map/return/all_to_all | solution.py:331
  (18 other events, 26.4 us)

commit v2 on v1

v2 whole, which is shorter than its diff:
```python
import functools

import jax
import jax.numpy as jnp
from jax import lax
from jax.experimental import pallas as pl
from jax.experimental.pallas import tpu as pltpu
from jax.sharding import Mesh
from jax.sharding import PartitionSpec as P

D = 7168
NOPE = 128
ROPE = 64
LAT = 512
VDIM = 128
EXPERTS = 16
TOP = 8
RESP = 1024
PROMPT = 7168
NX = 4
NY = 4
NZ = 4
GRP = 8
BLK = 8
CAP = 6
QCOLS = GRP * (NOPE + ROPE) + 128
KEYS = 2048
HALF = 256
ROWS = 256
CHUNK = D // NZ
SLOTS = NZ * CAP
EROWS = 16 * SLOTS
LOG2E = 1.4426950408889634
BF = jnp.bfloat16
F32 = jnp.float32
HIDE = -1e30


def shift(a, axis, n, d):
    return lax.ppermute(a, axis, [(i, (i + d) % n) for i in range(n)])


def split3(v):
    hi = v.astype(BF).astype(F32)
    mid = (v - hi).astype(BF).astype(F32)
    low = (v - hi - mid).astype(BF).astype(F32)
    return hi, mid, low


def cost(flops=0, nbytes=1):
    return pl.CostEstimate(flops=flops, bytes_accessed=nbytes, transcendentals=0)


def call(kernel, name, out_shape, in_specs, scratch, mib=48, **more):
    return pl.pallas_call(
        kernel,
        out_shape=out_shape,
        in_specs=in_specs,
        scratch_shapes=scratch,
        compiler_params=pltpu.CompilerParams(vmem_limit_bytes=mib * 2**20),
        cost_estimate=cost(),
        name=name,
        **more,
    )


VM = pl.BlockSpec(memory_space=pltpu.VMEM)
SM = pl.BlockSpec(memory_space=pltpu.SMEM)
AT = pl.BlockSpec(memory_space=pl.ANY)
PAIR = 2


def attention_kernel(
    pos_ref, q_ref, first_ref, last_ref, c0, c1, c2, c3, s1, s2, s3, ak_ref, av_ref, o_ref, kv, rp, st, hide, sem
):
    g = pl.program_id(0)

    @pl.when(g == 0)
    def _():
        copies = [pltpu.make_async_copy(c0, kv.at[pl.ds(pl.multiple_of(pos_ref[0], HALF), 2 * HALF)], sem.at[0])]
        for i, piece in enumerate((c1, c2, c3, s1, s2, s3)):
            to = kv.at[pl.ds(pl.multiple_of(pos_ref[1 + i], HALF), HALF)]
            copies.append(pltpu.make_async_copy(piece, to, sem.at[1 + i]))
        for c in copies:
            c.start()
        col = lax.broadcasted_iota(jnp.int32, (ROWS, KEYS // 2), 1)
        hide[...] = jnp.where((col >= first_ref[...]) & (col <= last_ref[...]), 0.0, HIDE)
        st[...] = jnp.zeros_like(st)
        for c in copies:
            c.wait()
        r = kv[:, LAT:]
        rp[...] = jnp.concatenate([r, r], axis=1)

    lane = lax.broadcasted_iota(jnp.int32, (ROWS, 128), 1)
    nt = (((1,), (1,)), ((), ()))
    step = 512
    scale = LOG2E * (NOPE + ROPE) ** (-0.5)
    scored = []
    for i in range(PAIR):
        h = g * PAIR + i
        nope = q_ref[:, pl.ds(pl.multiple_of(h * NOPE, NOPE), NOPE)]
        q_lat = jnp.dot(nope, ak_ref[i], preferred_element_type=F32).astype(BF)
        pair = q_ref[:, pl.ds(pl.multiple_of(GRP * NOPE + (h // 2) * 128, 128), 128)].astype(F32)
        rope = jnp.where(lane // ROPE == h % 2, pair, 0.0).astype(BF)
        parts = []
        for j in range(0, KEYS, step):
            s = lax.dot_general(q_lat, kv[j : j + step, :LAT], nt, preferred_element_type=F32)
            s = s + lax.dot_general(rope, rp[j : j + step, :], nt, preferred_element_type=F32)
            if j >= KEYS // 2:
                s = s + hide[:, j - KEYS // 2 : j - KEYS // 2 + step]
            parts.append(s)
        scored.append(parts)
    for i, parts in enumerate(scored):
        h = g * PAIR + i
        top = jnp.max(parts[0], axis=1, keepdims=True)
        for s in parts[1:]:
            top = jnp.maximum(top, jnp.max(s, axis=1, keepdims=True))
        total = jnp.zeros((ROWS, 1), F32)
        acc = jnp.zeros((ROWS, LAT), F32)
        for n, s in enumerate(parts):
            p = jnp.exp2((s - top) * scale)
            total = total + jnp.sum(p, axis=1, keepdims=True)
            acc = acc + jnp.dot(p.astype(BF), kv[n * step : (n + 1) * step, :LAT], preferred_element_type=F32)
        lat = (acc / total).astype(BF)
        o_ref[:, pl.ds(pl.multiple_of(h * VDIM, VDIM), VDIM)] = jnp.dot(
            lat, av_ref[i], preferred_element_type=F32
        ).astype(BF)
        add = jnp.zeros((ROWS, 128), F32)
        for n, v in enumerate(split3(top) + split3(total)):
            add = add + jnp.where(lane == n * GRP + h, v, 0.0)
        st[...] += add

    @pl.when(g == GRP // PAIR - 1)
    def _():
        o_ref[:, GRP * VDIM :] = st[...].astype(BF)


def attention(place, q, first, last, pieces, absorb_key, absorb_value):
    whole = lambda a: pl.BlockSpec(a.shape, lambda g: (0,) * a.ndim)
    return call(
        attention_kernel,
        "attention",
        jax.ShapeDtypeStruct((ROWS, GRP * VDIM + 128), BF),
        [SM, whole(q), whole(first), whole(last)]
        + [AT] * 7
        + [
            pl.BlockSpec((PAIR, NOPE, LAT), lambda g: (g, 0, 0)),
            pl.BlockSpec((PAIR, LAT, VDIM), lambda g: (g, 0, 0)),
        ],
        [
            pltpu.VMEM((KEYS, LAT + ROPE), BF),
            pltpu.VMEM((KEYS, 2 * ROPE), BF),
            pltpu.VMEM((ROWS, 128), F32),
            pltpu.VMEM((ROWS, KEYS // 2), F32),
            pltpu.SemaphoreType.DMA((7,)),
        ],
        grid=(GRP // PAIR,),
        out_specs=pl.BlockSpec((ROWS, GRP * VDIM + 128), lambda g: (0, 0)),
    )(place, q, first, last, *pieces, absorb_key, absorb_value)


def routing_kernel(at_ref, col_ref, q_ref, pick_ref, blend_ref, held, sem):
    rows = q_ref.at[pl.ds(pl.multiple_of(at_ref[0], NZ * BLK), NZ * BLK), pl.ds(QCOLS - 128, 128)]
    copy = pltpu.make_async_copy(rows, held, sem)
    copy.start()
    copy.wait()
    info = held[...].astype(F32)
    rows = NZ * BLK
    route = info[:, :TOP]
    score = info[:, TOP : 2 * TOP] + info[:, 2 * TOP : 3 * TOP] + info[:, 3 * TOP : 4 * TOP]
    weight = 2.5 * score / jnp.sum(score, axis=1, keepdims=True)
    expert, block, slot = col_ref[0:1, :], col_ref[1:2, :], col_ref[2:3, :]
    named = jnp.zeros((rows, EROWS), F32)
    mix = jnp.zeros((rows, EROWS), F32)
    for n in range(TOP):
        hit = route[:, n : n + 1] == expert
        named = named + jnp.where(hit, 1.0, 0.0)
        mix = mix + jnp.where(hit, weight[:, n : n + 1], 0.0)
    i = lax.broadcasted_iota(jnp.int32, (rows, rows), 0)
    j = lax.broadcasted_iota(jnp.int32, (rows, rows), 1)
    ahead = jnp.where((j < i) & (j // BLK == i // BLK), 1.0, 0.0).astype(BF)
    rank = jnp.dot(ahead, named.astype(BF), preferred_element_type=F32)
    mine = (lax.broadcasted_iota(jnp.int32, (rows, EROWS), 0) // BLK).astype(F32)
    place = (named > 0.5) & (block == mine) & (slot == rank)
    pick_ref[...] = jnp.where(place, 1.0, 0.0).astype(BF)
    blend_ref[...] = jnp.where(place, mix, 0.0)


def routing(at, q):
    col = jnp.arange(EROWS, dtype=jnp.int32)
    cols = jnp.stack([col // SLOTS, col % SLOTS // CAP, col % CAP] + [col * 0] * 5).astype(F32)
    rows = NZ * BLK
    return call(
        routing_kernel,
        "routing",
        (jax.ShapeDtypeStruct((rows, EROWS), BF), jax.ShapeDtypeStruct((rows, EROWS), F32)),
        [SM, VM, AT],
        [pltpu.VMEM((rows, 128), BF), pltpu.SemaphoreType.DMA],
        out_specs=(VM, VM),
    )(at, cols, q)


def project_kernel(own_ref, o_ref, w_ref, res_ref, out_ref, head_out):
    @pl.when(pl.program_id(0) == 0)
    def _():
        tops, totals = [], []
        for s in range(NY):
            st = o_ref[s, :, GRP * VDIM :].astype(F32)
            part = [st[:, n * GRP : (n + 1) * GRP] for n in range(6)]
            tops.append(part[0] + part[1] + part[2])
            totals.append(part[3] + part[4] + part[5])
        top = jnp.maximum(jnp.maximum(tops[0], tops[1]), jnp.maximum(tops[2], tops[3]))
        scale = LOG2E * (NOPE + ROPE) ** (-0.5)
        share = [t * jnp.exp2((m - top) * scale) for m, t in zip(tops, totals)]
        whole = share[0] + share[1] + share[2] + share[3]
        share = [s / whole for s in share]
        for h in range(GRP):
            at = slice(h * VDIM, (h + 1) * VDIM)
            total = sum(o_ref[s, :, at].astype(F32) * share[s][:, h : h + 1] for s in range(NY))
            head_out[:, at] = total.astype(BF)

    part = jnp.dot(head_out[...], w_ref[...], preferred_element_type=F32)
    row = lax.broadcasted_iota(jnp.int32, part.shape, 0) // BLK
    res = jnp.concatenate([res_ref[...].astype(F32)] * 8, axis=0)
    part = (part + jnp.where(row == own_ref[0], res, 0.0)).astype(BF)
    out_ref[0, 0] = part[: NZ * BLK]
    out_ref[1, 0] = part[NZ * BLK :]


def project(own, o, out_proj, residual):
    width = CHUNK // 2
    return call(
        project_kernel,
        "project",
        jax.ShapeDtypeStruct((2, NZ, NZ * BLK, CHUNK), BF),
        [
            SM,
            pl.BlockSpec(o.shape, lambda j: (0, 0, 0)),
            pl.BlockSpec((GRP * VDIM, width), lambda j: (0, j)),
            pl.BlockSpec((BLK, width), lambda j: (0, j)),
        ],
        [pltpu.VMEM((64, GRP * VDIM), BF)],
        grid=(D // width,),
        out_specs=pl.BlockSpec((2, 1, NZ * BLK, width), lambda j: (0, j // 2, 0, j % 2)),
    )(own, o, out_proj, residual)


def spread_kernel(part_ref, gain_ref, pick_ref, hidden_ref, rows_ref):
    hidden = part_ref[0].astype(F32)
    for s in range(1, 8):
        hidden = hidden + part_ref[s].astype(F32)
    hidden_ref[...] = hidden
    scaled = (hidden * gain_ref[...]).astype(BF)
    tn = (((0,), (0,)), ((), ()))
    rows_ref[...] = lax.dot_general(pick_ref[...], scaled, tn, preferred_element_type=F32).astype(BF)


def spread(part, gain, pick):
    return call(
        spread_kernel,
        "spread",
        (jax.ShapeDtypeStruct((NZ * BLK, CHUNK), F32), jax.ShapeDtypeStruct((EROWS, CHUNK), BF)),
        [VM] * 3,
        [],
        out_specs=(VM, VM),
    )(part, gain, pick)


def gate_up_kernel(z_ref, x_ref, gain_ref, *refs):
    pieces, (o_ref, square_ref, w, sem) = refs[:8], refs[8:]
    copies = [
        pltpu.make_async_copy(p, w.at[:, pl.ds(i * 256, 256)], sem.at[i]) for i, p in enumerate(pieces)
    ]
    for c in copies:
        c.start()
    x = x_ref[...]
    raw = x.astype(F32) * gain_ref[...]
    ones = jnp.ones((8, CHUNK), BF)
    square_ref[...] = lax.dot_general(
        ones, (raw * raw).astype(BF), (((1,), (1,)), ((), ())), preferred_element_type=F32
    )
    for d in range(NZ):
        copies[2 * d].wait()
        copies[2 * d + 1].wait()
        part = jnp.dot(x, w[:, d * 512 : (d + 1) * 512], preferred_element_type=F32).astype(BF)
        o_ref[lax.rem(z_ref[0] + NZ - d, NZ)] = part


def gate_up(z, x, gain, pieces):
    return call(
        gate_up_kernel,
        "gate_up",
        (jax.ShapeDtypeStruct((NZ, EROWS, 512), BF), jax.ShapeDtypeStruct((8, EROWS), F32)),
        [SM, VM, VM] + [AT] * 8,
        [pltpu.VMEM((CHUNK, 2048), BF), pltpu.SemaphoreType.DMA((8,))],
        out_specs=(VM, VM),
    )(z, x, gain, *pieces)


def inner_kernel(part_ref, s0, s1, s2, s3, out_ref):
    square = s0[...] + s1[...] + s2[...] + s3[...]
    scale = lax.rsqrt(square / D + 1e-6).T[:, :1]
    total = part_ref[0].astype(F32)
    for s in range(1, NZ):
        total = total + part_ref[s].astype(F32)
    total = total * scale
    for k in range(2):
        gate, up = total[:, k * 256 : k * 256 + 128], total[:, k * 256 + 128 : k * 256 + 256]
        out_ref[:, k * 128 : (k + 1) * 128] = (gate / (1.0 + jnp.exp(-gate)) * up).astype(BF)


def inner_act(part, squares):
    return call(
        inner_kernel, "inner_act", jax.ShapeDtypeStruct((EROWS, 256), BF), [VM] * 5, [], out_specs=VM
    )(part, *squares)


def down_kernel(i0, i1, i2, i3, *refs):
    pieces, (o_ref, w, sem) = refs[:8], refs[8:]
    copies = [
        pltpu.make_async_copy(p, w.at[pl.ds(i * 128, 128)], sem.at[i]) for i, p in enumerate(pieces)
    ]
    for c in copies:
        c.start()
    inner = jnp.concatenate([i0[...], i1[...], i2[...], i3[...]], axis=1)
    for c in copies:
        c.wait()
    o_ref[...] = jnp.dot(inner, w[...], preferred_element_type=F32).astype(BF)


def down(inners, pieces):
    return call(
        down_kernel,
        "down",
        jax.ShapeDtypeStruct((EROWS, CHUNK), BF),
        [VM] * 4 + [AT] * 8,
        [pltpu.VMEM((1024, CHUNK), BF), pltpu.SemaphoreType.DMA((8,))],
        out_specs=VM,
    )(*inners, *pieces)


def after(arrays, token):
    out = lax.optimization_barrier(tuple(arrays) + (token,))
    return out[:-1]


def shards(
    queries,
    latent_cache,
    absorb_key,
    absorb_value,
    out_proj,
    residual,
    norm_gain,
    routes,
    route_score,
    response_doc,
    expert_gate,
    expert_up,
    expert_down,
):
    x, y, z, k = (lax.axis_index(a) for a in ("x", "y", "z", "core"))

    with jax.named_scope("cache_gather"):
        half = lax.dynamic_slice_in_dim(latent_cache, k * HALF, HALF, axis=0)
        mine = [shift(half, "x", NX, d) for d in range(1, NX)]

    with jax.named_scope("query_exchange"):
        score_hi = lax.reduce_precision(route_score, 8, 7)
        score_mid = lax.reduce_precision(route_score - score_hi, 8, 7)
        score_low = route_score - score_hi - score_mid
        info = jnp.concatenate(
            [routes.astype(BF)]
            + [s.astype(BF) for s in (score_hi, score_mid, score_low)]
            + [jnp.zeros((BLK, 128 - 4 * TOP), BF)],
            axis=1,
        )
        info = jnp.broadcast_to(info[:, None, None], (BLK, NZ, 2, 128))
        nope = queries[:, :, :NOPE].reshape(BLK, NZ, 2, GRP * NOPE)
        rope = queries[:, :, NOPE:].reshape(BLK, NZ, 2, GRP * ROPE)
        q = jnp.concatenate([nope, rope, info], axis=3).transpose(2, 1, 0, 3)
        q = jnp.broadcast_to(q[None], (NY, 2, NZ, BLK, QCOLS))
        q = q.reshape(NY * 2 * NZ, BLK, QCOLS)
        (q,) = after([q], mine[0])
        q = lax.all_to_all(q, ("y", "core", "z"), split_axis=0, concat_axis=0, tiled=True)
        q = q.reshape(ROWS, QCOLS)

    with jax.named_scope("weights"):
        gates = expert_gate[0].reshape(NZ, CHUNK, 128)
        ups = expert_up[0].reshape(NZ, CHUNK, 128)
        downs = expert_down[0]
        gu, dn = [], []
        for d in range(NZ):
            to = (z + d) % NZ
            g = lax.dynamic_index_in_dim(gates, to, 0, keepdims=False)
            u = lax.dynamic_index_in_dim(ups, to, 0, keepdims=False)
            gu.append(jnp.concatenate([g, u], axis=1))
            dn.append(lax.dynamic_slice_in_dim(downs, to * CHUNK, CHUNK, axis=1))
        gu[1], gu[3] = shift(gu[1], "z", NZ, 1), shift(gu[3], "z", NZ, 3)

    with jax.named_scope("cache_share"):
        other = [shift(m, "core", 2, 1) for m in mine]

    with jax.named_scope("attention"):
        doc = lax.dynamic_index_in_dim(response_doc.reshape(NY, NX, NZ, 2, BLK), x, 1, keepdims=False)
        doc = doc.transpose(0, 2, 1, 3).reshape(ROWS)
        ids = jnp.arange(RESP, dtype=jnp.int32).reshape(NY, NX, NZ, 2, BLK)
        ids = lax.dynamic_index_in_dim(ids, x, 1, keepdims=False).transpose(0, 2, 1, 3).reshape(ROWS)
        start = jnp.sum((response_doc[None, :] < doc[:, None]).astype(jnp.int32), axis=1)
        far = jnp.int32(1 << 20)
        first = jnp.where(y == NY - 1, start, -far)[:, None]
        last = jnp.where(y == NY - 1, ids, far)[:, None]
        at = [x * 512]
        for core in (k, 1 - k):
            at += [((x - d) % NX) * 512 + core * HALF for d in range(1, NX)]
        place_of = jnp.stack(at).astype(jnp.int32)

        q, gu[1], gu[3] = lax.optimization_barrier((q, gu[1], gu[3]))
        ahead = after([gu[2], dn[1], dn[3]], q)
        gu[2], dn[1], dn[3] = shift(ahead[0], "z", NZ, 2), shift(ahead[1], "z", NZ, 1), shift(ahead[2], "z", NZ, 3)
        out = attention(place_of, q, first, last, [latent_cache] + mine + other, absorb_key, absorb_value)

    with jax.named_scope("combine"):
        out = lax.all_to_all(out.reshape(NY, 64, -1), "y", split_axis=0, concat_axis=0, tiled=True)

    with jax.named_scope("routing"):
        pick, blend = routing(((y * 2 + k) * NZ * BLK).reshape(1), after([q], out)[0])

    with jax.named_scope("out_projection"):
        out, gu[2], dn[1], dn[3] = lax.optimization_barrier((out, gu[2], dn[1], dn[3]))
        gu_other = [shift(w, "core", 2, 1) for w in after(gu, out)]
        part = project((k * NZ + z).reshape(1), out, out_proj, residual)
        part = part.reshape(8, NZ * BLK, CHUNK)
        part = lax.all_to_all(part, ("core", "z"), split_axis=0, concat_axis=0, tiled=True)

    with jax.named_scope("dispatch"):
        gain = lax.dynamic_slice_in_dim(norm_gain, z * CHUNK, CHUNK)[None]
        part, *gu_other = lax.optimization_barrier((part, *gu_other))
        (ahead,) = after([dn[2]], part)
        dn[2] = shift(ahead, "z", NZ, 2)
        hidden, rows = spread(part, gain, pick)
        rows = rows.reshape(EXPERTS, SLOTS, CHUNK)
        rows = lax.all_to_all(rows, ("y", "x"), split_axis=0, concat_axis=0, tiled=True)
        rows = rows.reshape(EROWS, CHUNK)

    with jax.named_scope("experts"):
        rows, dn[2] = lax.optimization_barrier((rows, dn[2]))
        dn_other = [shift(w, "core", 2, 1) for w in after(dn, rows)]
        part, square = gate_up(z.reshape(1), rows, 1.0 / gain, [w for pair in zip(gu, gu_other) for w in pair])
        squares = [square] + [shift(square, "z", NZ, d) for d in range(1, NZ)]
        part, *dn_other = lax.optimization_barrier((part, *dn_other))
        part = lax.all_to_all(part, "z", split_axis=0, concat_axis=0, tiled=True)
        inner = inner_act(part, squares)
        inners = [inner] + [shift(inner, "z", NZ, d) for d in range(1, NZ)]
        result = down(inners, [w for pair in zip(dn, dn_other) for w in pair])

    with jax.named_scope("return"):
        back = lax.all_to_all(
            result.reshape(EXPERTS, SLOTS, CHUNK), ("y", "x"), split_axis=0, concat_axis=0, tiled=True
        ).reshape(EROWS, CHUNK)
        mixed = jnp.dot(blend, back.astype(F32), precision=lax.Precision.HIGHEST, preferred_element_type=F32)
        done = (hidden + mixed).astype(BF).reshape(NZ, BLK, CHUNK)
        done = lax.all_to_all(done, "z", split_axis=0, concat_axis=0, tiled=True)
        return done.transpose(1, 0, 2).reshape(BLK, D)


def solution(mesh):
    fine = Mesh(mesh.devices.reshape(NY, NX, NZ, 2), ("y", "x", "z", "core"))
    ctx, head = ("y", "x"), ("z", "core")
    both = ctx + head
    in_specs = (
        P(both, None, None),
        P(ctx, None),
        P(head, None, None),
        P(head, None, None),
        P(head, None),
        P(both, None),
        P(),
        P(both, None),
        P(both, None),
        P(),
        P(ctx, None, head),
        P(ctx, None, head),
        P(ctx, head, None),
    )
    return jax.shard_map(shards, mesh=fine, in_specs=in_specs, out_specs=P(both, None), check_vma=False)
```

time: 308 us -> 234 us (0.76)
  waiting for transfers between devices: 130 us -> 78.4 us
  local copies, waits for them, and re-layouts: 42.4 us -> 19.3 us
  blocking collectives: 9.62 us -> 32.7 us
  starting transfers between devices: 65.6 us -> 52.3 us
  matrix products: 10.3 us -> 0.66 us
  Pallas kernels: 34.6 us -> 40.7 us
  other arithmetic: 9.87 us -> 5.72 us
    ppermute x29 -> x26, waiting for transfers between devices: 87.3 us -> 50.9 us  [shift(): return lax.ppermute(a, axis, [(i, (i + d) % n) for i in range(n)])]
    all_to_all x0 -> x1, blocking collectives: none -> 22.5 us  [shards(): lax.all_to_all(result.reshape(EXPERTS, SLOTS, CHUNK), ('y', 'x'), split_a...]
    all_to_all x2 -> x1, waiting for transfers between devices: 27.2 us -> 7.48 us  [shards(): lax.all_to_all(out.reshape(NY, 64, -1), 'y', split_axis=0, concat_axis=0,...]
    dot_general x2 -> x0, matrix products: 9.58 us -> none  [the longest x1 7.89 us: shards(): part = jnp.dot(head_out, out_proj, preferred_element_type=F32).astype(BF)]
    ppermute x29 -> x26, starting transfers between devices: 30 us -> 23.1 us  [shift(): return lax.ppermute(a, axis, [(i, (i + d) % n) for i in range(n)])]
    all_to_all x2 -> x1, starting transfers between devices: 11.7 us -> 5.06 us  [shards(): lax.all_to_all(out.reshape(NY, 64, -1), 'y', split_axis=0, concat_axis=0,...]
    pallas_call x3 -> x7, Pallas kernels: 34.6 us -> 40.7 us  [the longest x1 17.6 us: attention(): call(attention_kernel, 'attention', jax.ShapeDtypeStruct((ROWS, GRP * VDI...]
    unnamed x70 -> x58, local copies, waits for them, and re-layouts: 18 us -> 12.5 us
  transfers between devices with their start and end apart: 35 -> 31, of which waited for: 16 -> 13; matrix products, arithmetic and copies ran while one was open for 11% -> 5% of each run, Pallas kernels for 0% -> 15%
where the time goes in v2:
time: 234 us; the launch traced here: 230 us
  waiting for transfers between devices  78.4 us (34%)
  starting transfers between devices  52.3 us (22%)
  Pallas kernels  40.7 us (17%)
  blocking collectives  32.7 us (14%)
  local copies, waits for them, and re-layouts  19.3 us (8%)
  other arithmetic  5.72 us (2%)
    ppermute x26, waiting for transfers between devices, shift(): return lax.ppermute(a, axis, [(i, (i + d) % n) for i in range(n)])  50.9 us
    ppermute x26, starting transfers between devices, shift(): return lax.ppermute(a, axis, [(i, (i + d) % n) for i in range(n)])  23.1 us
    all_to_all x1, blocking collectives, shards(): lax.all_to_all(result.reshape(EXPERTS, SLOTS, CHUNK), ('y', 'x'), split_a...  22.5 us
    pallas_call x1, Pallas kernels, attention(): call(attention_kernel, 'attention', jax.ShapeDtypeStruct((ROWS, GRP * VDI...  17.6 us
    unnamed x58, local copies, waits for them, and re-layouts  12.5 us
    all_to_all x1, waiting for transfers between devices, shards(): lax.all_to_all(part, ('core', 'z'), split_axis=0, concat_axis=0, tiled=True)  11.3 us
    all_to_all x1, blocking collectives, shards(): done = lax.all_to_all(done, 'z', split_axis=0, concat_axis=0, tiled=True)  10.2 us
    pallas_call x1, Pallas kernels, project(): call(project_kernel, 'project', jax.ShapeDtypeStruct((2, NZ, NZ * BLK, CH...  9.42 us
  transfers between devices with their start and end apart: 31, of which 13 were waited for; matrix products, arithmetic and copies ran while one was open for 5% of the time, Pallas kernels for 15%

profile of v2, /device:TPU:40, one launch (start us, length us, event | category | flops | bytes accessed | tf_op | source)
XLA Modules:
  0.0 230.1 jit_solution(2949848488692090457)
XLA Ops:
  0.0 1.5 copy.34.c0
  2.3 1.5 collective-permute-start
  3.8 2.8 %dynamic-slice_bitcast_fusion.2 = (bf16[1792,128]{1,0:T(8,128)(2,1)}, bf16[1792,128]{1,0:T(8,128)(2,1)}, bf16[1792,128]{1,0:T(8,128)(2,1)S(1)}, bf16[1792,128]{1...) fusion(bf16[4,1792,128]{2,1,0:T(8,128)(2,1)S(1)} %bitcast.68, ...), kind=kLoop, calls=%fused_computation.7 | loop fusion | bytes 7340048 | tf_op jit(solution)/shard_map/weights/jit(dynamic_index_in_dim)/squeeze | solution.py:396
  6.5 1.0 pad_maximum_fusion
  7.6 1.9 collective-permute-start.1
  9.5 1.0 pad_maximum_fusion.1
  11.2 2.0 collective-permute-done.c1
  13.2 1.0 broadcast_in_dim.30
  14.2 8.1 %all-to-all-start = ((bf16[32,8,1664]{2,1,0:T(8,128)(2,1)}), bf16[32,8,1664]{2,1,0:T(8,128)(2,1)S(1)}, u32[]{:S(2)}, u32[]{:S(2)}) async-start(bf16[32,8,1664]{2,1,0:T(8,128)(2,1)} %bitcast.9), calls=%async_computation | async-start | bytes 1703936 | tf_op jit(solution)/shard_map/query_exchange/all_to_all | solution.py:385
  22.3 1.6 collective-permute-start.4
  24.8 1.3 dynamic-slice_bitcast_fusion
  26.5 1.1 pad_maximum_fusion.2
  27.7 10.0 %collective-permute-done.1.refs_2_ = bf16[1792,256]{1,0:T(8,128)(2,1)} collective-permute-done((bf16[1792,256]{1,0:T(8,128)(2,1)}, bf16[1792,256]{1,0:T(8,128)(2,1)}, u32[]{:S(2)}, u32[]{:S(2)}) %collective-permute-start.1) | collective-permute-done | bytes 917536 | tf_op jit(solution)/shard_map/weights/ppermute | solution.py:40
  37.7 2.4 %collective-permute-done.2.refs_6_ = bf16[1792,256]{1,0:T(8,128)(2,1)} collective-permute-done((bf16[1792,256]{1,0:T(8,128)(2,1)}, bf16[1792,256]{1,0:T(8,128)(2,1)}, u32[]{:S(2)}, u32[]{:S(2)}) %collective-permute-start.2) | collective-permute-done | bytes 917536 | tf_op jit(solution)/shard_map/weights/ppermute | solution.py:40
  40.1 1.5 all-to-all-done
  41.6 2.3 %collective-permute-start.8 = (bf16[1792,256]{1,0:T(8,128)(2,1)}, bf16[1792,256]{1,0:T(8,128)(2,1)}, u32[]{:S(2)}, u32[]{:S(2)}) collective-permute-start(bf16[1792,256]{1,0:T(8,128)(2,1)} %pad_maximum_fusion.2), channel_id=1, source_target_pairs={{0,4},{2,6},{4,0},{6,2},{1,5},{3,7},{5,1},{7,3},{8,12},{10,14},{12... | collective-permute-start | bytes 2752520 | tf_op jit(solution)/shard_map/attention/ppermute | solution.py:40
  45.1 0.9 collective-permute-done.7.s3
  46.7 1.1 collective-permute-start.10
  48.2 1.0 copy-done.17
  49.2 17.6 %attention.1 = bf16[256,1152]{1,0:T(8,128)(2,1)} custom-call(s32[7]{0:T(128)S(1)} %stack.41.pos_ref, bf16[256,1664]{1,0:T(8,128)(2,1)S(1)} %bitcast.62, s32[256,1]{1,0:T(8,128)S(1)} %copy.36.first_ref, s32[256,1]{1,0:T(8,128)S(1)} %select_n.193.last_ref, bf16[512,576]{1,0:T(8,128)(2,1)S(1)} %copy.34.c0, bf16[256,576]{1,0:T(8,128)(2,1)} %collective-permute-done.c1, ...), custom_call_target="tpu_custom_call" | custom-call | bytes 1 | tf_op jit(solution)/shard_map/attention/attention/pallas_call | solution.py:140
  66.8 5.1 %all-to-all-start.1 = ((bf16[4,64,1152]{2,1,0:T(8,128)(2,1)}), bf16[4,64,1152]{2,1,0:T(8,128)(2,1)S(1)}, u32[]{:S(2)}, u32[]{:S(2)}) async-start(bf16[4,64,1152]{2,1,0:T(8,128)(2,1)} %bitcast.22), calls=%async_computation.1 | async-start | bytes 1179648 | tf_op jit(solution)/shard_map/combine/all_to_all | solution.py:424
  71.9 1.3 pad_maximum_fusion.3.refs_0_
  73.2 7.5 %all-to-all-done.1.o_ref = bf16[4,64,1152]{2,1,0:T(8,128)(2,1)S(1)} async-done(((bf16[4,64,1152]{2,1,0:T(8,128)(2,1)}), bf16[4,64,1152]{2,1,0:T(8,128)(2,1)S(1)}, u32[]{:S(2)}, u32[]{:S(2)}) %all-to-all-start.1) | async-done | bytes 589856 | tf_op jit(solution)/shard_map/combine/all_to_all | solution.py:424
  81.8 9.4 %project.1 = bf16[2,4,32,1792]{3,2,1,0:T(8,128)(2,1)S(1)} custom-call(s32[1]{0:T(128)} %bitcast.own_ref, bf16[4,64,1152]{2,1,0:T(8,128)(2,1)S(1)} %all-to-all-done.1.o_ref, bf16[1024,7168]{1,0:T(8,128)(2,1)} %w_ref.1, bf16[8,7168]{1,0:T(8,128)(2,1)S(1)} %copy-done.20), custom_call_target="tpu_custom_call" | custom-call | bytes 1 | tf_op jit(solution)/shard_map/out_projection/project/pallas_call | solution.py:232
  91.2 1.0 copy-done
  92.2 5.5 %all-to-all-start.2 = ((bf16[8,32,1792]{2,1,0:T(8,128)(2,1)}), bf16[8,32,1792]{2,1,0:T(8,128)(2,1)S(1)}, u32[]{:S(2)}, u32[]{:S(2)}) async-start(bf16[8,32,1792]{2,1,0:T(8,128)(2,1)} %bitcast.65), calls=%async_computation.2 | async-start | bytes 1835008 | tf_op jit(solution)/shard_map/out_projection/all_to_all | solution.py:434
  99.0 11.3 %all-to-all-done.2.part_ref = bf16[8,32,1792]{2,1,0:T(8,128)(2,1)S(1)} async-done(((bf16[8,32,1792]{2,1,0:T(8,128)(2,1)}), bf16[8,32,1792]{2,1,0:T(8,128)(2,1)S(1)}, u32[]{:S(2)}, u32[]{:S(2)}) %all-to-all-start.2) | async-done | bytes 917536 | tf_op jit(solution)/shard_map/out_projection/all_to_all | solution.py:434
  111.0 1.1 copy-done.3
  112.1 6.1 %all-to-all-start.3 = ((bf16[16,24,1792]{2,1,0:T(8,128)(2,1)}), bf16[16,24,1792]{2,1,0:T(8,128)(2,1)}, u32[]{:S(2)}, u32[]{:S(2)}) async-start(bf16[16,24,1792]{2,1,0:T(8,128)(2,1)} %bitcast.66), calls=%async_computation.3 | async-start | bytes 2752512 | tf_op jit(solution)/shard_map/dispatch/all_to_all | solution.py:443
  118.2 1.9 collective-permute-start.15
  120.1 11.9 %collective-permute-done.15.refs_4_ = bf16[128,1792]{1,0:T(8,128)(2,1)S(1)} collective-permute-done((bf16[128,1792]{1,0:T(8,128)(2,1)}, bf16[128,1792]{1,0:T(8,128)(2,1)S(1)}, u32[]{:S(2)}, u32[]{:S(2)}) %collective-permute-start.15) | collective-permute-done | bytes 458784 | tf_op jit(solution)/shard_map/dispatch/ppermute | solution.py:40
  132.0 7.2 %all-to-all-done.3 = bf16[16,24,1792]{2,1,0:T(8,128)(2,1)} async-done(((bf16[16,24,1792]{2,1,0:T(8,128)(2,1)}), bf16[16,24,1792]{2,1,0:T(8,128)(2,1)}, u32[]{:S(2)}, u32[]{:S(2)}) %all-to-all-start.3) | async-done | bytes 1376288 | tf_op jit(solution)/shard_map/dispatch/all_to_all | solution.py:443
  140.2 7.9 %gate_up.1 = (bf16[4,384,512]{2,1,0:T(8,128)(2,1)}, f32[8,384]{1,0:T(8,128)S(1)}) custom-call(s32[1]{0:T(128)} %bitcast.31.z_ref, bf16[384,1792]{1,0:T(8,128)(2,1)} %bitcast.33.x_ref, f32[1,1792]{1,0:T(1,128)S(1)} %div.36.gain_ref, bf16[1792,256]{1,0:T(8,128)(2,1)S(1)} %pad_maximum_fusion.3.refs_0_, bf16[1792,256]{1,0:T(8,128)(2,1)} %collective-permute-done.11.refs_1_, ...), custom_call_target="tpu_custom_call" | custom-call | bytes 1 | tf_op jit(solution)/shard_map/experts/gate_up/pallas_call | solution.py:290
  151.3 4.5 %all-to-all-start.4 = ((bf16[4,384,512]{2,1,0:T(8,128)(2,1)}), bf16[4,384,512]{2,1,0:T(8,128)(2,1)S(1)}, u32[]{:S(2)}, u32[]{:S(2)}) async-start(bf16[4,384,512]{2,1,0:T(8,128)(2,1)} %get-tuple-element.77), calls=%async_computation.4 | async-start | bytes 3145728 | tf_op jit(solution)/shard_map/experts/all_to_all | solution.py:452
  155.9 2.8 %collective-permute-start.21 = (f32[8,384]{1,0:T(8,128)S(1)}, f32[8,384]{1,0:T(8,128)S(1)}, u32[]{:S(2)}, u32[]{:S(2)}) collective-permute-start(f32[8,384]{1,0:T(8,128)S(1)} %get-tuple-element.78.s0), channel_id=1, source_target_pairs={{0,4},{2,6},{4,0},{6,2},{1,5},{3,7},{5,1},{7,3},{8,12},{10,14},{12... | collective-permute-start | bytes 36872 | tf_op jit(solution)/shard_map/experts/ppermute | solution.py:40
  158.7 1.8 collective-permute-start.20
  160.5 12.9 %collective-permute-done.22.s3 = f32[8,384]{1,0:T(8,128)S(1)} collective-permute-done((f32[8,384]{1,0:T(8,128)S(1)}, f32[8,384]{1,0:T(8,128)S(1)}, u32[]{:S(2)}, u32[]{:S(2)}) %collective-permute-start.22) | collective-permute-done | bytes 12320 | tf_op jit(solution)/shard_map/experts/ppermute | solution.py:40
  173.4 2.7 %collective-permute-done.21.s2 = f32[8,384]{1,0:T(8,128)S(1)} collective-permute-done((f32[8,384]{1,0:T(8,128)S(1)}, f32[8,384]{1,0:T(8,128)S(1)}, u32[]{:S(2)}, u32[]{:S(2)}) %collective-permute-start.21) | collective-permute-done | bytes 12320 | tf_op jit(solution)/shard_map/experts/ppermute | solution.py:40
  176.6 1.4 collective-permute-start.25
  178.5 2.2 collective-permute-start.23
  180.7 6.2 %collective-permute-done.25.i3 = bf16[384,256]{1,0:T(8,128)(2,1)S(1)} collective-permute-done((bf16[384,256]{1,0:T(8,128)(2,1)S(1)}, bf16[384,256]{1,0:T(8,128)(2,1)S(1)}, u32[]{:S(2)}, u32[]{:S(2)}) %collective-permute-start.25) | collective-permute-done | bytes 196640 | tf_op jit(solution)/shard_map/experts/ppermute | solution.py:40
  186.9 1.8 collective-permute-done.23.i1
  188.7 1.0 copy-done.9
  189.8 1.0 copy-done.11
  190.8 1.0 copy-done.13
  191.8 4.3 %down.1 = bf16[384,1792]{1,0:T(8,128)(2,1)S(1)} custom-call(bf16[384,256]{1,0:T(8,128)(2,1)S(1)} %inner_act.1.i0, bf16[384,256]{1,0:T(8,128)(2,1)S(1)} %collective-permute-done.23.i1, bf16[384,256]{1,0:T(8,128)(2,1)S(1)} %collective-permute-done.24.i2, bf16[384,256]{1,0:T(8,128)(2,1)S(1)} %collective-permute-done.25.i3, bf16[128,1792]{1,0:T(8,128)(2,1)S(1)} %copy-done.2, ...), custom_call_target="tpu_custom_call" | custom-call | bytes 1 | tf_op jit(solution)/shard_map/experts/down/pallas_call | solution.py:332
  196.1 22.5 %all_to_all.35 = bf16[16,24,1792]{2,1,0:T(8,128)(2,1)S(1)} all-to-all(bf16[16,24,1792]{2,1,0:T(8,128)(2,1)S(1)} %bitcast.64), channel_id=1, replica_groups=mesh['y'=4,'x'=4,'z'=4,'core'=2] {'y','x'}, dimensions={0} | all-to-all | bytes 2752512 | tf_op jit(solution)/shard_map/return/all_to_all | solution.py:458
  219.3 10.2 %all_to_all.36 = bf16[4,8,1792]{2,1,0:T(8,128)(2,1)S(1)} all-to-all(bf16[4,8,1792]{2,1,0:T(8,128)(2,1)S(1)} %fusion), channel_id=1, replica_groups=mesh['y'=4,'x'=4,'z'=4,'core'=2] {'z'}, dimensions={0} | all-to-all | bytes 229376 | tf_op jit(solution)/shard_map/return/all_to_all | solution.py:463
  (123 shorter events, 14.5 us)
Async XLA Ops:
  0.0 3.8 %copy-start.24 = (bf16[1,7168,128]{2,1,0:T(8,128)(2,1)S(1)}, bf16[1,7168,128]{2,1,0:T(8,128)(2,1)}, u32[]{:S(2)}) copy-start(bf16[1,7168,128]{2,1,0:T(8,128)(2,1)} %param.24) | copy-start | bytes 5505028
  2.3 11.0 %collective-permute-start = (bf16[256,576]{1,0:T(8,128)(2,1)}, bf16[256,576]{1,0:T(8,128)(2,1)}, u32[]{:S(2)}, u32[]{:S(2)}) collective-permute-start(bf16[256,576]{1,0:T(8,128)(2,1)} %constant_dynamic-slice_fusion), channel_id=1, source_target_pairs={{0,8},{8,16},{16,24},{24,0},{1,9},{9,17},{17,25},{25,1},{2,10},{10... | collective-permute-start | bytes 884744 | tf_op jit(solution)/shard_map/cache_gather/ppermute | solution.py:40
  6.5 4.1 %copy-start.27 = (f32[8,8]{1,0:T(8,128)S(1)}, f32[8,8]{1,0:T(8,128)}, u32[]{:S(2)}) copy-start(f32[8,8]{1,0:T(8,128)} %param.21) | copy-start | bytes 772
  6.5 4.1 %copy-start.26 = (s32[8,8]{1,0:T(8,128)S(1)}, s32[8,8]{1,0:T(8,128)}, u32[]{:S(2)}) copy-start(s32[8,8]{1,0:T(8,128)} %param.20) | copy-start | bytes 772
  6.5 4.1 %slice-start = ((bf16[8,64,192]{2,1,0:T(8,128)(2,1)}), bf16[8,64,64]{2,1,0:T(8,128)(2,1)S(1)}, s32[]{:S(2)}) async-start(bf16[8,64,192]{2,1,0:T(8,128)(2,1)} %param.13), calls=%async_computation.7 | async-start | bytes 262144 | tf_op jit(solution)/shard_map/query_exchange/slice | solution.py:380
  6.5 4.3 %slice-start.1 = ((bf16[8,64,192]{2,1,0:T(8,128)(2,1)}), bf16[8,64,128]{2,1,0:T(8,128)(2,1)S(1)}, s32[]{:S(2)}) async-start(bf16[8,64,192]{2,1,0:T(8,128)(2,1)} %param.13), calls=%async_computation.8 | async-start | bytes 262144 | tf_op jit(solution)/shard_map/query_exchange/slice | solution.py:379
  7.6 30.1 %collective-permute-start.1 = (bf16[1792,256]{1,0:T(8,128)(2,1)}, bf16[1792,256]{1,0:T(8,128)(2,1)}, u32[]{:S(2)}, u32[]{:S(2)}) collective-permute-start(bf16[1792,256]{1,0:T(8,128)(2,1)} %pad_maximum_fusion), channel_id=1, source_target_pairs={{0,2},{2,4},{4,6},{6,0},{1,3},{3,5},{5,7},{7,1},{8,10},{10,12},{12... | collective-permute-start | bytes 2752520 | tf_op jit(solution)/shard_map/weights/ppermute | solution.py:40
  10.5 29.5 %collective-permute-start.2 = (bf16[1792,256]{1,0:T(8,128)(2,1)}, bf16[1792,256]{1,0:T(8,128)(2,1)}, u32[]{:S(2)}, u32[]{:S(2)}) collective-permute-start(bf16[1792,256]{1,0:T(8,128)(2,1)} %pad_maximum_fusion.1), channel_id=1, source_target_pairs={{0,6},{2,0},{4,2},{6,4},{1,7},{3,1},{5,3},{7,5},{8,14},{10,8},{12,... | collective-permute-start | bytes 2752520 | tf_op jit(solution)/shard_map/weights/ppermute | solution.py:40
  11.0 13.8 %copy-start.21 = (bf16[1,128,7168]{2,1,0:T(8,128)(2,1)S(1)}, bf16[1,128,7168]{2,1,0:T(8,128)(2,1)}, u32[]{:S(2)}) copy-start(bf16[1,128,7168]{2,1,0:T(8,128)(2,1)} %param.25) | copy-start | bytes 5505028
  14.2 27.4 %all-to-all-start = ((bf16[32,8,1664]{2,1,0:T(8,128)(2,1)}), bf16[32,8,1664]{2,1,0:T(8,128)(2,1)S(1)}, u32[]{:S(2)}, u32[]{:S(2)}) async-start(bf16[32,8,1664]{2,1,0:T(8,128)(2,1)} %bitcast.9), calls=%async_computation | async-start | bytes 1703936 | tf_op jit(solution)/shard_map/query_exchange/all_to_all | solution.py:385
  22.3 21.7 %collective-permute-start.4 = (bf16[256,576]{1,0:T(8,128)(2,1)}, bf16[256,576]{1,0:T(8,128)(2,1)}, u32[]{:S(2)}, u32[]{:S(2)}) collective-permute-start(bf16[256,576]{1,0:T(8,128)(2,1)} %constant_dynamic-slice_fusion), channel_id=1, source_target_pairs={{0,24},{8,0},{16,8},{24,16},{1,25},{9,1},{17,9},{25,17},{2,26},{10... | collective-permute-start | bytes 884744 | tf_op jit(solution)/shard_map/cache_gather/ppermute | solution.py:40
  24.0 21.0 %collective-permute-start.3 = (bf16[256,576]{1,0:T(8,128)(2,1)}, bf16[256,576]{1,0:T(8,128)(2,1)}, u32[]{:S(2)}, u32[]{:S(2)}) collective-permute-start(bf16[256,576]{1,0:T(8,128)(2,1)} %constant_dynamic-slice_fusion), channel_id=1, source_target_pairs={{0,16},{8,24},{16,0},{24,8},{1,17},{9,25},{17,1},{25,9},{2,18},{10... | collective-permute-start | bytes 884744 | tf_op jit(solution)/shard_map/cache_gather/ppermute | solution.py:40
  24.8 1.7 copy-start.23
  26.1 22.1 %copy-start.4 = (bf16[8,128,512]{2,1,0:T(8,128)(2,1)S(1)}, bf16[8,128,512]{2,1,0:T(8,128)(2,1)}, u32[]{:S(2)}) copy-start(bf16[8,128,512]{2,1,0:T(8,128)(2,1)} %ak_ref.1) | copy-start | bytes 3145732
  41.6 39.1 %collective-permute-start.8 = (bf16[1792,256]{1,0:T(8,128)(2,1)}, bf16[1792,256]{1,0:T(8,128)(2,1)}, u32[]{:S(2)}, u32[]{:S(2)}) collective-permute-start(bf16[1792,256]{1,0:T(8,128)(2,1)} %pad_maximum_fusion.2), channel_id=1, source_target_pairs={{0,4},{2,6},{4,0},{6,2},{1,5},{3,7},{5,1},{7,3},{8,12},{10,14},{12... | collective-permute-start | bytes 2752520 | tf_op jit(solution)/shard_map/attention/ppermute | solution.py:40
  44.1 1.9 collective-permute-start.7
  44.4 3.8 %collective-permute-start.5 = (bf16[256,576]{1,0:T(8,128)(2,1)}, bf16[256,576]{1,0:T(8,128)(2,1)}, u32[]{:S(2)}, u32[]{:S(2)}) collective-permute-start(bf16[256,576]{1,0:T(8,128)(2,1)} %collective-permute-done.c1), channel_id=1, source_target_pairs={{0,1},{1,0},{2,3},{3,2},{4,5},{5,4},{6,7},{7,6},{8,9},{9,8},{10,11... | collective-permute-start | bytes 884744 | tf_op jit(solution)/shard_map/cache_share/ppermute | solution.py:40
  45.0 3.2 %collective-permute-start.6 = (bf16[256,576]{1,0:T(8,128)(2,1)}, bf16[256,576]{1,0:T(8,128)(2,1)}, u32[]{:S(2)}, u32[]{:S(2)}) collective-permute-start(bf16[256,576]{1,0:T(8,128)(2,1)} %collective-permute-done.3.c2), channel_id=1, source_target_pairs={{0,1},{1,0},{2,3},{3,2},{4,5},{5,4},{6,7},{7,6},{8,9},{9,8},{10,11... | collective-permute-start | bytes 884744 | tf_op jit(solution)/shard_map/cache_share/ppermute | solution.py:40
  45.1 35.5 %collective-permute-start.9 = (bf16[128,1792]{1,0:T(8,128)(2,1)}, bf16[128,1792]{1,0:T(8,128)(2,1)S(1)}, u32[]{:S(2)}, u32[]{:S(2)}) collective-permute-start(bf16[128,1792]{1,0:T(8,128)(2,1)} %get-tuple-element.47), channel_id=1, source_target_pairs={{0,2},{2,4},{4,6},{6,0},{1,3},{3,5},{5,7},{7,1},{8,10},{10,12},{12... | collective-permute-start | bytes 1376264 | tf_op jit(solution)/shard_map/attention/ppermute | solution.py:40
  46.7 33.9 %collective-permute-start.10 = (bf16[128,1792]{1,0:T(8,128)(2,1)}, bf16[128,1792]{1,0:T(8,128)(2,1)}, u32[]{:S(2)}, u32[]{:S(2)}) collective-permute-start(bf16[128,1792]{1,0:T(8,128)(2,1)} %get-tuple-element.48), channel_id=1, source_target_pairs={{0,6},{2,0},{4,2},{6,4},{1,7},{3,1},{5,3},{7,5},{8,14},{10,8},{12,... | collective-permute-start | bytes 1376264 | tf_op jit(solution)/shard_map/attention/ppermute | solution.py:40
  66.8 14.9 %copy-start.20 = (bf16[8,7168]{1,0:T(8,128)(2,1)S(1)}, bf16[8,7168]{1,0:T(8,128)(2,1)}, u32[]{:S(2)}) copy-start(bf16[8,7168]{1,0:T(8,128)(2,1)} %res_ref.1) | copy-start | bytes 344068
  66.8 13.8 %all-to-all-start.1 = ((bf16[4,64,1152]{2,1,0:T(8,128)(2,1)}), bf16[4,64,1152]{2,1,0:T(8,128)(2,1)S(1)}, u32[]{:S(2)}, u32[]{:S(2)}) async-start(bf16[4,64,1152]{2,1,0:T(8,128)(2,1)} %bitcast.22), calls=%async_computation.1 | async-start | bytes 1179648 | tf_op jit(solution)/shard_map/combine/all_to_all | solution.py:424
  80.6 10.5 %copy-start.5 = (bf16[128,1792]{1,0:T(8,128)(2,1)}, bf16[128,1792]{1,0:T(8,128)(2,1)S(1)}, u32[]{:S(2)}) copy-start(bf16[128,1792]{1,0:T(8,128)(2,1)S(1)} %collective-permute-done.9.refs_2_) | copy-start | bytes 1376260
  80.7 29.7 %collective-permute-start.11 = (bf16[1792,256]{1,0:T(8,128)(2,1)S(1)}, bf16[1792,256]{1,0:T(8,128)(2,1)}, u32[]{:S(2)}, u32[]{:S(2)}) collective-permute-start(bf16[1792,256]{1,0:T(8,128)(2,1)S(1)} %pad_maximum_fusion.3.refs_0_), channel_id=1, source_target_pairs={{0,1},{1,0},{2,3},{3,2},{4,5},{5,4},{6,7},{7,6},{8,9},{9,8},{10,11... | collective-permute-start | bytes 2752520 | tf_op jit(solution)/shard_map/out_projection/ppermute | solution.py:40
  80.8 29.6 %collective-permute-start.12 = (bf16[1792,256]{1,0:T(8,128)(2,1)}, bf16[1792,256]{1,0:T(8,128)(2,1)}, u32[]{:S(2)}, u32[]{:S(2)}) collective-permute-start(bf16[1792,256]{1,0:T(8,128)(2,1)} %collective-permute-done.1.refs_2_), channel_id=1, source_target_pairs={{0,1},{1,0},{2,3},{3,2},{4,5},{5,4},{6,7},{7,6},{8,9},{9,8},{10,11... | collective-permute-start | bytes 2752520 | tf_op jit(solution)/shard_map/out_projection/ppermute | solution.py:40
  81.2 29.1 %collective-permute-start.13 = (bf16[1792,256]{1,0:T(8,128)(2,1)}, bf16[1792,256]{1,0:T(8,128)(2,1)}, u32[]{:S(2)}, u32[]{:S(2)}) collective-permute-start(bf16[1792,256]{1,0:T(8,128)(2,1)} %collective-permute-done.8.refs_4_), channel_id=1, source_target_pairs={{0,1},{1,0},{2,3},{3,2},{4,5},{5,4},{6,7},{7,6},{8,9},{9,8},{10,11... | collective-permute-start | bytes 2752520 | tf_op jit(solution)/shard_map/out_projection/ppermute | solution.py:40
  81.3 29.0 %collective-permute-start.14 = (bf16[1792,256]{1,0:T(8,128)(2,1)}, bf16[1792,256]{1,0:T(8,128)(2,1)}, u32[]{:S(2)}, u32[]{:S(2)}) collective-permute-start(bf16[1792,256]{1,0:T(8,128)(2,1)} %collective-permute-done.2.refs_6_), channel_id=1, source_target_pairs={{0,1},{1,0},{2,3},{3,2},{4,5},{5,4},{6,7},{7,6},{8,9},{9,8},{10,11... | collective-permute-start | bytes 2752520 | tf_op jit(solution)/shard_map/out_projection/ppermute | solution.py:40
  92.2 18.2 %all-to-all-start.2 = ((bf16[8,32,1792]{2,1,0:T(8,128)(2,1)}), bf16[8,32,1792]{2,1,0:T(8,128)(2,1)S(1)}, u32[]{:S(2)}, u32[]{:S(2)}) async-start(bf16[8,32,1792]{2,1,0:T(8,128)(2,1)} %bitcast.65), calls=%async_computation.2 | async-start | bytes 1835008 | tf_op jit(solution)/shard_map/out_projection/all_to_all | solution.py:434
  110.4 28.8 %copy-start.1 = (bf16[128,1792]{1,0:T(8,128)(2,1)S(1)}, bf16[128,1792]{1,0:T(8,128)(2,1)}, u32[]{:S(2)}) copy-start(bf16[128,1792]{1,0:T(8,128)(2,1)} %get-tuple-element.73.refs_0_) | copy-start | bytes 1376260
  110.4 28.8 %copy-start.6 = (bf16[128,1792]{1,0:T(8,128)(2,1)S(1)}, bf16[128,1792]{1,0:T(8,128)(2,1)}, u32[]{:S(2)}) copy-start(bf16[128,1792]{1,0:T(8,128)(2,1)} %copy-done.5) | copy-start | bytes 1376260
  112.1 36.1 %copy-start.18 = (f32[32,1792]{1,0:T(8,128)}, f32[32,1792]{1,0:T(8,128)S(1)}, u32[]{:S(2)}) copy-start(f32[32,1792]{1,0:T(8,128)S(1)} %get-tuple-element.60) | copy-start | bytes 688132
  112.1 27.1 %all-to-all-start.3 = ((bf16[16,24,1792]{2,1,0:T(8,128)(2,1)}), bf16[16,24,1792]{2,1,0:T(8,128)(2,1)}, u32[]{:S(2)}, u32[]{:S(2)}) async-start(bf16[16,24,1792]{2,1,0:T(8,128)(2,1)} %bitcast.66), calls=%async_computation.3 | async-start | bytes 2752512 | tf_op jit(solution)/shard_map/dispatch/all_to_all | solution.py:443
  118.2 13.9 %collective-permute-start.15 = (bf16[128,1792]{1,0:T(8,128)(2,1)}, bf16[128,1792]{1,0:T(8,128)(2,1)S(1)}, u32[]{:S(2)}, u32[]{:S(2)}) collective-permute-start(bf16[128,1792]{1,0:T(8,128)(2,1)} %get-tuple-element.63), channel_id=1, source_target_pairs={{0,4},{2,6},{4,0},{6,2},{1,5},{3,7},{5,1},{7,3},{8,12},{10,14},{12... | collective-permute-start | bytes 1376264 | tf_op jit(solution)/shard_map/dispatch/ppermute | solution.py:40
  139.2 9.0 %collective-permute-start.16 = (bf16[128,1792]{1,0:T(8,128)(2,1)S(1)}, bf16[128,1792]{1,0:T(8,128)(2,1)S(1)}, u32[]{:S(2)}, u32[]{:S(2)}) collective-permute-start(bf16[128,1792]{1,0:T(8,128)(2,1)S(1)} %copy-done.1), channel_id=1, source_target_pairs={{0,1},{1,0},{2,3},{3,2},{4,5},{5,4},{6,7},{7,6},{8,9},{9,8},{10,11... | collective-permute-start | bytes 1376264 | tf_op jit(solution)/shard_map/experts/ppermute | solution.py:40
  139.2 9.8 %collective-permute-start.17 = (bf16[128,1792]{1,0:T(8,128)(2,1)S(1)}, bf16[128,1792]{1,0:T(8,128)(2,1)S(1)}, u32[]{:S(2)}, u32[]{:S(2)}) collective-permute-start(bf16[128,1792]{1,0:T(8,128)(2,1)S(1)} %copy-done.6), channel_id=1, source_target_pairs={{0,1},{1,0},{2,3},{3,2},{4,5},{5,4},{6,7},{7,6},{8,9},{9,8},{10,11... | collective-permute-start | bytes 1376264 | tf_op jit(solution)/shard_map/experts/ppermute | solution.py:40
  139.7 10.0 %collective-permute-start.18 = (bf16[128,1792]{1,0:T(8,128)(2,1)S(1)}, bf16[128,1792]{1,0:T(8,128)(2,1)S(1)}, u32[]{:S(2)}, u32[]{:S(2)}) collective-permute-start(bf16[128,1792]{1,0:T(8,128)(2,1)S(1)} %collective-permute-done.15.refs_4_), channel_id=1, source_target_pairs={{0,1},{1,0},{2,3},{3,2},{4,5},{5,4},{6,7},{7,6},{8,9},{9,8},{10,11... | collective-permute-start | bytes 1376264 | tf_op jit(solution)/shard_map/experts/ppermute | solution.py:40
  139.8 10.7 %collective-permute-start.19 = (bf16[128,1792]{1,0:T(8,128)(2,1)}, bf16[128,1792]{1,0:T(8,128)(2,1)S(1)}, u32[]{:S(2)}, u32[]{:S(2)}) collective-permute-start(bf16[128,1792]{1,0:T(8,128)(2,1)} %collective-permute-done.10.refs_6_), channel_id=1, source_target_pairs={{0,1},{1,0},{2,3},{3,2},{4,5},{5,4},{6,7},{7,6},{8,9},{9,8},{10,11... | collective-permute-start | bytes 1376264 | tf_op jit(solution)/shard_map/experts/ppermute | solution.py:40
  151.3 37.4 %copy-start.2 = (bf16[128,1792]{1,0:T(8,128)(2,1)S(1)}, bf16[128,1792]{1,0:T(8,128)(2,1)}, u32[]{:S(2)}) copy-start(bf16[128,1792]{1,0:T(8,128)(2,1)} %get-tuple-element.73.refs_0_) | copy-start | bytes 1376260
  151.3 37.4 %copy-start.7 = (bf16[128,1792]{1,0:T(8,128)(2,1)S(1)}, bf16[128,1792]{1,0:T(8,128)(2,1)}, u32[]{:S(2)}) copy-start(bf16[128,1792]{1,0:T(8,128)(2,1)} %copy-done.5) | copy-start | bytes 1376260
  151.3 24.8 %all-to-all-start.4 = ((bf16[4,384,512]{2,1,0:T(8,128)(2,1)}), bf16[4,384,512]{2,1,0:T(8,128)(2,1)S(1)}, u32[]{:S(2)}, u32[]{:S(2)}) async-start(bf16[4,384,512]{2,1,0:T(8,128)(2,1)} %get-tuple-element.77), calls=%async_computation.4 | async-start | bytes 3145728 | tf_op jit(solution)/shard_map/experts/all_to_all | solution.py:452
  155.8 17.7 %collective-permute-start.22 = (f32[8,384]{1,0:T(8,128)S(1)}, f32[8,384]{1,0:T(8,128)S(1)}, u32[]{:S(2)}, u32[]{:S(2)}) collective-permute-start(f32[8,384]{1,0:T(8,128)S(1)} %get-tuple-element.78.s0), channel_id=1, source_target_pairs={{0,6},{2,0},{4,2},{6,4},{1,7},{3,1},{5,3},{7,5},{8,14},{10,8},{12,... | collective-permute-start | bytes 36872 | tf_op jit(solution)/shard_map/experts/ppermute | solution.py:40
  155.9 20.2 %collective-permute-start.21 = (f32[8,384]{1,0:T(8,128)S(1)}, f32[8,384]{1,0:T(8,128)S(1)}, u32[]{:S(2)}, u32[]{:S(2)}) collective-permute-start(f32[8,384]{1,0:T(8,128)S(1)} %get-tuple-element.78.s0), channel_id=1, source_target_pairs={{0,4},{2,6},{4,0},{6,2},{1,5},{3,7},{5,1},{7,3},{8,12},{10,14},{12... | collective-permute-start | bytes 36872 | tf_op jit(solution)/shard_map/experts/ppermute | solution.py:40
  158.7 17.4 %collective-permute-start.20 = (f32[8,384]{1,0:T(8,128)S(1)}, f32[8,384]{1,0:T(8,128)S(1)}, u32[]{:S(2)}, u32[]{:S(2)}) collective-permute-start(f32[8,384]{1,0:T(8,128)S(1)} %get-tuple-element.78.s0), channel_id=1, source_target_pairs={{0,2},{2,4},{4,6},{6,0},{1,3},{3,5},{5,7},{7,1},{8,10},{10,12},{12... | collective-permute-start | bytes 36872 | tf_op jit(solution)/shard_map/experts/ppermute | solution.py:40
  176.1 12.6 %copy-start.15 = (bf16[128,1792]{1,0:T(8,128)(2,1)S(1)}, bf16[128,1792]{1,0:T(8,128)(2,1)}, u32[]{:S(2)}) copy-start(bf16[128,1792]{1,0:T(8,128)(2,1)} %copy-done.14) | copy-start | bytes 1376260
  176.6 10.3 %collective-permute-start.25 = (bf16[384,256]{1,0:T(8,128)(2,1)S(1)}, bf16[384,256]{1,0:T(8,128)(2,1)S(1)}, u32[]{:S(2)}, u32[]{:S(2)}) collective-permute-start(bf16[384,256]{1,0:T(8,128)(2,1)S(1)} %inner_act.1.i0), channel_id=1, source_target_pairs={{0,6},{2,0},{4,2},{6,4},{1,7},{3,1},{5,3},{7,5},{8,14},{10,8},{12,... | collective-permute-start | bytes 589832 | tf_op jit(solution)/shard_map/experts/ppermute | solution.py:40
  178.0 8.9 %collective-permute-start.24 = (bf16[384,256]{1,0:T(8,128)(2,1)S(1)}, bf16[384,256]{1,0:T(8,128)(2,1)S(1)}, u32[]{:S(2)}, u32[]{:S(2)}) collective-permute-start(bf16[384,256]{1,0:T(8,128)(2,1)S(1)} %inner_act.1.i0), channel_id=1, source_target_pairs={{0,4},{2,6},{4,0},{6,2},{1,5},{3,7},{5,1},{7,3},{8,12},{10,14},{12... | collective-permute-start | bytes 589832 | tf_op jit(solution)/shard_map/experts/ppermute | solution.py:40
  178.5 10.2 %collective-permute-start.23 = (bf16[384,256]{1,0:T(8,128)(2,1)S(1)}, bf16[384,256]{1,0:T(8,128)(2,1)S(1)}, u32[]{:S(2)}, u32[]{:S(2)}) collective-permute-start(bf16[384,256]{1,0:T(8,128)(2,1)S(1)} %inner_act.1.i0), channel_id=1, source_target_pairs={{0,2},{2,4},{4,6},{6,0},{1,3},{3,5},{5,7},{7,1},{8,10},{10,12},{12... | collective-permute-start | bytes 589832 | tf_op jit(solution)/shard_map/experts/ppermute | solution.py:40
  196.1 23.1 %copy-start.19 = (f32[32,1792]{1,0:T(8,128)S(1)}, f32[32,1792]{1,0:T(8,128)}, u32[]{:S(2)}) copy-start(f32[32,1792]{1,0:T(8,128)} %copy-done.18) | copy-start | bytes 688132
  (13 other events, 12.8 us)

commit v3 on v2

--- a/solution.py
+++ b/solution.py
@@ -51,7 +51,7 @@
     return pl.CostEstimate(flops=flops, bytes_accessed=nbytes, transcendentals=0)
 
 
-def call(kernel, name, out_shape, in_specs, scratch, mib=48, **more):
+def call(kernel, name, out_shape, in_specs, scratch, mib=32, **more):
     return pl.pallas_call(
         kernel,
         out_shape=out_shape,
@@ -66,14 +66,19 @@
 
 VM = pl.BlockSpec(memory_space=pltpu.VMEM)
 SM = pl.BlockSpec(memory_space=pltpu.SMEM)
-AT = pl.BlockSpec(memory_space=pl.ANY)
+AT = pl.BlockSpec(memory_space=pltpu.HBM)
 PAIR = 2
 
 
 def attention_kernel(
-    pos_ref, q_ref, first_ref, last_ref, c0, c1, c2, c3, s1, s2, s3, ak_ref, av_ref, o_ref, kv, rp, st, hide, sem
+    pos_ref, q_ref, first_ref, last_ref, c0, c1, c2, c3, s1, s2, s3, ak_ref, av_ref, o0, o1, o2, o3, kv, rp, st, hide, sem
 ):
     g = pl.program_id(0)
+    outs = (o0, o1, o2, o3)
+
+    def query(at):
+        blocks = [lax.rem(pos_ref[7] + d, NY) for d in range(NY)]
+        return jnp.concatenate([q_ref[b, :, pl.ds(pl.multiple_of(at, 128), 128)] for b in blocks], axis=0)
 
     @pl.when(g == 0)
     def _():
@@ -98,9 +103,9 @@
     scored = []
     for i in range(PAIR):
         h = g * PAIR + i
-        nope = q_ref[:, pl.ds(pl.multiple_of(h * NOPE, NOPE), NOPE)]
+        nope = query(h * NOPE)
         q_lat = jnp.dot(nope, ak_ref[i], preferred_element_type=F32).astype(BF)
-        pair = q_ref[:, pl.ds(pl.multiple_of(GRP * NOPE + (h // 2) * 128, 128), 128)].astype(F32)
+        pair = query(GRP * NOPE + (h // 2) * 128).astype(F32)
         rope = jnp.where(lane // ROPE == h % 2, pair, 0.0).astype(BF)
         parts = []
         for j in range(0, KEYS, step):
@@ -122,9 +127,9 @@
             total = total + jnp.sum(p, axis=1, keepdims=True)
             acc = acc + jnp.dot(p.astype(BF), kv[n * step : (n + 1) * step, :LAT], preferred_element_type=F32)
         lat = (acc / total).astype(BF)
-        o_ref[:, pl.ds(pl.multiple_of(h * VDIM, VDIM), VDIM)] = jnp.dot(
-            lat, av_ref[i], preferred_element_type=F32
-        ).astype(BF)
+        head = jnp.dot(lat, av_ref[i], preferred_element_type=F32).astype(BF)
+        for d, o in enumerate(outs):
+            o[:, pl.ds(pl.multiple_of(h * VDIM, VDIM), VDIM)] = head[d * 64 : (d + 1) * 64]
         add = jnp.zeros((ROWS, 128), F32)
         for n, v in enumerate(split3(top) + split3(total)):
             add = add + jnp.where(lane == n * GRP + h, v, 0.0)
@@ -132,7 +137,8 @@
 
     @pl.when(g == GRP // PAIR - 1)
     def _():
-        o_ref[:, GRP * VDIM :] = st[...].astype(BF)
+        for d, o in enumerate(outs):
+            o[:, GRP * VDIM :] = st[d * 64 : (d + 1) * 64, :].astype(BF)
 
 
 def attention(place, q, first, last, pieces, absorb_key, absorb_value):
@@ -140,7 +146,7 @@
     return call(
         attention_kernel,
         "attention",
-        jax.ShapeDtypeStruct((ROWS, GRP * VDIM + 128), BF),
+        (jax.ShapeDtypeStruct((64, GRP * VDIM + 128), BF),) * NY,
         [SM, whole(q), whole(first), whole(last)]
         + [AT] * 7
         + [
@@ -155,7 +161,7 @@
             pltpu.SemaphoreType.DMA((7,)),
         ],
         grid=(GRP // PAIR,),
-        out_specs=pl.BlockSpec((ROWS, GRP * VDIM + 128), lambda g: (0, 0)),
+        out_specs=(pl.BlockSpec((64, GRP * VDIM + 128), lambda g: (0, 0)),) * NY,
     )(place, q, first, last, *pieces, absorb_key, absorb_value)
 
 
@@ -200,74 +206,124 @@
     )(at, cols, q)
 
 
-def project_kernel(own_ref, o_ref, w_ref, res_ref, out_ref, head_out):
-    @pl.when(pl.program_id(0) == 0)
-    def _():
-        tops, totals = [], []
-        for s in range(NY):
-            st = o_ref[s, :, GRP * VDIM :].astype(F32)
-            part = [st[:, n * GRP : (n + 1) * GRP] for n in range(6)]
-            tops.append(part[0] + part[1] + part[2])
-            totals.append(part[3] + part[4] + part[5])
-        top = jnp.maximum(jnp.maximum(tops[0], tops[1]), jnp.maximum(tops[2], tops[3]))
-        scale = LOG2E * (NOPE + ROPE) ** (-0.5)
-        share = [t * jnp.exp2((m - top) * scale) for m, t in zip(tops, totals)]
-        whole = share[0] + share[1] + share[2] + share[3]
-        share = [s / whole for s in share]
-        for h in range(GRP):
-            at = slice(h * VDIM, (h + 1) * VDIM)
-            total = sum(o_ref[s, :, at].astype(F32) * share[s][:, h : h + 1] for s in range(NY))
-            head_out[:, at] = total.astype(BF)
-
-    part = jnp.dot(head_out[...], w_ref[...], preferred_element_type=F32)
-    row = lax.broadcasted_iota(jnp.int32, part.shape, 0) // BLK
-    res = jnp.concatenate([res_ref[...].astype(F32)] * 8, axis=0)
-    part = (part + jnp.where(row == own_ref[0], res, 0.0)).astype(BF)
-    out_ref[0, 0] = part[: NZ * BLK]
-    out_ref[1, 0] = part[NZ * BLK :]
-
-
-def project(own, o, out_proj, residual):
-    width = CHUNK // 2
-    return call(
-        project_kernel,
+def merge_kernel(o0, o1, o2, o3, head_out):
+    outs = (o0, o1, o2, o3)
+    tops, totals = [], []
+    for o in outs:
+        st = o[:, GRP * VDIM :].astype(F32)
+        part = [st[:, n * GRP : (n + 1) * GRP] for n in range(6)]
+        tops.append(part[0] + part[1] + part[2])
+        totals.append(part[3] + part[4] + part[5])
+    top = jnp.maximum(jnp.maximum(tops[0], tops[1]), jnp.maximum(tops[2], tops[3]))
+    scale = LOG2E * (NOPE + ROPE) ** (-0.5)
+    share = [t * jnp.exp2((m - top) * scale) for m, t in zip(tops, totals)]
+    whole = share[0] + share[1] + share[2] + share[3]
+    share = [s / whole for s in share]
+    for h in range(GRP):
+        at = slice(h * VDIM, (h + 1) * VDIM)
+        total = sum(o[:, at].astype(F32) * share[s][:, h : h + 1] for s, o in enumerate(outs))
+        head_out[:, at] = total.astype(BF)
+
+
+def merge(outs):
+    return call(
+        merge_kernel,
+        "merge",
+        jax.ShapeDtypeStruct((64, GRP * VDIM), BF),
+        [VM] * 4,
+        [],
+        out_specs=VM,
+    )(*outs)
+
+
+def stage_kernel(token_ref, w_ref, held_ref, sem):
+    rows = w_ref.shape[0] // 8
+    copies = [
+        pltpu.make_async_copy(w_ref.at[pl.ds(i * rows, rows)], held_ref.at[pl.ds(i * rows, rows)], sem.at[i])
+        for i in range(8)
+    ]
+    for c in copies:
+        c.start()
+    for c in copies:
+        c.wait()
+
+
+def stage(token, w):
+    return call(
+        stage_kernel,
+        "stage",
+        pltpu.VMEM(w.shape, w.dtype),
+        [AT, AT],
+        [pltpu.SemaphoreType.DMA((8,))],
+        mib=44,
+        out_specs=VM,
+    )(token, w)
+
+
+def project_kernel(ways, own_ref, head_ref, w_ref, res_ref, *outs):
+    half = NZ * BLK
+    for n, d in enumerate(ways):
+        keep_ref, send_ref = outs[2 * n], outs[2 * n + 1]
+        at = pl.ds(pl.multiple_of(lax.rem(own_ref[1] + d, NZ) * CHUNK, CHUNK), CHUNK)
+        part = jnp.dot(head_ref[...], w_ref[:, at], preferred_element_type=F32)
+        row = lax.broadcasted_iota(jnp.int32, part.shape, 0) // BLK
+        res = jnp.concatenate([res_ref[:, at].astype(F32)] * 8, axis=0)
+        part = part + jnp.where(row == own_ref[0] * NZ + own_ref[1], res, 0.0)
+        low = jnp.broadcast_to(own_ref[0], (half, CHUNK)) == 0
+        keep_ref[...] = jnp.where(low, part[:half], part[half:])
+        send_ref[...] = jnp.where(low, part[half:], part[:half]).astype(BF)
+
+
+def project(ways, own, head_out, out_proj, residual):
+    shape = (NZ * BLK, CHUNK)
+    return call(
+        functools.partial(project_kernel, ways),
         "project",
-        jax.ShapeDtypeStruct((2, NZ, NZ * BLK, CHUNK), BF),
-        [
-            SM,
-            pl.BlockSpec(o.shape, lambda j: (0, 0, 0)),
-            pl.BlockSpec((GRP * VDIM, width), lambda j: (0, j)),
-            pl.BlockSpec((BLK, width), lambda j: (0, j)),
-        ],
-        [pltpu.VMEM((64, GRP * VDIM), BF)],
-        grid=(D // width,),
-        out_specs=pl.BlockSpec((2, 1, NZ * BLK, width), lambda j: (0, j // 2, 0, j % 2)),
-    )(own, o, out_proj, residual)
-
-
-def spread_kernel(part_ref, gain_ref, pick_ref, hidden_ref, rows_ref):
-    hidden = part_ref[0].astype(F32)
-    for s in range(1, 8):
-        hidden = hidden + part_ref[s].astype(F32)
+        (jax.ShapeDtypeStruct(shape, F32), jax.ShapeDtypeStruct(shape, BF)) * len(ways),
+        [SM] + [VM] * 3,
+        [],
+        out_specs=(VM,) * (2 * len(ways)),
+    )(own, head_out, out_proj, residual)
+
+
+def fold_kernel(n, *refs):
+    for keep, got, out in zip(refs[:n], refs[n : 2 * n], refs[2 * n :]):
+        out[...] = (keep[...] + got[...].astype(F32)).astype(BF)
+
+
+def fold(keeps, gots):
+    n = len(keeps)
+    return call(
+        functools.partial(fold_kernel, n),
+        "fold",
+        (jax.ShapeDtypeStruct((NZ * BLK, CHUNK), BF),) * n,
+        [VM] * (2 * n),
+        [],
+        out_specs=(VM,) * n,
+    )(*keeps, *gots)
+
+
+def spread_kernel(keep_ref, got_ref, p1, p2, p3, gain_ref, pick_ref, hidden_ref, rows_ref):
+    hidden = keep_ref[...] + got_ref[...].astype(F32) + p1[...].astype(F32) + p2[...].astype(F32) + p3[...].astype(F32)
     hidden_ref[...] = hidden
     scaled = (hidden * gain_ref[...]).astype(BF)
     tn = (((0,), (0,)), ((), ()))
     rows_ref[...] = lax.dot_general(pick_ref[...], scaled, tn, preferred_element_type=F32).astype(BF)
 
 
-def spread(part, gain, pick):
+def spread(parts, gain, pick):
     return call(
         spread_kernel,
         "spread",
-        (jax.ShapeDtypeStruct((NZ * BLK, CHUNK), F32), jax.ShapeDtypeStruct((EROWS, CHUNK), BF)),
-        [VM] * 3,
+        (jax.ShapeDtypeStruct((NZ * BLK, CHUNK), F32), pltpu.VMEM((EROWS, CHUNK), BF)),
+        [VM] * 7,
         [],
         out_specs=(VM, VM),
-    )(part, gain, pick)
+    )(*parts, gain, pick)
 
 
 def gate_up_kernel(z_ref, x_ref, gain_ref, *refs):
-    pieces, (o_ref, square_ref, w, sem) = refs[:8], refs[8:]
+    pieces, (o_ref, w, sem) = refs[:8], refs[8:]
     copies = [
         pltpu.make_async_copy(p, w.at[:, pl.ds(i * 256, 256)], sem.at[i]) for i, p in enumerate(pieces)
     ]
@@ -276,43 +332,48 @@
     x = x_ref[...]
     raw = x.astype(F32) * gain_ref[...]
     ones = jnp.ones((8, CHUNK), BF)
-    square_ref[...] = lax.dot_general(
+    square = lax.dot_general(
         ones, (raw * raw).astype(BF), (((1,), (1,)), ((), ())), preferred_element_type=F32
     )
+    row = lax.broadcasted_iota(jnp.int32, square.shape, 0)
+    hi, mid, low = split3(square)
+    coded = jnp.where(row == 0, hi, jnp.where(row == 1, mid, jnp.where(row == 2, low, 0.0)))
+    coded = jnp.concatenate([coded, jnp.zeros_like(coded)], axis=0).astype(BF)
+    coded = jnp.concatenate([coded, jnp.zeros((16, 512 - EROWS), BF)], axis=1)
     for d in range(NZ):
         copies[2 * d].wait()
         copies[2 * d + 1].wait()
         part = jnp.dot(x, w[:, d * 512 : (d + 1) * 512], preferred_element_type=F32).astype(BF)
-        o_ref[lax.rem(z_ref[0] + NZ - d, NZ)] = part
+        to = lax.rem(z_ref[0] + NZ - d, NZ)
+        o_ref[to, :EROWS] = part
+        o_ref[to, EROWS:] = coded
 
 
 def gate_up(z, x, gain, pieces):
     return call(
         gate_up_kernel,
         "gate_up",
-        (jax.ShapeDtypeStruct((NZ, EROWS, 512), BF), jax.ShapeDtypeStruct((8, EROWS), F32)),
+        pltpu.VMEM((NZ, EROWS + 16, 512), BF),
         [SM, VM, VM] + [AT] * 8,
         [pltpu.VMEM((CHUNK, 2048), BF), pltpu.SemaphoreType.DMA((8,))],
-        out_specs=(VM, VM),
+        out_specs=VM,
     )(z, x, gain, *pieces)
 
 
-def inner_kernel(part_ref, s0, s1, s2, s3, out_ref):
-    square = s0[...] + s1[...] + s2[...] + s3[...]
-    scale = lax.rsqrt(square / D + 1e-6).T[:, :1]
+def inner_kernel(part_ref, out_ref):
     total = part_ref[0].astype(F32)
     for s in range(1, NZ):
         total = total + part_ref[s].astype(F32)
-    total = total * scale
+    square = jnp.sum(total[EROWS : EROWS + 8], axis=0, keepdims=True)
+    scale = lax.rsqrt(jnp.broadcast_to(square[:, :EROWS], (8, EROWS)) / D + 1e-6).T[:, :1]
+    total = total[:EROWS] * scale
     for k in range(2):
         gate, up = total[:, k * 256 : k * 256 + 128], total[:, k * 256 + 128 : k * 256 + 256]
         out_ref[:, k * 128 : (k + 1) * 128] = (gate / (1.0 + jnp.exp(-gate)) * up).astype(BF)
 
 
-def inner_act(part, squares):
-    return call(
-        inner_kernel, "inner_act", jax.ShapeDtypeStruct((EROWS, 256), BF), [VM] * 5, [], out_specs=VM
-    )(part, *squares)
+def inner_act(part):
+    return call(inner_kernel, "inner_act", jax.ShapeDtypeStruct((EROWS, 256), BF), [VM], [], out_specs=VM)(part)
 
 
 def down_kernel(i0, i1, i2, i3, *refs):
@@ -332,7 +393,7 @@
     return call(
         down_kernel,
         "down",
-        jax.ShapeDtypeStruct((EROWS, CHUNK), BF),
+        pltpu.VMEM((EROWS, CHUNK), BF),
         [VM] * 4 + [AT] * 8,
         [pltpu.VMEM((1024, CHUNK), BF), pltpu.SemaphoreType.DMA((8,))],
         out_specs=VM,
@@ -342,6 +403,10 @@
 def after(arrays, token):
     out = lax.optimization_barrier(tuple(arrays) + (token,))
     return out[:-1]
+
+
+def turned(a, by):
+    return lax.dynamic_slice_in_dim(jnp.concatenate([a, a]), by, a.shape[0], axis=0).reshape(-1)
 
 
 def shards(
@@ -396,16 +461,15 @@
             u = lax.dynamic_index_in_dim(ups, to, 0, keepdims=False)
             gu.append(jnp.concatenate([g, u], axis=1))
             dn.append(lax.dynamic_slice_in_dim(downs, to * CHUNK, CHUNK, axis=1))
-        gu[1], gu[3] = shift(gu[1], "z", NZ, 1), shift(gu[3], "z", NZ, 3)
-
     with jax.named_scope("cache_share"):
         other = [shift(m, "core", 2, 1) for m in mine]
 
     with jax.named_scope("attention"):
         doc = lax.dynamic_index_in_dim(response_doc.reshape(NY, NX, NZ, 2, BLK), x, 1, keepdims=False)
-        doc = doc.transpose(0, 2, 1, 3).reshape(ROWS)
+        doc = turned(doc.transpose(0, 2, 1, 3).reshape(NY, 64), y)
         ids = jnp.arange(RESP, dtype=jnp.int32).reshape(NY, NX, NZ, 2, BLK)
-        ids = lax.dynamic_index_in_dim(ids, x, 1, keepdims=False).transpose(0, 2, 1, 3).reshape(ROWS)
+        ids = lax.dynamic_index_in_dim(ids, x, 1, keepdims=False).transpose(0, 2, 1, 3).reshape(NY, 64)
+        ids = turned(ids, y)
         start = jnp.sum((response_doc[None, :] < doc[:, None]).astype(jnp.int32), axis=1)
         far = jnp.int32(1 << 20)
         first = jnp.where(y == NY - 1, start, -far)[:, None]
@@ -413,44 +477,52 @@
         at = [x * 512]
         for core in (k, 1 - k):
             at += [((x - d) % NX) * 512 + core * HALF for d in range(1, NX)]
-        place_of = jnp.stack(at).astype(jnp.int32)
-
-        q, gu[1], gu[3] = lax.optimization_barrier((q, gu[1], gu[3]))
-        ahead = after([gu[2], dn[1], dn[3]], q)
-        gu[2], dn[1], dn[3] = shift(ahead[0], "z", NZ, 2), shift(ahead[1], "z", NZ, 1), shift(ahead[2], "z", NZ, 3)
-        out = attention(place_of, q, first, last, [latent_cache] + mine + other, absorb_key, absorb_value)
+        place_of = jnp.stack(at + [y]).astype(jnp.int32)
+
+        ahead = after(gu[1:], q)
+        gu = gu[:1] + [shift(w, "z", NZ, d + 1) for d, w in enumerate(ahead)]
+        outs = attention(place_of, q.reshape(NY, 64, QCOLS), first, last, [latent_cache] + mine + other, absorb_key, absorb_value)
 
     with jax.named_scope("combine"):
-        out = lax.all_to_all(out.reshape(NY, 64, -1), "y", split_axis=0, concat_axis=0, tiled=True)
+        held = stage(outs[0], out_proj)
+        outs = [outs[0]] + [shift(o, "y", NY, d + 1) for d, o in enumerate(outs[1:])]
 
     with jax.named_scope("routing"):
-        pick, blend = routing(((y * 2 + k) * NZ * BLK).reshape(1), after([q], out)[0])
+        pick, blend = routing(((y * 2 + k) * NZ * BLK).reshape(1), after([q], outs[0])[0])
 
     with jax.named_scope("out_projection"):
-        out, gu[2], dn[1], dn[3] = lax.optimization_barrier((out, gu[2], dn[1], dn[3]))
-        gu_other = [shift(w, "core", 2, 1) for w in after(gu, out)]
-        part = project((k * NZ + z).reshape(1), out, out_proj, residual)
-        part = part.reshape(8, NZ * BLK, CHUNK)
-        part = lax.all_to_all(part, ("core", "z"), split_axis=0, concat_axis=0, tiled=True)
+        own = jnp.stack([k, z])
+        head_out = merge(outs)
+        keep1, send1, keep2, send2 = project((1, 2), own, head_out, held, residual)
+        swap1 = [shift(a, "core", 2, 1) for a in (send1, send2)]
+        (head_out,) = after([head_out], send1)
+        keep3, send3, keep, send = project((3, 0), own, head_out, held, residual)
+        swap2 = [shift(a, "core", 2, 1) for a in (send3, send)]
+        keep, *moved = lax.optimization_barrier((keep, *gu[1:]))
+        gu = gu[:1] + list(moved)
+        part1, part2 = fold([keep1, keep2], swap1)
+        (part3,) = fold([keep3], swap2[:1])
+        parts = [shift(p, "z", NZ, d + 1) for d, p in enumerate((part1, part2, part3))]
+        parts = [keep, swap2[1]] + parts
 
     with jax.named_scope("dispatch"):
         gain = lax.dynamic_slice_in_dim(norm_gain, z * CHUNK, CHUNK)[None]
-        part, *gu_other = lax.optimization_barrier((part, *gu_other))
-        (ahead,) = after([dn[2]], part)
-        dn[2] = shift(ahead, "z", NZ, 2)
-        hidden, rows = spread(part, gain, pick)
+        gu_other = [shift(w, "core", 2, 1) for w in after(gu, keep)]
+        hidden, rows = spread(parts, gain, pick)
+        ahead = after(dn[1:], hidden)
+        dn = dn[:1] + [shift(w, "z", NZ, d + 1) for d, w in enumerate(ahead)]
         rows = rows.reshape(EXPERTS, SLOTS, CHUNK)
         rows = lax.all_to_all(rows, ("y", "x"), split_axis=0, concat_axis=0, tiled=True)
         rows = rows.reshape(EROWS, CHUNK)
 
     with jax.named_scope("experts"):
-        rows, dn[2] = lax.optimization_barrier((rows, dn[2]))
-        dn_other = [shift(w, "core", 2, 1) for w in after(dn, rows)]
-        part, square = gate_up(z.reshape(1), rows, 1.0 / gain, [w for pair in zip(gu, gu_other) for w in pair])
-        squares = [square] + [shift(square, "z", NZ, d) for d in range(1, NZ)]
-        part, *dn_other = lax.optimization_barrier((part, *dn_other))
+        rows, *gu_other = lax.optimization_barrier((rows, *gu_other))
+        part = gate_up(z.reshape(1), rows, 1.0 / gain, [w for pair in zip(gu, gu_other) for w in pair])
+        part, *moved = lax.optimization_barrier((part, *dn[1:]))
+        dn = dn[:1] + list(moved)
+        dn_other = [shift(w, "core", 2, 1) for w in after(dn, part)]
         part = lax.all_to_all(part, "z", split_axis=0, concat_axis=0, tiled=True)
-        inner = inner_act(part, squares)
+        inner = inner_act(part)
         inners = [inner] + [shift(inner, "z", NZ, d) for d in range(1, NZ)]
         result = down(inners, [w for pair in zip(dn, dn_other) for w in pair])
 

time: 234 us -> 210 us (0.90)
  waiting for transfers between devices: 78.4 us -> 53.9 us
  starting transfers between devices: 52.3 us -> 56.1 us
  local copies, waits for them, and re-layouts: 19.3 us -> 15.6 us
    ppermute x26 -> x33, waiting for transfers between devices: 50.9 us -> 17.8 us  [shift(): return lax.ppermute(a, axis, [(i, (i + d) % n) for i in range(n)])]
    all_to_all x1, waiting for transfers between devices: 0.01 us -> 18.9 us  [shards(): part = lax.all_to_all(part, 'z', split_axis=0, concat_axis=0, tiled=True)]
    all_to_all x2 -> x0, waiting for transfers between devices: 18.8 us -> none  [the longest x1 11.3 us: shards(): lax.all_to_all(part, ('core', 'z'), split_axis=0, concat_axis=0, tiled=True)]
    ppermute x26 -> x33, starting transfers between devices: 23.1 us -> 37.7 us  [shift(): return lax.ppermute(a, axis, [(i, (i + d) % n) for i in range(n)])]
    all_to_all x2 -> x0, starting transfers between devices: 10.6 us -> none  [the longest x1 5.52 us: shards(): lax.all_to_all(part, ('core', 'z'), split_axis=0, concat_axis=0, tiled=True)]
    all_to_all x1, waiting for transfers between devices: 1.52 us -> 8.9 us  [shards(): lax.all_to_all(q, ('y', 'core', 'z'), split_axis=0, concat_axis=0, tiled=...]
    unnamed x58 -> x28, local copies, waits for them, and re-layouts: 12.5 us -> 6.81 us
    pallas_call x4 -> x9, Pallas kernels: 39.3 us -> 37.1 us  [the longest x1 16.5 us: attention(): call(attention_kernel, 'attention', (jax.ShapeDtypeStruct((64, GRP * VDIM...]
  transfers between devices with their start and end apart: 31 -> 36, of which waited for: 13 -> 11; matrix products, arithmetic and copies ran while one was open for 5% -> 7% of each run, Pallas kernels for 15% -> 17%
where the time goes in v3:
time: 210 us; the launch traced here: 206 us
  starting transfers between devices  56.1 us (27%)
  waiting for transfers between devices  53.9 us (26%)
  Pallas kernels  38.5 us (18%)
  blocking collectives  34.9 us (17%)
  local copies, waits for them, and re-layouts  15.6 us (7%)
  other arithmetic  5.83 us (3%)
    ppermute x33, starting transfers between devices, shift(): return lax.ppermute(a, axis, [(i, (i + d) % n) for i in range(n)])  37.7 us
    all_to_all x1, blocking collectives, shards(): lax.all_to_all(result.reshape(EXPERTS, SLOTS, CHUNK), ('y', 'x'), split_a...  24.4 us
    all_to_all x1, waiting for transfers between devices, shards(): part = lax.all_to_all(part, 'z', split_axis=0, concat_axis=0, tiled=True)  18.9 us
    ppermute x33, waiting for transfers between devices, shift(): return lax.ppermute(a, axis, [(i, (i + d) % n) for i in range(n)])  17.8 us
    pallas_call x1, Pallas kernels, attention(): call(attention_kernel, 'attention', (jax.ShapeDtypeStruct((64, GRP * VDIM...  16.5 us
    all_to_all x1, blocking collectives, shards(): done = lax.all_to_all(done, 'z', split_axis=0, concat_axis=0, tiled=True)  10.5 us
    all_to_all x1, waiting for transfers between devices, shards(): lax.all_to_all(q, ('y', 'core', 'z'), split_axis=0, concat_axis=0, tiled=...  8.9 us
    all_to_all x1, waiting for transfers between devices, shards(): lax.all_to_all(rows, ('y', 'x'), split_axis=0, concat_axis=0, tiled=True)  8.25 us
  transfers between devices with their start and end apart: 36, of which 11 were waited for; matrix products, arithmetic and copies ran while one was open for 7% of the time, Pallas kernels for 17%

profile of v3, /device:TPU:40, one launch (start us, length us, event | category | flops | bytes accessed | tf_op | source)
XLA Modules:
  0.0 206.0 jit_solution(14022687255628486363)
XLA Ops:
  0.0 1.5 copy.34.c0
  1.5 0.7 constant_dynamic-slice_fusion.2
  2.2 1.5 collective-permute-start
  3.7 2.7 %collective-permute-start.1 = (bf16[256,576]{1,0:T(8,128)(2,1)}, bf16[256,576]{1,0:T(8,128)(2,1)}, u32[]{:S(2)}, u32[]{:S(2)}) collective-permute-start(bf16[256,576]{1,0:T(8,128)(2,1)} %constant_dynamic-slice_fusion.2), channel_id=1, source_target_pairs={{0,16},{8,24},{16,0},{24,8},{1,17},{9,25},{17,1},{25,9},{2,18},{10... | collective-permute-start | bytes 884744 | tf_op jit(solution)/shard_map/cache_gather/ppermute | solution.py:40
  6.5 1.4 collective-permute-start.2
  8.3 3.3 %dynamic-slice_bitcast_fusion.4 = (bf16[1792,128]{1,0:T(8,128)(2,1)}, bf16[1792,128]{1,0:T(8,128)(2,1)}, bf16[1792,128]{1,0:T(8,128)(2,1)S(1)}, bf16[1792,128]{1...) fusion(bf16[4,1792,128]{2,1,0:T(8,128)(2,1)} %bitcast.69, ...), kind=kLoop, calls=%fused_computation.12 | loop fusion | bytes 7340048 | tf_op jit(solution)/shard_map/weights/jit(dynamic_index_in_dim)/squeeze | solution.py:461
  11.6 1.1 pad_maximum_fusion
  13.1 1.1 pad_maximum_fusion.1
  14.2 1.0 broadcast_in_dim.30
  15.2 8.2 %all-to-all-start = ((bf16[32,8,1664]{2,1,0:T(8,128)(2,1)}), bf16[32,8,1664]{2,1,0:T(8,128)(2,1)S(1)}, u32[]{:S(2)}, u32[]{:S(2)}) async-start(bf16[32,8,1664]{2,1,0:T(8,128)(2,1)} %bitcast.68), calls=%async_computation | async-start | bytes 1703936 | tf_op jit(solution)/shard_map/query_exchange/all_to_all | solution.py:450
  23.6 2.2 %pad_maximum_fusion.2 = bf16[1792,256]{1,0:T(8,128)(2,1)} fusion(bf16[1792,128]{1,0:T(8,128)(2,1)} %get-tuple-element.112, bf16[1792,128]{1,0:T(8,128)(2,1)} %get-tuple-element.122), kind=kLoop, calls=%fused_computation.6 | loop fusion | flops 1835008 | bytes 1835008 | tf_op jit(solution)/shard_map/weights/concatenate | solution.py:462
  26.9 8.9 %all-to-all-done = bf16[32,8,1664]{2,1,0:T(8,128)(2,1)S(1)} async-done(((bf16[32,8,1664]{2,1,0:T(8,128)(2,1)}), bf16[32,8,1664]{2,1,0:T(8,128)(2,1)S(1)}, u32[]{:S(2)}, u32[]{:S(2)}) %all-to-all-start) | async-done | bytes 852000 | tf_op jit(solution)/shard_map/query_exchange/all_to_all | solution.py:450
  35.8 2.1 %collective-permute-start.10 = (bf16[1792,256]{1,0:T(8,128)(2,1)}, bf16[1792,256]{1,0:T(8,128)(2,1)}, u32[]{:S(2)}, u32[]{:S(2)}) collective-permute-start(bf16[1792,256]{1,0:T(8,128)(2,1)} %pad_maximum_fusion.1), channel_id=1, source_target_pairs={{0,4},{2,6},{4,0},{6,2},{1,5},{3,7},{5,1},{7,3},{8,12},{10,14},{12... | collective-permute-start | bytes 2752520 | tf_op jit(solution)/shard_map/attention/ppermute | solution.py:40
  37.9 1.4 collective-permute-start.11
  39.4 0.7 copy-done.6
  41.1 1.2 copy-done.2
  42.3 1.0 copy-done.7
  43.3 16.5 %attention.1 = (bf16[64,1152]{1,0:T(8,128)(2,1)S(1)}, bf16[64,1152]{1,0:T(8,128)(2,1)S(1)}, bf16[64,1152]{1,0:T(8,128)(2,1)S(1)}, bf16[64,1152]{1,0:T(8,128)(2,1)S(1)}) custom-call(s32[8]{0:T(128)S(1)} %stack.57.pos_ref, bf16[4,64,1664]{2,1,0:T(8,128)(2,1)S(1)} %bitcast.62, s32[256,1]{1,0:T(8,128)S(1)} %copy.36.first_ref, s32[256,1]{1,0:T(8,128)S(1)} %select_n.190.last_ref, ...), custom_call_target="tpu_custom_call" | custom-call | bytes 1 | tf_op jit(solution)/shard_map/attention/attention/pallas_call | solution.py:146
  60.4 0.8 collective-permute-start.6
  61.2 2.7 %collective-permute-start.7 = (bf16[64,1152]{1,0:T(8,128)(2,1)S(1)}, bf16[64,1152]{1,0:T(8,128)(2,1)S(1)}, u32[]{:S(2)}, u32[]{:S(2)}) collective-permute-start(bf16[64,1152]{1,0:T(8,128)(2,1)S(1)} %get-tuple-element.56), channel_id=1, source_target_pairs={{0,64},{32,96},{64,0},{96,32},{1,65},{33,97},{65,1},{97,33},{2,66}... | collective-permute-start | bytes 442376 | tf_op jit(solution)/shard_map/combine/ppermute | solution.py:40
  63.9 3.0 %collective-permute-done.6.o1 = bf16[64,1152]{1,0:T(8,128)(2,1)S(1)} collective-permute-done((bf16[64,1152]{1,0:T(8,128)(2,1)S(1)}, bf16[64,1152]{1,0:T(8,128)(2,1)S(1)}, u32[]{:S(2)}, u32[]{:S(2)}) %collective-permute-start.6) | collective-permute-done | bytes 147488 | tf_op jit(solution)/shard_map/combine/ppermute | solution.py:40
  66.9 4.1 %collective-permute-start.8 = (bf16[64,1152]{1,0:T(8,128)(2,1)S(1)}, bf16[64,1152]{1,0:T(8,128)(2,1)S(1)}, u32[]{:S(2)}, u32[]{:S(2)}) collective-permute-start(bf16[64,1152]{1,0:T(8,128)(2,1)S(1)} %get-tuple-element.57), channel_id=1, source_target_pairs={{0,96},{32,0},{64,32},{96,64},{1,97},{33,1},{65,33},{97,65},{2,98}... | collective-permute-start | bytes 442376 | tf_op jit(solution)/shard_map/combine/ppermute | solution.py:40
  71.0 5.3 %stage.1.w_ref = bf16[1024,7168]{1,0:T(8,128)(2,1)S(1)} custom-call(bf16[64,1152]{1,0:T(8,128)(2,1)} %copy-done.3, bf16[1024,7168]{1,0:T(8,128)(2,1)} %w_ref.1), custom_call_target="tpu_custom_call" | custom-call | bytes 1 | tf_op jit(solution)/shard_map/combine/stage/pallas_call | solution.py:252
  77.0 2.0 project.2
  79.0 2.0 project.3
  81.6 0.8 collective-permute-done.17.refs_1_
  83.7 1.2 collective-permute-start.18
  85.0 0.9 collective-permute-start.15
  85.9 4.1 %collective-permute-start.16 = (bf16[32,1792]{1,0:T(8,128)(2,1)S(1)}, bf16[32,1792]{1,0:T(8,128)(2,1)S(1)}, u32[]{:S(2)}, u32[]{:S(2)}) collective-permute-start(bf16[32,1792]{1,0:T(8,128)(2,1)S(1)} %get-tuple-element.70), channel_id=1, source_target_pairs={{0,4},{2,6},{4,0},{6,2},{1,5},{3,7},{5,1},{7,3},{8,12},{10,14},{12... | collective-permute-start | bytes 344072 | tf_op jit(solution)/shard_map/out_projection/ppermute | solution.py:40
  90.7 0.8 broadcast_divide_fusion
  91.9 1.0 collective-permute-done.16.p2
  93.5 1.1 copy-done
  94.6 4.6 %all-to-all-start.1 = ((bf16[16,24,1792]{2,1,0:T(8,128)(2,1)}), bf16[16,24,1792]{2,1,0:T(8,128)(2,1)S(1)}, u32[]{:S(2)}, u32[]{:S(2)}) async-start(bf16[16,24,1792]{2,1,0:T(8,128)(2,1)} %bitcast.66), calls=%async_computation.1 | async-start | bytes 2752512 | tf_op jit(solution)/shard_map/dispatch/all_to_all | solution.py:515
  99.7 2.5 %dynamic-slice_bitcast_fusion = (bf16[128,1792]{1,0:T(8,128)(2,1)S(1)}, bf16[128,1792]{1,0:T(8,128)(2,1)}, bf16[128,1792]{1,0:T(8,128)(2,1)}, bf16[128,1792]{1,0:T(8,128)(2,1)}) fusion(bf16[1,128,7168]{2,1,0:T(8,128)(2,1)} %param.25, s32[]{:T(128)S(6)} %select_n.189, s32[]{:T(128)S(6)} %select_n.187, s32[]{:T(128)S(6)} %select_n.186, s32[]{:T(128)S(6)} %select_n.188), kind=kLoop, calls=%fused_computation.8 | loop fusion | bytes 3670032 | tf_op jit(solution)/shard_map/weights/dynamic_slice | solution.py:463
  102.2 2.1 %collective-permute-start.23 = (bf16[128,1792]{1,0:T(8,128)(2,1)}, bf16[128,1792]{1,0:T(8,128)(2,1)S(1)}, u32[]{:S(2)}, u32[]{:S(2)}) collective-permute-start(bf16[128,1792]{1,0:T(8,128)(2,1)} %get-tuple-element.90), channel_id=1, source_target_pairs={{0,2},{2,4},{4,6},{6,0},{1,3},{3,5},{5,7},{7,1},{8,10},{10,12},{12... | collective-permute-start | bytes 1376264 | tf_op jit(solution)/shard_map/dispatch/ppermute | solution.py:40
  104.4 3.6 %collective-permute-start.24 = (bf16[128,1792]{1,0:T(8,128)(2,1)}, bf16[128,1792]{1,0:T(8,128)(2,1)}, u32[]{:S(2)}, u32[]{:S(2)}) collective-permute-start(bf16[128,1792]{1,0:T(8,128)(2,1)} %get-tuple-element.91), channel_id=1, source_target_pairs={{0,4},{2,6},{4,0},{6,2},{1,5},{3,7},{5,1},{7,3},{8,12},{10,14},{12... | collective-permute-start | bytes 1376264 | tf_op jit(solution)/shard_map/dispatch/ppermute | solution.py:40
  108.3 8.2 %all-to-all-done.1 = bf16[16,24,1792]{2,1,0:T(8,128)(2,1)S(1)} async-done(((bf16[16,24,1792]{2,1,0:T(8,128)(2,1)}), bf16[16,24,1792]{2,1,0:T(8,128)(2,1)S(1)}, u32[]{:S(2)}, u32[]{:S(2)}) %all-to-all-start.1) | async-done | bytes 1376288 | tf_op jit(solution)/shard_map/dispatch/all_to_all | solution.py:515
  116.6 6.7 %gate_up.1 = bf16[4,400,512]{2,1,0:T(8,128)(2,1)} custom-call(s32[1]{0:T(128)} %bitcast.1.z_ref, bf16[384,1792]{1,0:T(8,128)(2,1)S(1)} %bitcast.65, f32[1,1792]{1,0:T(1,128)S(1)} %div.36.gain_ref, bf16[1792,256]{1,0:T(8,128)(2,1)S(1)} %pad_maximum_fusion.3.refs_0_, bf16[1792,256]{1,0:T(8,128)(2,1)} %collective-permute-done.19.refs_1_, ...), custom_call_target="tpu_custom_call" | custom-call | bytes 1 | tf_op jit(solution)/shard_map/experts/gate_up/pallas_call | solution.py:353
  123.3 5.3 %collective-permute-done.25.refs_6_ = bf16[128,1792]{1,0:T(8,128)(2,1)} collective-permute-done((bf16[128,1792]{1,0:T(8,128)(2,1)}, bf16[128,1792]{1,0:T(8,128)(2,1)}, u32[]{:S(2)}, u32[]{:S(2)}) %collective-permute-start.25) | collective-permute-done | bytes 458784 | tf_op jit(solution)/shard_map/dispatch/ppermute | solution.py:40
  128.6 5.5 %all-to-all-start.2 = ((bf16[4,400,512]{2,1,0:T(8,128)(2,1)}), bf16[4,400,512]{2,1,0:T(8,128)(2,1)S(1)}, u32[]{:S(2)}, u32[]{:S(2)}) async-start(bf16[4,400,512]{2,1,0:T(8,128)(2,1)} %gate_up.1), calls=%async_computation.2 | async-start | bytes 3276800 | tf_op jit(solution)/shard_map/experts/all_to_all | solution.py:524
  135.1 18.9 %all-to-all-done.2.part_ref = bf16[4,400,512]{2,1,0:T(8,128)(2,1)S(1)} async-done(((bf16[4,400,512]{2,1,0:T(8,128)(2,1)}), bf16[4,400,512]{2,1,0:T(8,128)(2,1)S(1)}, u32[]{:S(2)}, u32[]{:S(2)}) %all-to-all-start.2) | async-done | bytes 1638432 | tf_op jit(solution)/shard_map/experts/all_to_all | solution.py:524
  154.5 3.5 %collective-permute-start.27 = (bf16[384,256]{1,0:T(8,128)(2,1)S(1)}, bf16[384,256]{1,0:T(8,128)(2,1)S(1)}, u32[]{:S(2)}, u32[]{:S(2)}) collective-permute-start(bf16[384,256]{1,0:T(8,128)(2,1)S(1)} %inner_act.1.i0), channel_id=1, source_target_pairs={{0,4},{2,6},{4,0},{6,2},{1,5},{3,7},{5,1},{7,3},{8,12},{10,14},{12... | collective-permute-start | bytes 589832 | tf_op jit(solution)/shard_map/experts/ppermute | solution.py:40
  158.6 3.4 %collective-permute-done.26.i1 = bf16[384,256]{1,0:T(8,128)(2,1)S(1)} collective-permute-done((bf16[384,256]{1,0:T(8,128)(2,1)S(1)}, bf16[384,256]{1,0:T(8,128)(2,1)S(1)}, u32[]{:S(2)}, u32[]{:S(2)}) %collective-permute-start.26) | collective-permute-done | bytes 196640 | tf_op jit(solution)/shard_map/experts/ppermute | solution.py:40
  162.0 1.6 collective-permute-done.27.i2
  163.7 2.1 %collective-permute-done.28.i3 = bf16[384,256]{1,0:T(8,128)(2,1)S(1)} collective-permute-done((bf16[384,256]{1,0:T(8,128)(2,1)S(1)}, bf16[384,256]{1,0:T(8,128)(2,1)S(1)}, u32[]{:S(2)}, u32[]{:S(2)}) %collective-permute-start.28) | collective-permute-done | bytes 196640 | tf_op jit(solution)/shard_map/experts/ppermute | solution.py:40
  165.7 4.0 %down.1 = bf16[384,1792]{1,0:T(8,128)(2,1)S(1)} custom-call(bf16[384,256]{1,0:T(8,128)(2,1)S(1)} %inner_act.1.i0, bf16[384,256]{1,0:T(8,128)(2,1)S(1)} %collective-permute-done.26.i1, bf16[384,256]{1,0:T(8,128)(2,1)S(1)} %collective-permute-done.27.i2, bf16[384,256]{1,0:T(8,128)(2,1)S(1)} %collective-permute-done.28.i3, ...), custom_call_target="tpu_custom_call" | custom-call | bytes 1 | tf_op jit(solution)/shard_map/experts/down/pallas_call | solution.py:393
  169.8 24.4 %all_to_all.25 = bf16[16,24,1792]{2,1,0:T(8,128)(2,1)S(1)} all-to-all(bf16[16,24,1792]{2,1,0:T(8,128)(2,1)S(1)} %bitcast.64), channel_id=1, replica_groups=mesh['y'=4,'x'=4,'z'=4,'core'=2] {'y','x'}, dimensions={0} | all-to-all | bytes 2752512 | tf_op jit(solution)/shard_map/return/all_to_all | solution.py:530
  194.9 10.5 %all_to_all.26 = bf16[4,8,1792]{2,1,0:T(8,128)(2,1)S(1)} all-to-all(bf16[4,8,1792]{2,1,0:T(8,128)(2,1)S(1)} %fusion.1), channel_id=1, replica_groups=mesh['y'=4,'x'=4,'z'=4,'core'=2] {'z'}, dimensions={0} | all-to-all | bytes 229376 | tf_op jit(solution)/shard_map/return/all_to_all | solution.py:535
  (114 shorter events, 12.1 us)
Async XLA Ops:
  0.0 8.1 %slice-start = ((bf16[8,64,192]{2,1,0:T(8,128)(2,1)}), bf16[8,64,128]{2,1,0:T(8,128)(2,1)S(1)}, s32[]{:S(2)}) async-start(bf16[8,64,192]{2,1,0:T(8,128)(2,1)} %param.13), calls=%async_computation.5 | async-start | bytes 262144 | tf_op jit(solution)/shard_map/query_exchange/slice | solution.py:444
  0.0 8.1 %slice-start.1 = ((bf16[8,64,192]{2,1,0:T(8,128)(2,1)}), bf16[8,64,64]{2,1,0:T(8,128)(2,1)S(1)}, s32[]{:S(2)}) async-start(bf16[8,64,192]{2,1,0:T(8,128)(2,1)} %param.13), calls=%async_computation.6 | async-start | bytes 262144 | tf_op jit(solution)/shard_map/query_exchange/slice | solution.py:445
  0.0 7.9 %copy-start.10 = (s32[1024]{0:T(1024)S(1)}, s32[1024]{0:T(1024)}, u32[]{:S(2)}) copy-start(s32[1024]{0:T(1024)} %param.22) | copy-start | bytes 12292
  0.0 8.0 %copy-start.12 = (f32[8,8]{1,0:T(8,128)S(1)}, f32[8,8]{1,0:T(8,128)}, u32[]{:S(2)}) copy-start(f32[8,8]{1,0:T(8,128)} %param.21) | copy-start | bytes 772
  0.0 8.1 %copy-start.11 = (s32[8,8]{1,0:T(8,128)S(1)}, s32[8,8]{1,0:T(8,128)}, u32[]{:S(2)}) copy-start(s32[8,8]{1,0:T(8,128)} %param.20) | copy-start | bytes 772
  2.2 12.0 %collective-permute-start = (bf16[256,576]{1,0:T(8,128)(2,1)}, bf16[256,576]{1,0:T(8,128)(2,1)S(1)}, u32[]{:S(2)}, u32[]{:S(2)}) collective-permute-start(bf16[256,576]{1,0:T(8,128)(2,1)} %constant_dynamic-slice_fusion.2), channel_id=1, source_target_pairs={{0,8},{8,16},{16,24},{24,0},{1,9},{9,17},{17,25},{25,1},{2,10},{10... | collective-permute-start | bytes 884744 | tf_op jit(solution)/shard_map/cache_gather/ppermute | solution.py:40
  3.7 22.5 %collective-permute-start.1 = (bf16[256,576]{1,0:T(8,128)(2,1)}, bf16[256,576]{1,0:T(8,128)(2,1)}, u32[]{:S(2)}, u32[]{:S(2)}) collective-permute-start(bf16[256,576]{1,0:T(8,128)(2,1)} %constant_dynamic-slice_fusion.2), channel_id=1, source_target_pairs={{0,16},{8,24},{16,0},{24,8},{1,17},{9,25},{17,1},{25,9},{2,18},{10... | collective-permute-start | bytes 884744 | tf_op jit(solution)/shard_map/cache_gather/ppermute | solution.py:40
  6.5 20.2 %collective-permute-start.2 = (bf16[256,576]{1,0:T(8,128)(2,1)}, bf16[256,576]{1,0:T(8,128)(2,1)}, u32[]{:S(2)}, u32[]{:S(2)}) collective-permute-start(bf16[256,576]{1,0:T(8,128)(2,1)} %constant_dynamic-slice_fusion.2), channel_id=1, source_target_pairs={{0,24},{8,0},{16,8},{24,16},{1,25},{9,1},{17,9},{25,17},{2,26},{10... | collective-permute-start | bytes 884744 | tf_op jit(solution)/shard_map/cache_gather/ppermute | solution.py:40
  15.2 25.9 %copy-start.1 = (bf16[8,128,512]{2,1,0:T(8,128)(2,1)S(1)}, bf16[8,128,512]{2,1,0:T(8,128)(2,1)}, u32[]{:S(2)}) copy-start(bf16[8,128,512]{2,1,0:T(8,128)(2,1)} %ak_ref.1) | copy-start | bytes 3145732
  15.2 20.6 %all-to-all-start = ((bf16[32,8,1664]{2,1,0:T(8,128)(2,1)}), bf16[32,8,1664]{2,1,0:T(8,128)(2,1)S(1)}, u32[]{:S(2)}, u32[]{:S(2)}) async-start(bf16[32,8,1664]{2,1,0:T(8,128)(2,1)} %bitcast.68), calls=%async_computation | async-start | bytes 1703936 | tf_op jit(solution)/shard_map/query_exchange/all_to_all | solution.py:450
  26.0 13.3 %collective-permute-start.3 = (bf16[256,576]{1,0:T(8,128)(2,1)S(1)}, bf16[256,576]{1,0:T(8,128)(2,1)S(1)}, u32[]{:S(2)}, u32[]{:S(2)}) collective-permute-start(bf16[256,576]{1,0:T(8,128)(2,1)S(1)} %collective-permute-done.c1), channel_id=1, source_target_pairs={{0,1},{1,0},{2,3},{3,2},{4,5},{5,4},{6,7},{7,6},{8,9},{9,8},{10,11... | collective-permute-start | bytes 884744 | tf_op jit(solution)/shard_map/cache_share/ppermute | solution.py:40
  26.3 14.8 %collective-permute-start.4 = (bf16[256,576]{1,0:T(8,128)(2,1)}, bf16[256,576]{1,0:T(8,128)(2,1)}, u32[]{:S(2)}, u32[]{:S(2)}) collective-permute-start(bf16[256,576]{1,0:T(8,128)(2,1)} %collective-permute-done.1.c2), channel_id=1, source_target_pairs={{0,1},{1,0},{2,3},{3,2},{4,5},{5,4},{6,7},{7,6},{8,9},{9,8},{10,11... | collective-permute-start | bytes 884744 | tf_op jit(solution)/shard_map/cache_share/ppermute | solution.py:40
  26.6 14.5 %collective-permute-start.5 = (bf16[256,576]{1,0:T(8,128)(2,1)}, bf16[256,576]{1,0:T(8,128)(2,1)}, u32[]{:S(2)}, u32[]{:S(2)}) collective-permute-start(bf16[256,576]{1,0:T(8,128)(2,1)} %collective-permute-done.2.c3), channel_id=1, source_target_pairs={{0,1},{1,0},{2,3},{3,2},{4,5},{5,4},{6,7},{7,6},{8,9},{9,8},{10,11... | collective-permute-start | bytes 884744 | tf_op jit(solution)/shard_map/cache_share/ppermute | solution.py:40
  35.8 49.2 %collective-permute-start.10 = (bf16[1792,256]{1,0:T(8,128)(2,1)}, bf16[1792,256]{1,0:T(8,128)(2,1)}, u32[]{:S(2)}, u32[]{:S(2)}) collective-permute-start(bf16[1792,256]{1,0:T(8,128)(2,1)} %pad_maximum_fusion.1), channel_id=1, source_target_pairs={{0,4},{2,6},{4,0},{6,2},{1,5},{3,7},{5,1},{7,3},{8,12},{10,14},{12... | collective-permute-start | bytes 2752520 | tf_op jit(solution)/shard_map/attention/ppermute | solution.py:40
  37.9 48.0 %collective-permute-start.11 = (bf16[1792,256]{1,0:T(8,128)(2,1)}, bf16[1792,256]{1,0:T(8,128)(2,1)}, u32[]{:S(2)}, u32[]{:S(2)}) collective-permute-start(bf16[1792,256]{1,0:T(8,128)(2,1)} %pad_maximum_fusion.2), channel_id=1, source_target_pairs={{0,6},{2,0},{4,2},{6,4},{1,7},{3,1},{5,3},{7,5},{8,14},{10,8},{12,... | collective-permute-start | bytes 2752520 | tf_op jit(solution)/shard_map/attention/ppermute | solution.py:40
  40.1 50.0 %collective-permute-start.9 = (bf16[1792,256]{1,0:T(8,128)(2,1)}, bf16[1792,256]{1,0:T(8,128)(2,1)}, u32[]{:S(2)}, u32[]{:S(2)}) collective-permute-start(bf16[1792,256]{1,0:T(8,128)(2,1)} %pad_maximum_fusion), channel_id=1, source_target_pairs={{0,2},{2,4},{4,6},{6,0},{1,3},{3,5},{5,7},{7,1},{8,10},{10,12},{12... | collective-permute-start | bytes 2752520 | tf_op jit(solution)/shard_map/attention/ppermute | solution.py:40
  41.1 1.2 copy-start.2
  60.4 6.4 %collective-permute-start.6 = (bf16[64,1152]{1,0:T(8,128)(2,1)S(1)}, bf16[64,1152]{1,0:T(8,128)(2,1)S(1)}, u32[]{:S(2)}, u32[]{:S(2)}) collective-permute-start(bf16[64,1152]{1,0:T(8,128)(2,1)S(1)} %get-tuple-element.55), channel_id=1, source_target_pairs={{0,32},{32,64},{64,96},{96,0},{1,33},{33,65},{65,97},{97,1},{2,34}... | collective-permute-start | bytes 442376 | tf_op jit(solution)/shard_map/combine/ppermute | solution.py:40
  61.2 15.2 %collective-permute-start.7 = (bf16[64,1152]{1,0:T(8,128)(2,1)S(1)}, bf16[64,1152]{1,0:T(8,128)(2,1)S(1)}, u32[]{:S(2)}, u32[]{:S(2)}) collective-permute-start(bf16[64,1152]{1,0:T(8,128)(2,1)S(1)} %get-tuple-element.56), channel_id=1, source_target_pairs={{0,64},{32,96},{64,0},{96,32},{1,65},{33,97},{65,1},{97,33},{2,66}... | collective-permute-start | bytes 442376 | tf_op jit(solution)/shard_map/combine/ppermute | solution.py:40
  66.9 9.5 %collective-permute-start.8 = (bf16[64,1152]{1,0:T(8,128)(2,1)S(1)}, bf16[64,1152]{1,0:T(8,128)(2,1)S(1)}, u32[]{:S(2)}, u32[]{:S(2)}) collective-permute-start(bf16[64,1152]{1,0:T(8,128)(2,1)S(1)} %get-tuple-element.57), channel_id=1, source_target_pairs={{0,96},{32,0},{64,32},{96,64},{1,97},{33,1},{65,33},{97,65},{2,98}... | collective-permute-start | bytes 442376 | tf_op jit(solution)/shard_map/combine/ppermute | solution.py:40
  71.0 5.4 %copy-start.4 = (bf16[64,1152]{1,0:T(8,128)(2,1)S(1)}, bf16[64,1152]{1,0:T(8,128)(2,1)}, u32[]{:S(2)}) copy-start(bf16[64,1152]{1,0:T(8,128)(2,1)} %copy-done.3) | copy-start | bytes 442372
  71.0 6.0 %copy-start.5 = (bf16[8,7168]{1,0:T(8,128)(2,1)S(1)}, bf16[8,7168]{1,0:T(8,128)(2,1)}, u32[]{:S(2)}) copy-start(bf16[8,7168]{1,0:T(8,128)(2,1)} %res_ref.3) | copy-start | bytes 344068
  79.0 3.6 %copy-start.8 = (bf16[1792,128]{1,0:T(8,128)(2,1)S(1)}, bf16[1792,128]{1,0:T(8,128)(2,1)}, u32[]{:S(2)}) copy-start(bf16[1792,128]{1,0:T(8,128)(2,1)} %get-tuple-element.111) | copy-start | bytes 1376260
  79.0 3.6 %copy-start.9 = (bf16[1792,128]{1,0:T(8,128)(2,1)S(1)}, bf16[1792,128]{1,0:T(8,128)(2,1)}, u32[]{:S(2)}) copy-start(bf16[1792,128]{1,0:T(8,128)(2,1)} %get-tuple-element.123) | copy-start | bytes 1376260
  81.0 1.4 collective-permute-start.17
  81.1 1.6 collective-permute-start.13
  82.4 1.3 collective-permute-start.14
  82.6 7.5 %collective-permute-start.12 = (bf16[32,1792]{1,0:T(8,128)(2,1)S(1)}, bf16[32,1792]{1,0:T(8,128)(2,1)S(1)}, u32[]{:S(2)}, u32[]{:S(2)}) collective-permute-start(bf16[32,1792]{1,0:T(8,128)(2,1)S(1)} %get-tuple-element.65), channel_id=1, source_target_pairs={{0,1},{1,0},{2,3},{3,2},{4,5},{5,4},{6,7},{7,6},{8,9},{9,8},{10,11... | collective-permute-start | bytes 344072 | tf_op jit(solution)/shard_map/out_projection/ppermute | solution.py:40
  83.7 8.2 %collective-permute-start.18 = (bf16[32,1792]{1,0:T(8,128)(2,1)S(1)}, bf16[32,1792]{1,0:T(8,128)(2,1)S(1)}, u32[]{:S(2)}, u32[]{:S(2)}) collective-permute-start(bf16[32,1792]{1,0:T(8,128)(2,1)S(1)} %fold.3), channel_id=1, source_target_pairs={{0,6},{2,0},{4,2},{6,4},{1,7},{3,1},{5,3},{7,5},{8,14},{10,8},{12,... | collective-permute-start | bytes 344072 | tf_op jit(solution)/shard_map/out_projection/ppermute | solution.py:40
  85.0 6.9 %collective-permute-start.15 = (bf16[32,1792]{1,0:T(8,128)(2,1)S(1)}, bf16[32,1792]{1,0:T(8,128)(2,1)S(1)}, u32[]{:S(2)}, u32[]{:S(2)}) collective-permute-start(bf16[32,1792]{1,0:T(8,128)(2,1)S(1)} %get-tuple-element.69), channel_id=1, source_target_pairs={{0,2},{2,4},{4,6},{6,0},{1,3},{3,5},{5,7},{7,1},{8,10},{10,12},{12... | collective-permute-start | bytes 344072 | tf_op jit(solution)/shard_map/out_projection/ppermute | solution.py:40
  85.9 7.0 %collective-permute-start.16 = (bf16[32,1792]{1,0:T(8,128)(2,1)S(1)}, bf16[32,1792]{1,0:T(8,128)(2,1)S(1)}, u32[]{:S(2)}, u32[]{:S(2)}) collective-permute-start(bf16[32,1792]{1,0:T(8,128)(2,1)S(1)} %get-tuple-element.70), channel_id=1, source_target_pairs={{0,4},{2,6},{4,0},{6,2},{1,5},{3,7},{5,1},{7,3},{8,12},{10,14},{12... | collective-permute-start | bytes 344072 | tf_op jit(solution)/shard_map/out_projection/ppermute | solution.py:40
  90.1 14.3 %collective-permute-start.19 = (bf16[1792,256]{1,0:T(8,128)(2,1)S(1)}, bf16[1792,256]{1,0:T(8,128)(2,1)}, u32[]{:S(2)}, u32[]{:S(2)}) collective-permute-start(bf16[1792,256]{1,0:T(8,128)(2,1)S(1)} %pad_maximum_fusion.3.refs_0_), channel_id=1, source_target_pairs={{0,1},{1,0},{2,3},{3,2},{4,5},{5,4},{6,7},{7,6},{8,9},{9,8},{10,11... | collective-permute-start | bytes 2752520 | tf_op jit(solution)/shard_map/dispatch/ppermute | solution.py:40
  90.2 17.7 %collective-permute-start.20 = (bf16[1792,256]{1,0:T(8,128)(2,1)}, bf16[1792,256]{1,0:T(8,128)(2,1)}, u32[]{:S(2)}, u32[]{:S(2)}) collective-permute-start(bf16[1792,256]{1,0:T(8,128)(2,1)} %collective-permute-done.9.refs_2_), channel_id=1, source_target_pairs={{0,1},{1,0},{2,3},{3,2},{4,5},{5,4},{6,7},{7,6},{8,9},{9,8},{10,11... | collective-permute-start | bytes 2752520 | tf_op jit(solution)/shard_map/dispatch/ppermute | solution.py:40
  93.5 1.1 copy-start
  94.6 22.0 %all-to-all-start.1 = ((bf16[16,24,1792]{2,1,0:T(8,128)(2,1)}), bf16[16,24,1792]{2,1,0:T(8,128)(2,1)S(1)}, u32[]{:S(2)}, u32[]{:S(2)}) async-start(bf16[16,24,1792]{2,1,0:T(8,128)(2,1)} %bitcast.66), calls=%async_computation.1 | async-start | bytes 2752512 | tf_op jit(solution)/shard_map/dispatch/all_to_all | solution.py:515
  99.2 9.1 %collective-permute-start.21 = (bf16[1792,256]{1,0:T(8,128)(2,1)}, bf16[1792,256]{1,0:T(8,128)(2,1)}, u32[]{:S(2)}, u32[]{:S(2)}) collective-permute-start(bf16[1792,256]{1,0:T(8,128)(2,1)} %collective-permute-done.10.refs_4_), channel_id=1, source_target_pairs={{0,1},{1,0},{2,3},{3,2},{4,5},{5,4},{6,7},{7,6},{8,9},{9,8},{10,11... | collective-permute-start | bytes 2752520 | tf_op jit(solution)/shard_map/dispatch/ppermute | solution.py:40
  99.2 9.1 %collective-permute-start.22 = (bf16[1792,256]{1,0:T(8,128)(2,1)}, bf16[1792,256]{1,0:T(8,128)(2,1)}, u32[]{:S(2)}, u32[]{:S(2)}) collective-permute-start(bf16[1792,256]{1,0:T(8,128)(2,1)} %collective-permute-done.11.refs_6_), channel_id=1, source_target_pairs={{0,1},{1,0},{2,3},{3,2},{4,5},{5,4},{6,7},{7,6},{8,9},{9,8},{10,11... | collective-permute-start | bytes 2752520 | tf_op jit(solution)/shard_map/dispatch/ppermute | solution.py:40
  102.2 21.0 %collective-permute-start.23 = (bf16[128,1792]{1,0:T(8,128)(2,1)}, bf16[128,1792]{1,0:T(8,128)(2,1)S(1)}, u32[]{:S(2)}, u32[]{:S(2)}) collective-permute-start(bf16[128,1792]{1,0:T(8,128)(2,1)} %get-tuple-element.90), channel_id=1, source_target_pairs={{0,2},{2,4},{4,6},{6,0},{1,3},{3,5},{5,7},{7,1},{8,10},{10,12},{12... | collective-permute-start | bytes 1376264 | tf_op jit(solution)/shard_map/dispatch/ppermute | solution.py:40
  104.4 18.9 %collective-permute-start.24 = (bf16[128,1792]{1,0:T(8,128)(2,1)}, bf16[128,1792]{1,0:T(8,128)(2,1)}, u32[]{:S(2)}, u32[]{:S(2)}) collective-permute-start(bf16[128,1792]{1,0:T(8,128)(2,1)} %get-tuple-element.91), channel_id=1, source_target_pairs={{0,4},{2,6},{4,0},{6,2},{1,5},{3,7},{5,1},{7,3},{8,12},{10,14},{12... | collective-permute-start | bytes 1376264 | tf_op jit(solution)/shard_map/dispatch/ppermute | solution.py:40
  107.9 20.6 %collective-permute-start.25 = (bf16[128,1792]{1,0:T(8,128)(2,1)}, bf16[128,1792]{1,0:T(8,128)(2,1)}, u32[]{:S(2)}, u32[]{:S(2)}) collective-permute-start(bf16[128,1792]{1,0:T(8,128)(2,1)} %get-tuple-element.92), channel_id=1, source_target_pairs={{0,6},{2,0},{4,2},{6,4},{1,7},{3,1},{5,3},{7,5},{8,14},{10,8},{12,... | collective-permute-start | bytes 1376264 | tf_op jit(solution)/shard_map/dispatch/ppermute | solution.py:40
  128.6 25.4 %all-to-all-start.2 = ((bf16[4,400,512]{2,1,0:T(8,128)(2,1)}), bf16[4,400,512]{2,1,0:T(8,128)(2,1)S(1)}, u32[]{:S(2)}, u32[]{:S(2)}) async-start(bf16[4,400,512]{2,1,0:T(8,128)(2,1)} %gate_up.1), calls=%async_computation.2 | async-start | bytes 3276800 | tf_op jit(solution)/shard_map/experts/all_to_all | solution.py:524
  134.0 20.5 %collective-permute-start.29 = (bf16[128,1792]{1,0:T(8,128)(2,1)S(1)}, bf16[128,1792]{1,0:T(8,128)(2,1)S(1)}, u32[]{:S(2)}, u32[]{:S(2)}) collective-permute-start(bf16[128,1792]{1,0:T(8,128)(2,1)S(1)} %get-tuple-element.97.refs_0_), channel_id=1, source_target_pairs={{0,1},{1,0},{2,3},{3,2},{4,5},{5,4},{6,7},{7,6},{8,9},{9,8},{10,11... | collective-permute-start | bytes 1376264 | tf_op jit(solution)/shard_map/experts/ppermute | solution.py:40
  134.0 24.0 %collective-permute-start.30 = (bf16[128,1792]{1,0:T(8,128)(2,1)S(1)}, bf16[128,1792]{1,0:T(8,128)(2,1)}, u32[]{:S(2)}, u32[]{:S(2)}) collective-permute-start(bf16[128,1792]{1,0:T(8,128)(2,1)S(1)} %collective-permute-done.23.refs_2_), channel_id=1, source_target_pairs={{0,1},{1,0},{2,3},{3,2},{4,5},{5,4},{6,7},{7,6},{8,9},{9,8},{10,11... | collective-permute-start | bytes 1376264 | tf_op jit(solution)/shard_map/experts/ppermute | solution.py:40
  134.6 24.0 %collective-permute-start.31 = (bf16[128,1792]{1,0:T(8,128)(2,1)}, bf16[128,1792]{1,0:T(8,128)(2,1)}, u32[]{:S(2)}, u32[]{:S(2)}) collective-permute-start(bf16[128,1792]{1,0:T(8,128)(2,1)} %collective-permute-done.24.refs_4_), channel_id=1, source_target_pairs={{0,1},{1,0},{2,3},{3,2},{4,5},{5,4},{6,7},{7,6},{8,9},{9,8},{10,11... | collective-permute-start | bytes 1376264 | tf_op jit(solution)/shard_map/experts/ppermute | solution.py:40
  134.6 24.0 %collective-permute-start.32 = (bf16[128,1792]{1,0:T(8,128)(2,1)}, bf16[128,1792]{1,0:T(8,128)(2,1)}, u32[]{:S(2)}, u32[]{:S(2)}) collective-permute-start(bf16[128,1792]{1,0:T(8,128)(2,1)} %collective-permute-done.25.refs_6_), channel_id=1, source_target_pairs={{0,1},{1,0},{2,3},{3,2},{4,5},{5,4},{6,7},{7,6},{8,9},{9,8},{10,11... | collective-permute-start | bytes 1376264 | tf_op jit(solution)/shard_map/experts/ppermute | solution.py:40
  154.4 7.6 %collective-permute-start.26 = (bf16[384,256]{1,0:T(8,128)(2,1)S(1)}, bf16[384,256]{1,0:T(8,128)(2,1)S(1)}, u32[]{:S(2)}, u32[]{:S(2)}) collective-permute-start(bf16[384,256]{1,0:T(8,128)(2,1)S(1)} %inner_act.1.i0), channel_id=1, source_target_pairs={{0,2},{2,4},{4,6},{6,0},{1,3},{3,5},{5,7},{7,1},{8,10},{10,12},{12... | collective-permute-start | bytes 589832 | tf_op jit(solution)/shard_map/experts/ppermute | solution.py:40
  154.5 9.1 %collective-permute-start.27 = (bf16[384,256]{1,0:T(8,128)(2,1)S(1)}, bf16[384,256]{1,0:T(8,128)(2,1)S(1)}, u32[]{:S(2)}, u32[]{:S(2)}) collective-permute-start(bf16[384,256]{1,0:T(8,128)(2,1)S(1)} %inner_act.1.i0), channel_id=1, source_target_pairs={{0,4},{2,6},{4,0},{6,2},{1,5},{3,7},{5,1},{7,3},{8,12},{10,14},{12... | collective-permute-start | bytes 589832 | tf_op jit(solution)/shard_map/experts/ppermute | solution.py:40
  158.0 7.7 %collective-permute-start.28 = (bf16[384,256]{1,0:T(8,128)(2,1)S(1)}, bf16[384,256]{1,0:T(8,128)(2,1)S(1)}, u32[]{:S(2)}, u32[]{:S(2)}) collective-permute-start(bf16[384,256]{1,0:T(8,128)(2,1)S(1)} %inner_act.1.i0), channel_id=1, source_target_pairs={{0,6},{2,0},{4,2},{6,4},{1,7},{3,1},{5,3},{7,5},{8,14},{10,8},{12,... | collective-permute-start | bytes 589832 | tf_op jit(solution)/shard_map/experts/ppermute | solution.py:40
  (3 other events, 2.4 us)

commit v4 on v3

--- a/solution.py
+++ b/solution.py
@@ -322,13 +322,34 @@
     )(*parts, gain, pick)
 
 
-def gate_up_kernel(z_ref, x_ref, gain_ref, *refs):
-    pieces, (o_ref, w, sem) = refs[:8], refs[8:]
-    copies = [
-        pltpu.make_async_copy(p, w.at[:, pl.ds(i * 256, 256)], sem.at[i]) for i, p in enumerate(pieces)
-    ]
+def gather_kernel(axis, *refs):
+    pieces, (held_ref, sem) = refs[:8], refs[8:]
+    n = pieces[0].shape[axis]
+    copies = []
+    for i, p in enumerate(pieces):
+        to = held_ref.at[:, pl.ds(i * n, n)] if axis else held_ref.at[pl.ds(i * n, n)]
+        copies.append(pltpu.make_async_copy(p, to, sem.at[i]))
     for c in copies:
         c.start()
+    for c in copies:
+        c.wait()
+
+
+def gather(axis, name, pieces):
+    shape = list(pieces[0].shape)
+    shape[axis] *= 8
+    return call(
+        functools.partial(gather_kernel, axis),
+        name,
+        pltpu.VMEM(tuple(shape), BF),
+        [AT] * 8,
+        [pltpu.SemaphoreType.DMA((8,))],
+        mib=16,
+        out_specs=VM,
+    )(*pieces)
+
+
+def gate_up_kernel(z_ref, x_ref, gain_ref, w, o_ref):
     x = x_ref[...]
     raw = x.astype(F32) * gain_ref[...]
     ones = jnp.ones((8, CHUNK), BF)
@@ -341,23 +362,21 @@
     coded = jnp.concatenate([coded, jnp.zeros_like(coded)], axis=0).astype(BF)
     coded = jnp.concatenate([coded, jnp.zeros((16, 512 - EROWS), BF)], axis=1)
     for d in range(NZ):
-        copies[2 * d].wait()
-        copies[2 * d + 1].wait()
         part = jnp.dot(x, w[:, d * 512 : (d + 1) * 512], preferred_element_type=F32).astype(BF)
         to = lax.rem(z_ref[0] + NZ - d, NZ)
         o_ref[to, :EROWS] = part
         o_ref[to, EROWS:] = coded
 
 
-def gate_up(z, x, gain, pieces):
+def gate_up(z, x, gain, held):
     return call(
         gate_up_kernel,
         "gate_up",
         pltpu.VMEM((NZ, EROWS + 16, 512), BF),
-        [SM, VM, VM] + [AT] * 8,
-        [pltpu.VMEM((CHUNK, 2048), BF), pltpu.SemaphoreType.DMA((8,))],
+        [SM] + [VM] * 3,
+        [],
         out_specs=VM,
-    )(z, x, gain, *pieces)
+    )(z, x, gain, held)
 
 
 def inner_kernel(part_ref, out_ref):
@@ -376,28 +395,20 @@
     return call(inner_kernel, "inner_act", jax.ShapeDtypeStruct((EROWS, 256), BF), [VM], [], out_specs=VM)(part)
 
 
-def down_kernel(i0, i1, i2, i3, *refs):
-    pieces, (o_ref, w, sem) = refs[:8], refs[8:]
-    copies = [
-        pltpu.make_async_copy(p, w.at[pl.ds(i * 128, 128)], sem.at[i]) for i, p in enumerate(pieces)
-    ]
-    for c in copies:
-        c.start()
+def down_kernel(i0, i1, i2, i3, w, o_ref):
     inner = jnp.concatenate([i0[...], i1[...], i2[...], i3[...]], axis=1)
-    for c in copies:
-        c.wait()
     o_ref[...] = jnp.dot(inner, w[...], preferred_element_type=F32).astype(BF)
 
 
-def down(inners, pieces):
+def down(inners, held):
     return call(
         down_kernel,
         "down",
         pltpu.VMEM((EROWS, CHUNK), BF),
-        [VM] * 4 + [AT] * 8,
-        [pltpu.VMEM((1024, CHUNK), BF), pltpu.SemaphoreType.DMA((8,))],
+        [VM] * 5,
+        [],
         out_specs=VM,
-    )(*inners, *pieces)
+    )(*inners, held)
 
 
 def after(arrays, token):
@@ -516,15 +527,16 @@
         rows = rows.reshape(EROWS, CHUNK)
 
     with jax.named_scope("experts"):
-        rows, *gu_other = lax.optimization_barrier((rows, *gu_other))
-        part = gate_up(z.reshape(1), rows, 1.0 / gain, [w for pair in zip(gu, gu_other) for w in pair])
+        held = gather(1, "gate_up_weights", [w for pair in zip(gu, gu_other) for w in pair])
+        part = gate_up(z.reshape(1), rows, 1.0 / gain, held)
         part, *moved = lax.optimization_barrier((part, *dn[1:]))
         dn = dn[:1] + list(moved)
         dn_other = [shift(w, "core", 2, 1) for w in after(dn, part)]
         part = lax.all_to_all(part, "z", split_axis=0, concat_axis=0, tiled=True)
         inner = inner_act(part)
         inners = [inner] + [shift(inner, "z", NZ, d) for d in range(1, NZ)]
-        result = down(inners, [w for pair in zip(dn, dn_other) for w in pair])
+        held = gather(0, "down_weights", [w for pair in zip(dn, dn_other) for w in pair])
+        result = down(inners, held)
 
     with jax.named_scope("return"):
         back = lax.all_to_all(

time: 210 us -> 209 us (level)
  local copies, waits for them, and re-layouts: 15.6 us -> 21.7 us
  waiting for transfers between devices: 53.9 us -> 48.6 us
  starting transfers between devices: 56.1 us -> 51.6 us
    unnamed x28 -> x34, local copies, waits for them, and re-layouts: 6.81 us -> 12.9 us
    ppermute x33, starting transfers between devices: 37.7 us -> 34.2 us  [shift(): return lax.ppermute(a, axis, [(i, (i + d) % n) for i in range(n)])]
    ppermute x33, waiting for transfers between devices: 17.8 us -> 14.7 us  [shift(): return lax.ppermute(a, axis, [(i, (i + d) % n) for i in range(n)])]
    pallas_call x1 -> x3, Pallas kernels: 4.04 us -> 7.07 us  [the longest x2 5.49 us: gather(): call(functools.partial(gather_kernel, axis), name, pltpu.VMEM(tuple(shape...]
    all_to_all x1, waiting for transfers between devices: 8.25 us -> 5.82 us  [shards(): lax.all_to_all(rows, ('y', 'x'), split_axis=0, concat_axis=0, tiled=True)]
    pallas_call x1, Pallas kernels: 6.68 us -> 4.57 us  [gate_up(): call(gate_up_kernel, 'gate_up', pltpu.VMEM((NZ, EROWS + 16, 512), BF), [S...]
  transfers between devices with their start and end apart: 36 -> 36, of which waited for: 11 -> 12; matrix products, arithmetic and copies ran while one was open for 7% -> 7% of each run, Pallas kernels for 17% -> 19%
where the time goes in v4:
time: 209 us; the launch traced here: 205 us
  starting transfers between devices  51.6 us (25%)
  waiting for transfers between devices  48.6 us (23%)
  Pallas kernels  40.1 us (19%)
  blocking collectives  35.2 us (17%)
  local copies, waits for them, and re-layouts  21.7 us (10%)
  other arithmetic  6.38 us (3%)
    ppermute x33, starting transfers between devices, shift(): return lax.ppermute(a, axis, [(i, (i + d) % n) for i in range(n)])  34.2 us
    all_to_all x1, blocking collectives, shards(): lax.all_to_all(result.reshape(EXPERTS, SLOTS, CHUNK), ('y', 'x'), split_a...  24.6 us
    all_to_all x1, waiting for transfers between devices, shards(): part = lax.all_to_all(part, 'z', split_axis=0, concat_axis=0, tiled=True)  19.1 us
    pallas_call x1, Pallas kernels, attention(): call(attention_kernel, 'attention', (jax.ShapeDtypeStruct((64, GRP * VDIM...  16.5 us
    ppermute x33, waiting for transfers between devices, shift(): return lax.ppermute(a, axis, [(i, (i + d) % n) for i in range(n)])  14.7 us
    unnamed x34, local copies, waits for them, and re-layouts  12.9 us
    all_to_all x1, blocking collectives, shards(): done = lax.all_to_all(done, 'z', split_axis=0, concat_axis=0, tiled=True)  10.6 us
    all_to_all x1, waiting for transfers between devices, shards(): lax.all_to_all(q, ('y', 'core', 'z'), split_axis=0, concat_axis=0, tiled=...  8.92 us
  transfers between devices with their start and end apart: 36, of which 12 were waited for; matrix products, arithmetic and copies ran while one was open for 7% of the time, Pallas kernels for 19%

profile of v4, /device:TPU:40, one launch (start us, length us, event | category | flops | bytes accessed | tf_op | source)
XLA Modules:
  0.0 204.7 jit_solution(1609445042586842780)
XLA Ops:
  0.0 1.4 copy.34.c0
  2.3 1.5 collective-permute-start
  3.8 2.7 %collective-permute-start.1 = (bf16[256,576]{1,0:T(8,128)(2,1)}, bf16[256,576]{1,0:T(8,128)(2,1)}, u32[]{:S(2)}, u32[]{:S(2)}) collective-permute-start(bf16[256,576]{1,0:T(8,128)(2,1)} %constant_dynamic-slice_fusion.2), channel_id=1, source_target_pairs={{0,16},{8,24},{16,0},{24,8},{1,17},{9,25},{17,1},{25,9},{2,18},{10... | collective-permute-start | bytes 884744 | tf_op jit(solution)/shard_map/cache_gather/ppermute | solution.py:40
  6.5 1.4 collective-permute-start.2
  8.3 3.3 %dynamic-slice_bitcast_fusion.4 = (bf16[1792,128]{1,0:T(8,128)(2,1)}, bf16[1792,128]{1,0:T(8,128)(2,1)}, bf16[1792,128]{1,0:T(8,128)(2,1)S(1)}, bf16[1792,128]{1...) fusion(bf16[4,1792,128]{2,1,0:T(8,128)(2,1)} %bitcast.69, ...), kind=kLoop, calls=%fused_computation.12 | loop fusion | bytes 7340048 | tf_op jit(solution)/shard_map/weights/jit(dynamic_index_in_dim)/squeeze | solution.py:472
  11.6 1.0 pad_maximum_fusion
  13.1 1.1 pad_maximum_fusion.1
  14.2 1.0 broadcast_in_dim.30
  15.2 8.2 %all-to-all-start = ((bf16[32,8,1664]{2,1,0:T(8,128)(2,1)}), bf16[32,8,1664]{2,1,0:T(8,128)(2,1)S(1)}, u32[]{:S(2)}, u32[]{:S(2)}) async-start(bf16[32,8,1664]{2,1,0:T(8,128)(2,1)} %bitcast.68), calls=%async_computation | async-start | bytes 1703936 | tf_op jit(solution)/shard_map/query_exchange/all_to_all | solution.py:461
  23.6 2.2 %pad_maximum_fusion.2 = bf16[1792,256]{1,0:T(8,128)(2,1)} fusion(bf16[1792,128]{1,0:T(8,128)(2,1)} %get-tuple-element.102, bf16[1792,128]{1,0:T(8,128)(2,1)} %get-tuple-element.112), kind=kLoop, calls=%fused_computation.6 | loop fusion | flops 1835008 | bytes 1835008 | tf_op jit(solution)/shard_map/weights/concatenate | solution.py:473
  26.9 8.9 %all-to-all-done = bf16[32,8,1664]{2,1,0:T(8,128)(2,1)S(1)} async-done(((bf16[32,8,1664]{2,1,0:T(8,128)(2,1)}), bf16[32,8,1664]{2,1,0:T(8,128)(2,1)S(1)}, u32[]{:S(2)}, u32[]{:S(2)}) %all-to-all-start) | async-done | bytes 852000 | tf_op jit(solution)/shard_map/query_exchange/all_to_all | solution.py:461
  35.8 1.5 collective-permute-start.9
  37.3 2.3 %collective-permute-start.10 = (bf16[1792,256]{1,0:T(8,128)(2,1)}, bf16[1792,256]{1,0:T(8,128)(2,1)}, u32[]{:S(2)}, u32[]{:S(2)}) collective-permute-start(bf16[1792,256]{1,0:T(8,128)(2,1)} %pad_maximum_fusion.1), channel_id=1, source_target_pairs={{0,4},{2,6},{4,0},{6,2},{1,5},{3,7},{5,1},{7,3},{8,12},{10,14},{12... | collective-permute-start | bytes 2752520 | tf_op jit(solution)/shard_map/attention/ppermute | solution.py:40
  41.7 1.2 copy-done.4
  43.0 1.0 copy-done.9
  43.9 16.5 %attention.1 = (bf16[64,1152]{1,0:T(8,128)(2,1)S(1)}, bf16[64,1152]{1,0:T(8,128)(2,1)S(1)}, bf16[64,1152]{1,0:T(8,128)(2,1)S(1)}, bf16[64,1152]{1,0:T(8,128)(2,1)S(1)}) custom-call(s32[8]{0:T(128)S(1)} %stack.57.pos_ref, bf16[4,64,1664]{2,1,0:T(8,128)(2,1)S(1)} %bitcast.62, s32[256,1]{1,0:T(8,128)S(1)} %copy.36.first_ref, s32[256,1]{1,0:T(8,128)S(1)} %select_n.190.last_ref, ...), custom_call_target="tpu_custom_call" | custom-call | bytes 1 | tf_op jit(solution)/shard_map/attention/attention/pallas_call | solution.py:146
  61.8 2.7 %collective-permute-start.7 = (bf16[64,1152]{1,0:T(8,128)(2,1)S(1)}, bf16[64,1152]{1,0:T(8,128)(2,1)S(1)}, u32[]{:S(2)}, u32[]{:S(2)}) collective-permute-start(bf16[64,1152]{1,0:T(8,128)(2,1)S(1)} %get-tuple-element.51), channel_id=1, source_target_pairs={{0,64},{32,96},{64,0},{96,32},{1,65},{33,97},{65,1},{97,33},{2,66}... | collective-permute-start | bytes 442376 | tf_op jit(solution)/shard_map/combine/ppermute | solution.py:40
  64.5 3.0 %collective-permute-done.6.o1 = bf16[64,1152]{1,0:T(8,128)(2,1)S(1)} collective-permute-done((bf16[64,1152]{1,0:T(8,128)(2,1)S(1)}, bf16[64,1152]{1,0:T(8,128)(2,1)S(1)}, u32[]{:S(2)}, u32[]{:S(2)}) %collective-permute-start.6) | collective-permute-done | bytes 147488 | tf_op jit(solution)/shard_map/combine/ppermute | solution.py:40
  67.5 4.1 %collective-permute-start.8 = (bf16[64,1152]{1,0:T(8,128)(2,1)S(1)}, bf16[64,1152]{1,0:T(8,128)(2,1)S(1)}, u32[]{:S(2)}, u32[]{:S(2)}) collective-permute-start(bf16[64,1152]{1,0:T(8,128)(2,1)S(1)} %get-tuple-element.52), channel_id=1, source_target_pairs={{0,96},{32,0},{64,32},{96,64},{1,97},{33,1},{65,33},{97,65},{2,98}... | collective-permute-start | bytes 442376 | tf_op jit(solution)/shard_map/combine/ppermute | solution.py:40
  71.6 5.3 %stage.1.w_ref = bf16[1024,7168]{1,0:T(8,128)(2,1)S(1)} custom-call(bf16[64,1152]{1,0:T(8,128)(2,1)} %copy-done.5, bf16[1024,7168]{1,0:T(8,128)(2,1)} %w_ref.1), custom_call_target="tpu_custom_call" | custom-call | bytes 1 | tf_op jit(solution)/shard_map/combine/stage/pallas_call | solution.py:252
  77.6 2.0 project.2
  79.9 2.0 project.3
  83.8 1.4 broadcast_divide_fusion
  85.8 1.3 collective-permute-start.15
  87.1 2.1 %collective-permute-start.16 = (bf16[32,1792]{1,0:T(8,128)(2,1)S(1)}, bf16[32,1792]{1,0:T(8,128)(2,1)S(1)}, u32[]{:S(2)}, u32[]{:S(2)}) collective-permute-start(bf16[32,1792]{1,0:T(8,128)(2,1)S(1)} %get-tuple-element.65), channel_id=1, source_target_pairs={{0,4},{2,6},{4,0},{6,2},{1,5},{3,7},{5,1},{7,3},{8,12},{10,14},{12... | collective-permute-start | bytes 344072 | tf_op jit(solution)/shard_map/out_projection/ppermute | solution.py:40
  90.4 1.6 collective-permute-done.15.p1
  92.0 2.7 %collective-permute-done.16.p2 = bf16[32,1792]{1,0:T(8,128)(2,1)S(1)} collective-permute-done((bf16[32,1792]{1,0:T(8,128)(2,1)S(1)}, bf16[32,1792]{1,0:T(8,128)(2,1)S(1)}, u32[]{:S(2)}, u32[]{:S(2)}) %collective-permute-start.16) | collective-permute-done | bytes 114720 | tf_op jit(solution)/shard_map/out_projection/ppermute | solution.py:40
  94.7 1.3 collective-permute-done.18.p3
  96.7 1.2 copy-done.2
  97.8 4.7 %all-to-all-start.1 = ((bf16[16,24,1792]{2,1,0:T(8,128)(2,1)}), bf16[16,24,1792]{2,1,0:T(8,128)(2,1)S(1)}, u32[]{:S(2)}, u32[]{:S(2)}) async-start(bf16[16,24,1792]{2,1,0:T(8,128)(2,1)} %bitcast.66), calls=%async_computation.1 | async-start | bytes 2752512 | tf_op jit(solution)/shard_map/dispatch/all_to_all | solution.py:526
  103.0 2.5 %dynamic-slice_bitcast_fusion = (bf16[128,1792]{1,0:T(8,128)(2,1)S(1)}, bf16[128,1792]{1,0:T(8,128)(2,1)}, bf16[128,1792]{1,0:T(8,128)(2,1)}, bf16[128,1792]{1,0:T(8,128)(2,1)}) fusion(bf16[1,128,7168]{2,1,0:T(8,128)(2,1)} %param.25, s32[]{:T(128)S(6)} %select_n.189, s32[]{:T(128)S(6)} %select_n.187, s32[]{:T(128)S(6)} %select_n.186, s32[]{:T(128)S(6)} %select_n.188), kind=kLoop, calls=%fused_computation.8 | loop fusion | bytes 3670032 | tf_op jit(solution)/shard_map/weights/dynamic_slice | solution.py:474
  106.1 2.0 collective-permute-start.24
  108.1 2.1 %collective-permute-start.25 = (bf16[128,1792]{1,0:T(8,128)(2,1)}, bf16[128,1792]{1,0:T(8,128)(2,1)}, u32[]{:S(2)}, u32[]{:S(2)}) collective-permute-start(bf16[128,1792]{1,0:T(8,128)(2,1)} %get-tuple-element.82), channel_id=1, source_target_pairs={{0,6},{2,0},{4,2},{6,4},{1,7},{3,1},{5,3},{7,5},{8,14},{10,8},{12,... | collective-permute-start | bytes 1376264 | tf_op jit(solution)/shard_map/dispatch/ppermute | solution.py:40
  110.2 3.0 %gate_up_weights.1.w = bf16[1792,2048]{1,0:T(8,128)(2,1)S(1)} custom-call(bf16[1792,256]{1,0:T(8,128)(2,1)S(1)} %pad_maximum_fusion.3.refs_0_, bf16[1792,256]{1,0:T(8,128)(2,1)} %collective-permute-done.19.refs_1_, bf16[1792,256]{1,0:T(8,128)(2,1)} %collective-permute-done.9.refs_2_, bf16[1792,256]{1,0:T(8,128)(2,1)} %collective-permute-done.20.refs_3_, ...), custom_call_target="tpu_custom_call" | custom-call | bytes 1 | tf_op jit(solution)/shard_map/experts/gate_up_weights/pallas_call | solution.py:341
  113.3 2.9 %copy-done = bf16[1792,2048]{1,0:T(8,128)(2,1)} copy-done((bf16[1792,2048]{1,0:T(8,128)(2,1)}, bf16[1792,2048]{1,0:T(8,128)(2,1)S(1)}, u32[]{:S(2)}) %copy-start) | copy-done | bytes 7340056
  116.2 5.8 %all-to-all-done.1 = bf16[16,24,1792]{2,1,0:T(8,128)(2,1)S(1)} async-done(((bf16[16,24,1792]{2,1,0:T(8,128)(2,1)}), bf16[16,24,1792]{2,1,0:T(8,128)(2,1)S(1)}, u32[]{:S(2)}, u32[]{:S(2)}) %all-to-all-start.1) | async-done | bytes 1376288 | tf_op jit(solution)/shard_map/dispatch/all_to_all | solution.py:526
  122.0 3.1 %copy-done.1 = bf16[1792,2048]{1,0:T(8,128)(2,1)S(1)} copy-done((bf16[1792,2048]{1,0:T(8,128)(2,1)S(1)}, bf16[1792,2048]{1,0:T(8,128)(2,1)}, u32[]{:S(2)}) %copy-start.1) | copy-done | bytes 7340056
  125.1 4.6 %gate_up.1 = bf16[4,400,512]{2,1,0:T(8,128)(2,1)} custom-call(s32[1]{0:T(128)} %bitcast.1.z_ref, bf16[384,1792]{1,0:T(8,128)(2,1)S(1)} %bitcast.65, f32[1,1792]{1,0:T(1,128)S(1)} %div.36.gain_ref, bf16[1792,2048]{1,0:T(8,128)(2,1)S(1)} %copy-done.1), custom_call_target="tpu_custom_call" | custom-call | bytes 1 | tf_op jit(solution)/shard_map/experts/gate_up/pallas_call | solution.py:372
  130.0 4.4 %all-to-all-start.2 = ((bf16[4,400,512]{2,1,0:T(8,128)(2,1)}), bf16[4,400,512]{2,1,0:T(8,128)(2,1)S(1)}, u32[]{:S(2)}, u32[]{:S(2)}) async-start(bf16[4,400,512]{2,1,0:T(8,128)(2,1)} %gate_up.1), calls=%async_computation.2 | async-start | bytes 3276800 | tf_op jit(solution)/shard_map/experts/all_to_all | solution.py:535
  135.4 19.1 %all-to-all-done.2.part_ref = bf16[4,400,512]{2,1,0:T(8,128)(2,1)S(1)} async-done(((bf16[4,400,512]{2,1,0:T(8,128)(2,1)}), bf16[4,400,512]{2,1,0:T(8,128)(2,1)S(1)}, u32[]{:S(2)}, u32[]{:S(2)}) %all-to-all-start.2) | async-done | bytes 1638432 | tf_op jit(solution)/shard_map/experts/all_to_all | solution.py:535
  155.1 3.5 %collective-permute-start.27 = (bf16[384,256]{1,0:T(8,128)(2,1)S(1)}, bf16[384,256]{1,0:T(8,128)(2,1)S(1)}, u32[]{:S(2)}, u32[]{:S(2)}) collective-permute-start(bf16[384,256]{1,0:T(8,128)(2,1)S(1)} %inner_act.1.i0), channel_id=1, source_target_pairs={{0,4},{2,6},{4,0},{6,2},{1,5},{3,7},{5,1},{7,3},{8,12},{10,14},{12... | collective-permute-start | bytes 589832 | tf_op jit(solution)/shard_map/experts/ppermute | solution.py:40
  159.2 2.5 %down_weights.1.w = bf16[1024,1792]{1,0:T(8,128)(2,1)S(1)} custom-call(bf16[128,1792]{1,0:T(8,128)(2,1)S(1)} %get-tuple-element.87.refs_0_, bf16[128,1792]{1,0:T(8,128)(2,1)S(1)} %collective-permute-done.29.refs_1_, bf16[128,1792]{1,0:T(8,128)(2,1)S(1)} %collective-permute-done.23.refs_2_, bf16[128,1792]{1,0:T(8,128)(2,1)} %collective-permute-done.30.refs_3_, ...), custom_call_target="tpu_custom_call" | custom-call | bytes 1 | tf_op jit(solution)/shard_map/experts/down_weights/pallas_call | solution.py:341
  161.7 1.2 collective-permute-done.26.i1
  162.9 1.6 collective-permute-done.27.i2
  164.5 2.1 %collective-permute-done.28.i3 = bf16[384,256]{1,0:T(8,128)(2,1)S(1)} collective-permute-done((bf16[384,256]{1,0:T(8,128)(2,1)S(1)}, bf16[384,256]{1,0:T(8,128)(2,1)S(1)}, u32[]{:S(2)}, u32[]{:S(2)}) %collective-permute-start.28) | collective-permute-done | bytes 196640 | tf_op jit(solution)/shard_map/experts/ppermute | solution.py:40
  166.6 1.6 down.1
  168.2 24.6 %all_to_all.25 = bf16[16,24,1792]{2,1,0:T(8,128)(2,1)S(1)} all-to-all(bf16[16,24,1792]{2,1,0:T(8,128)(2,1)S(1)} %bitcast.64), channel_id=1, replica_groups=mesh['y'=4,'x'=4,'z'=4,'core'=2] {'y','x'}, dimensions={0} | all-to-all | bytes 2752512 | tf_op jit(solution)/shard_map/return/all_to_all | solution.py:542
  193.5 10.6 %all_to_all.26 = bf16[4,8,1792]{2,1,0:T(8,128)(2,1)S(1)} all-to-all(bf16[4,8,1792]{2,1,0:T(8,128)(2,1)S(1)} %fusion.1), channel_id=1, replica_groups=mesh['y'=4,'x'=4,'z'=4,'core'=2] {'z'}, dimensions={0} | all-to-all | bytes 229376 | tf_op jit(solution)/shard_map/return/all_to_all | solution.py:547
  (122 shorter events, 16.4 us)
Async XLA Ops:
  0.0 8.0 %slice-start = ((bf16[8,64,192]{2,1,0:T(8,128)(2,1)}), bf16[8,64,64]{2,1,0:T(8,128)(2,1)S(1)}, s32[]{:S(2)}) async-start(bf16[8,64,192]{2,1,0:T(8,128)(2,1)} %param.13), calls=%async_computation.5 | async-start | bytes 262144 | tf_op jit(solution)/shard_map/query_exchange/slice | solution.py:456
  0.0 8.1 %slice-start.1 = ((bf16[8,64,192]{2,1,0:T(8,128)(2,1)}), bf16[8,64,128]{2,1,0:T(8,128)(2,1)S(1)}, s32[]{:S(2)}) async-start(bf16[8,64,192]{2,1,0:T(8,128)(2,1)} %param.13), calls=%async_computation.6 | async-start | bytes 262144 | tf_op jit(solution)/shard_map/query_exchange/slice | solution.py:455
  0.0 7.9 %copy-start.14 = (s32[8,8]{1,0:T(8,128)S(1)}, s32[8,8]{1,0:T(8,128)}, u32[]{:S(2)}) copy-start(s32[8,8]{1,0:T(8,128)} %param.20) | copy-start | bytes 772
  0.0 7.9 %copy-start.15 = (f32[8,8]{1,0:T(8,128)S(1)}, f32[8,8]{1,0:T(8,128)}, u32[]{:S(2)}) copy-start(f32[8,8]{1,0:T(8,128)} %param.21) | copy-start | bytes 772
  0.0 8.1 %copy-start.13 = (s32[1024]{0:T(1024)S(1)}, s32[1024]{0:T(1024)}, u32[]{:S(2)}) copy-start(s32[1024]{0:T(1024)} %param.22) | copy-start | bytes 12292
  2.3 11.9 %collective-permute-start = (bf16[256,576]{1,0:T(8,128)(2,1)}, bf16[256,576]{1,0:T(8,128)(2,1)S(1)}, u32[]{:S(2)}, u32[]{:S(2)}) collective-permute-start(bf16[256,576]{1,0:T(8,128)(2,1)} %constant_dynamic-slice_fusion.2), channel_id=1, source_target_pairs={{0,8},{8,16},{16,24},{24,0},{1,9},{9,17},{17,25},{25,1},{2,10},{10... | collective-permute-start | bytes 884744 | tf_op jit(solution)/shard_map/cache_gather/ppermute | solution.py:40
  3.8 22.5 %collective-permute-start.1 = (bf16[256,576]{1,0:T(8,128)(2,1)}, bf16[256,576]{1,0:T(8,128)(2,1)}, u32[]{:S(2)}, u32[]{:S(2)}) collective-permute-start(bf16[256,576]{1,0:T(8,128)(2,1)} %constant_dynamic-slice_fusion.2), channel_id=1, source_target_pairs={{0,16},{8,24},{16,0},{24,8},{1,17},{9,25},{17,1},{25,9},{2,18},{10... | collective-permute-start | bytes 884744 | tf_op jit(solution)/shard_map/cache_gather/ppermute | solution.py:40
  6.5 20.1 %collective-permute-start.2 = (bf16[256,576]{1,0:T(8,128)(2,1)}, bf16[256,576]{1,0:T(8,128)(2,1)}, u32[]{:S(2)}, u32[]{:S(2)}) collective-permute-start(bf16[256,576]{1,0:T(8,128)(2,1)} %constant_dynamic-slice_fusion.2), channel_id=1, source_target_pairs={{0,24},{8,0},{16,8},{24,16},{1,25},{9,1},{17,9},{25,17},{2,26},{10... | collective-permute-start | bytes 884744 | tf_op jit(solution)/shard_map/cache_gather/ppermute | solution.py:40
  15.2 26.5 %copy-start.3 = (bf16[8,128,512]{2,1,0:T(8,128)(2,1)S(1)}, bf16[8,128,512]{2,1,0:T(8,128)(2,1)}, u32[]{:S(2)}) copy-start(bf16[8,128,512]{2,1,0:T(8,128)(2,1)} %ak_ref.1) | copy-start | bytes 3145732
  15.2 20.6 %all-to-all-start = ((bf16[32,8,1664]{2,1,0:T(8,128)(2,1)}), bf16[32,8,1664]{2,1,0:T(8,128)(2,1)S(1)}, u32[]{:S(2)}, u32[]{:S(2)}) async-start(bf16[32,8,1664]{2,1,0:T(8,128)(2,1)} %bitcast.68), calls=%async_computation | async-start | bytes 1703936 | tf_op jit(solution)/shard_map/query_exchange/all_to_all | solution.py:461
  26.0 13.6 %collective-permute-start.3 = (bf16[256,576]{1,0:T(8,128)(2,1)S(1)}, bf16[256,576]{1,0:T(8,128)(2,1)S(1)}, u32[]{:S(2)}, u32[]{:S(2)}) collective-permute-start(bf16[256,576]{1,0:T(8,128)(2,1)S(1)} %collective-permute-done.c1), channel_id=1, source_target_pairs={{0,1},{1,0},{2,3},{3,2},{4,5},{5,4},{6,7},{7,6},{8,9},{9,8},{10,11... | collective-permute-start | bytes 884744 | tf_op jit(solution)/shard_map/cache_share/ppermute | solution.py:40
  26.3 15.4 %collective-permute-start.4 = (bf16[256,576]{1,0:T(8,128)(2,1)}, bf16[256,576]{1,0:T(8,128)(2,1)}, u32[]{:S(2)}, u32[]{:S(2)}) collective-permute-start(bf16[256,576]{1,0:T(8,128)(2,1)} %collective-permute-done.1.c2), channel_id=1, source_target_pairs={{0,1},{1,0},{2,3},{3,2},{4,5},{5,4},{6,7},{7,6},{8,9},{9,8},{10,11... | collective-permute-start | bytes 884744 | tf_op jit(solution)/shard_map/cache_share/ppermute | solution.py:40
  26.6 15.1 %collective-permute-start.5 = (bf16[256,576]{1,0:T(8,128)(2,1)}, bf16[256,576]{1,0:T(8,128)(2,1)}, u32[]{:S(2)}, u32[]{:S(2)}) collective-permute-start(bf16[256,576]{1,0:T(8,128)(2,1)} %collective-permute-done.2.c3), channel_id=1, source_target_pairs={{0,1},{1,0},{2,3},{3,2},{4,5},{5,4},{6,7},{7,6},{8,9},{9,8},{10,11... | collective-permute-start | bytes 884744 | tf_op jit(solution)/shard_map/cache_share/ppermute | solution.py:40
  35.8 51.3 %collective-permute-start.9 = (bf16[1792,256]{1,0:T(8,128)(2,1)}, bf16[1792,256]{1,0:T(8,128)(2,1)}, u32[]{:S(2)}, u32[]{:S(2)}) collective-permute-start(bf16[1792,256]{1,0:T(8,128)(2,1)} %pad_maximum_fusion), channel_id=1, source_target_pairs={{0,2},{2,4},{4,6},{6,0},{1,3},{3,5},{5,7},{7,1},{8,10},{10,12},{12... | collective-permute-start | bytes 2752520 | tf_op jit(solution)/shard_map/attention/ppermute | solution.py:40
  37.3 51.9 %collective-permute-start.10 = (bf16[1792,256]{1,0:T(8,128)(2,1)}, bf16[1792,256]{1,0:T(8,128)(2,1)}, u32[]{:S(2)}, u32[]{:S(2)}) collective-permute-start(bf16[1792,256]{1,0:T(8,128)(2,1)} %pad_maximum_fusion.1), channel_id=1, source_target_pairs={{0,4},{2,6},{4,0},{6,2},{1,5},{3,7},{5,1},{7,3},{8,12},{10,14},{12... | collective-permute-start | bytes 2752520 | tf_op jit(solution)/shard_map/attention/ppermute | solution.py:40
  40.4 49.0 %collective-permute-start.11 = (bf16[1792,256]{1,0:T(8,128)(2,1)}, bf16[1792,256]{1,0:T(8,128)(2,1)}, u32[]{:S(2)}, u32[]{:S(2)}) collective-permute-start(bf16[1792,256]{1,0:T(8,128)(2,1)} %pad_maximum_fusion.2), channel_id=1, source_target_pairs={{0,6},{2,0},{4,2},{6,4},{1,7},{3,1},{5,3},{7,5},{8,14},{10,8},{12,... | collective-permute-start | bytes 2752520 | tf_op jit(solution)/shard_map/attention/ppermute | solution.py:40
  61.1 6.4 %collective-permute-start.6 = (bf16[64,1152]{1,0:T(8,128)(2,1)S(1)}, bf16[64,1152]{1,0:T(8,128)(2,1)S(1)}, u32[]{:S(2)}, u32[]{:S(2)}) collective-permute-start(bf16[64,1152]{1,0:T(8,128)(2,1)S(1)} %get-tuple-element.50), channel_id=1, source_target_pairs={{0,32},{32,64},{64,96},{96,0},{1,33},{33,65},{65,97},{97,1},{2,34}... | collective-permute-start | bytes 442376 | tf_op jit(solution)/shard_map/combine/ppermute | solution.py:40
  61.8 15.2 %collective-permute-start.7 = (bf16[64,1152]{1,0:T(8,128)(2,1)S(1)}, bf16[64,1152]{1,0:T(8,128)(2,1)S(1)}, u32[]{:S(2)}, u32[]{:S(2)}) collective-permute-start(bf16[64,1152]{1,0:T(8,128)(2,1)S(1)} %get-tuple-element.51), channel_id=1, source_target_pairs={{0,64},{32,96},{64,0},{96,32},{1,65},{33,97},{65,1},{97,33},{2,66}... | collective-permute-start | bytes 442376 | tf_op jit(solution)/shard_map/combine/ppermute | solution.py:40
  67.5 9.5 %collective-permute-start.8 = (bf16[64,1152]{1,0:T(8,128)(2,1)S(1)}, bf16[64,1152]{1,0:T(8,128)(2,1)S(1)}, u32[]{:S(2)}, u32[]{:S(2)}) collective-permute-start(bf16[64,1152]{1,0:T(8,128)(2,1)S(1)} %get-tuple-element.52), channel_id=1, source_target_pairs={{0,96},{32,0},{64,32},{96,64},{1,97},{33,1},{65,33},{97,65},{2,98}... | collective-permute-start | bytes 442376 | tf_op jit(solution)/shard_map/combine/ppermute | solution.py:40
  71.6 5.4 %copy-start.6 = (bf16[64,1152]{1,0:T(8,128)(2,1)S(1)}, bf16[64,1152]{1,0:T(8,128)(2,1)}, u32[]{:S(2)}) copy-start(bf16[64,1152]{1,0:T(8,128)(2,1)} %copy-done.5) | copy-start | bytes 442372
  71.6 6.0 %copy-start.7 = (bf16[8,7168]{1,0:T(8,128)(2,1)S(1)}, bf16[8,7168]{1,0:T(8,128)(2,1)}, u32[]{:S(2)}) copy-start(bf16[8,7168]{1,0:T(8,128)(2,1)} %res_ref.3) | copy-start | bytes 344068
  79.6 3.0 %copy-start.10 = (bf16[1792,128]{1,0:T(8,128)(2,1)S(1)}, bf16[1792,128]{1,0:T(8,128)(2,1)}, u32[]{:S(2)}) copy-start(bf16[1792,128]{1,0:T(8,128)(2,1)} %get-tuple-element.101) | copy-start | bytes 1376260
  79.6 3.0 %copy-start.11 = (bf16[1792,128]{1,0:T(8,128)(2,1)S(1)}, bf16[1792,128]{1,0:T(8,128)(2,1)}, u32[]{:S(2)}) copy-start(bf16[1792,128]{1,0:T(8,128)(2,1)} %get-tuple-element.113) | copy-start | bytes 1376260
  79.6 2.8 %collective-permute-start.13 = (bf16[32,1792]{1,0:T(8,128)(2,1)S(1)}, bf16[32,1792]{1,0:T(8,128)(2,1)S(1)}, u32[]{:S(2)}, u32[]{:S(2)}) collective-permute-start(bf16[32,1792]{1,0:T(8,128)(2,1)S(1)} %get-tuple-element.53), channel_id=1, source_target_pairs={{0,1},{1,0},{2,3},{3,2},{4,5},{5,4},{6,7},{7,6},{8,9},{9,8},{10,11... | collective-permute-start | bytes 344072 | tf_op jit(solution)/shard_map/out_projection/ppermute | solution.py:40
  81.9 1.5 collective-permute-start.14
  82.4 3.4 %collective-permute-start.17 = (bf16[32,1792]{1,0:T(8,128)(2,1)S(1)}, bf16[32,1792]{1,0:T(8,128)(2,1)S(1)}, u32[]{:S(2)}, u32[]{:S(2)}) collective-permute-start(bf16[32,1792]{1,0:T(8,128)(2,1)S(1)} %get-tuple-element.67), channel_id=1, source_target_pairs={{0,1},{1,0},{2,3},{3,2},{4,5},{5,4},{6,7},{7,6},{8,9},{9,8},{10,11... | collective-permute-start | bytes 344072 | tf_op jit(solution)/shard_map/out_projection/ppermute | solution.py:40
  83.4 6.0 %collective-permute-start.12 = (bf16[32,1792]{1,0:T(8,128)(2,1)S(1)}, bf16[32,1792]{1,0:T(8,128)(2,1)S(1)}, u32[]{:S(2)}, u32[]{:S(2)}) collective-permute-start(bf16[32,1792]{1,0:T(8,128)(2,1)S(1)} %get-tuple-element.60), channel_id=1, source_target_pairs={{0,1},{1,0},{2,3},{3,2},{4,5},{5,4},{6,7},{7,6},{8,9},{9,8},{10,11... | collective-permute-start | bytes 344072 | tf_op jit(solution)/shard_map/out_projection/ppermute | solution.py:40
  85.8 6.2 %collective-permute-start.15 = (bf16[32,1792]{1,0:T(8,128)(2,1)}, bf16[32,1792]{1,0:T(8,128)(2,1)S(1)}, u32[]{:S(2)}, u32[]{:S(2)}) collective-permute-start(bf16[32,1792]{1,0:T(8,128)(2,1)} %get-tuple-element.64), channel_id=1, source_target_pairs={{0,2},{2,4},{4,6},{6,0},{1,3},{3,5},{5,7},{7,1},{8,10},{10,12},{12... | collective-permute-start | bytes 344072 | tf_op jit(solution)/shard_map/out_projection/ppermute | solution.py:40
  87.1 7.6 %collective-permute-start.16 = (bf16[32,1792]{1,0:T(8,128)(2,1)S(1)}, bf16[32,1792]{1,0:T(8,128)(2,1)S(1)}, u32[]{:S(2)}, u32[]{:S(2)}) collective-permute-start(bf16[32,1792]{1,0:T(8,128)(2,1)S(1)} %get-tuple-element.65), channel_id=1, source_target_pairs={{0,4},{2,6},{4,0},{6,2},{1,5},{3,7},{5,1},{7,3},{8,12},{10,14},{12... | collective-permute-start | bytes 344072 | tf_op jit(solution)/shard_map/out_projection/ppermute | solution.py:40
  89.2 6.9 %collective-permute-start.18 = (bf16[32,1792]{1,0:T(8,128)(2,1)S(1)}, bf16[32,1792]{1,0:T(8,128)(2,1)S(1)}, u32[]{:S(2)}, u32[]{:S(2)}) collective-permute-start(bf16[32,1792]{1,0:T(8,128)(2,1)S(1)} %fold.3), channel_id=1, source_target_pairs={{0,6},{2,0},{4,2},{6,4},{1,7},{3,1},{5,3},{7,5},{8,14},{10,8},{12,... | collective-permute-start | bytes 344072 | tf_op jit(solution)/shard_map/out_projection/ppermute | solution.py:40
  89.3 16.8 %collective-permute-start.19 = (bf16[1792,256]{1,0:T(8,128)(2,1)S(1)}, bf16[1792,256]{1,0:T(8,128)(2,1)}, u32[]{:S(2)}, u32[]{:S(2)}) collective-permute-start(bf16[1792,256]{1,0:T(8,128)(2,1)S(1)} %pad_maximum_fusion.3.refs_0_), channel_id=1, source_target_pairs={{0,1},{1,0},{2,3},{3,2},{4,5},{5,4},{6,7},{7,6},{8,9},{9,8},{10,11... | collective-permute-start | bytes 2752520 | tf_op jit(solution)/shard_map/dispatch/ppermute | solution.py:40
  89.5 18.7 %collective-permute-start.20 = (bf16[1792,256]{1,0:T(8,128)(2,1)}, bf16[1792,256]{1,0:T(8,128)(2,1)}, u32[]{:S(2)}, u32[]{:S(2)}) collective-permute-start(bf16[1792,256]{1,0:T(8,128)(2,1)} %collective-permute-done.9.refs_2_), channel_id=1, source_target_pairs={{0,1},{1,0},{2,3},{3,2},{4,5},{5,4},{6,7},{7,6},{8,9},{9,8},{10,11... | collective-permute-start | bytes 2752520 | tf_op jit(solution)/shard_map/dispatch/ppermute | solution.py:40
  97.8 24.2 %all-to-all-start.1 = ((bf16[16,24,1792]{2,1,0:T(8,128)(2,1)}), bf16[16,24,1792]{2,1,0:T(8,128)(2,1)S(1)}, u32[]{:S(2)}, u32[]{:S(2)}) async-start(bf16[16,24,1792]{2,1,0:T(8,128)(2,1)} %bitcast.66), calls=%async_computation.1 | async-start | bytes 2752512 | tf_op jit(solution)/shard_map/dispatch/all_to_all | solution.py:526
  102.5 7.7 %collective-permute-start.21 = (bf16[1792,256]{1,0:T(8,128)(2,1)}, bf16[1792,256]{1,0:T(8,128)(2,1)}, u32[]{:S(2)}, u32[]{:S(2)}) collective-permute-start(bf16[1792,256]{1,0:T(8,128)(2,1)} %collective-permute-done.10.refs_4_), channel_id=1, source_target_pairs={{0,1},{1,0},{2,3},{3,2},{4,5},{5,4},{6,7},{7,6},{8,9},{9,8},{10,11... | collective-permute-start | bytes 2752520 | tf_op jit(solution)/shard_map/dispatch/ppermute | solution.py:40
  102.5 7.7 %collective-permute-start.22 = (bf16[1792,256]{1,0:T(8,128)(2,1)}, bf16[1792,256]{1,0:T(8,128)(2,1)}, u32[]{:S(2)}, u32[]{:S(2)}) collective-permute-start(bf16[1792,256]{1,0:T(8,128)(2,1)} %collective-permute-done.11.refs_6_), channel_id=1, source_target_pairs={{0,1},{1,0},{2,3},{3,2},{4,5},{5,4},{6,7},{7,6},{8,9},{9,8},{10,11... | collective-permute-start | bytes 2752520 | tf_op jit(solution)/shard_map/dispatch/ppermute | solution.py:40
  103.0 7.2 %copy-start.12 = (f32[1792]{0:T(1024)S(1)}, f32[1792]{0:T(1024)}, u32[]{:S(2)}) copy-start(f32[1792]{0:T(1024)} %get-tuple-element.91) | copy-start | bytes 21508
  105.5 24.1 %collective-permute-start.23 = (bf16[128,1792]{1,0:T(8,128)(2,1)}, bf16[128,1792]{1,0:T(8,128)(2,1)S(1)}, u32[]{:S(2)}, u32[]{:S(2)}) collective-permute-start(bf16[128,1792]{1,0:T(8,128)(2,1)} %get-tuple-element.80), channel_id=1, source_target_pairs={{0,2},{2,4},{4,6},{6,0},{1,3},{3,5},{5,7},{7,1},{8,10},{10,12},{12... | collective-permute-start | bytes 1376264 | tf_op jit(solution)/shard_map/dispatch/ppermute | solution.py:40
  106.1 23.5 %collective-permute-start.24 = (bf16[128,1792]{1,0:T(8,128)(2,1)}, bf16[128,1792]{1,0:T(8,128)(2,1)}, u32[]{:S(2)}, u32[]{:S(2)}) collective-permute-start(bf16[128,1792]{1,0:T(8,128)(2,1)} %get-tuple-element.81), channel_id=1, source_target_pairs={{0,4},{2,6},{4,0},{6,2},{1,5},{3,7},{5,1},{7,3},{8,12},{10,14},{12... | collective-permute-start | bytes 1376264 | tf_op jit(solution)/shard_map/dispatch/ppermute | solution.py:40
  108.1 21.9 %collective-permute-start.25 = (bf16[128,1792]{1,0:T(8,128)(2,1)}, bf16[128,1792]{1,0:T(8,128)(2,1)}, u32[]{:S(2)}, u32[]{:S(2)}) collective-permute-start(bf16[128,1792]{1,0:T(8,128)(2,1)} %get-tuple-element.82), channel_id=1, source_target_pairs={{0,6},{2,0},{4,2},{6,4},{1,7},{3,1},{5,3},{7,5},{8,14},{10,8},{12,... | collective-permute-start | bytes 1376264 | tf_op jit(solution)/shard_map/dispatch/ppermute | solution.py:40
  122.0 3.1 %copy-start.1 = (bf16[1792,2048]{1,0:T(8,128)(2,1)S(1)}, bf16[1792,2048]{1,0:T(8,128)(2,1)}, u32[]{:S(2)}) copy-start(bf16[1792,2048]{1,0:T(8,128)(2,1)} %copy-done) | copy-start | bytes 22020100
  130.0 24.6 %all-to-all-start.2 = ((bf16[4,400,512]{2,1,0:T(8,128)(2,1)}), bf16[4,400,512]{2,1,0:T(8,128)(2,1)S(1)}, u32[]{:S(2)}, u32[]{:S(2)}) async-start(bf16[4,400,512]{2,1,0:T(8,128)(2,1)} %gate_up.1), calls=%async_computation.2 | async-start | bytes 3276800 | tf_op jit(solution)/shard_map/experts/all_to_all | solution.py:535
  134.4 20.7 %collective-permute-start.29 = (bf16[128,1792]{1,0:T(8,128)(2,1)S(1)}, bf16[128,1792]{1,0:T(8,128)(2,1)S(1)}, u32[]{:S(2)}, u32[]{:S(2)}) collective-permute-start(bf16[128,1792]{1,0:T(8,128)(2,1)S(1)} %get-tuple-element.87.refs_0_), channel_id=1, source_target_pairs={{0,1},{1,0},{2,3},{3,2},{4,5},{5,4},{6,7},{7,6},{8,9},{9,8},{10,11... | collective-permute-start | bytes 1376264 | tf_op jit(solution)/shard_map/experts/ppermute | solution.py:40
  134.4 24.2 %collective-permute-start.30 = (bf16[128,1792]{1,0:T(8,128)(2,1)S(1)}, bf16[128,1792]{1,0:T(8,128)(2,1)}, u32[]{:S(2)}, u32[]{:S(2)}) collective-permute-start(bf16[128,1792]{1,0:T(8,128)(2,1)S(1)} %collective-permute-done.23.refs_2_), channel_id=1, source_target_pairs={{0,1},{1,0},{2,3},{3,2},{4,5},{5,4},{6,7},{7,6},{8,9},{9,8},{10,11... | collective-permute-start | bytes 1376264 | tf_op jit(solution)/shard_map/experts/ppermute | solution.py:40
  134.9 24.3 %collective-permute-start.31 = (bf16[128,1792]{1,0:T(8,128)(2,1)}, bf16[128,1792]{1,0:T(8,128)(2,1)}, u32[]{:S(2)}, u32[]{:S(2)}) collective-permute-start(bf16[128,1792]{1,0:T(8,128)(2,1)} %collective-permute-done.24.refs_4_), channel_id=1, source_target_pairs={{0,1},{1,0},{2,3},{3,2},{4,5},{5,4},{6,7},{7,6},{8,9},{9,8},{10,11... | collective-permute-start | bytes 1376264 | tf_op jit(solution)/shard_map/experts/ppermute | solution.py:40
  134.9 24.3 %collective-permute-start.32 = (bf16[128,1792]{1,0:T(8,128)(2,1)}, bf16[128,1792]{1,0:T(8,128)(2,1)}, u32[]{:S(2)}, u32[]{:S(2)}) collective-permute-start(bf16[128,1792]{1,0:T(8,128)(2,1)} %collective-permute-done.25.refs_6_), channel_id=1, source_target_pairs={{0,1},{1,0},{2,3},{3,2},{4,5},{5,4},{6,7},{7,6},{8,9},{9,8},{10,11... | collective-permute-start | bytes 1376264 | tf_op jit(solution)/shard_map/experts/ppermute | solution.py:40
  155.0 7.8 %collective-permute-start.26 = (bf16[384,256]{1,0:T(8,128)(2,1)S(1)}, bf16[384,256]{1,0:T(8,128)(2,1)S(1)}, u32[]{:S(2)}, u32[]{:S(2)}) collective-permute-start(bf16[384,256]{1,0:T(8,128)(2,1)S(1)} %inner_act.1.i0), channel_id=1, source_target_pairs={{0,2},{2,4},{4,6},{6,0},{1,3},{3,5},{5,7},{7,1},{8,10},{10,12},{12... | collective-permute-start | bytes 589832 | tf_op jit(solution)/shard_map/experts/ppermute | solution.py:40
  155.1 9.4 %collective-permute-start.27 = (bf16[384,256]{1,0:T(8,128)(2,1)S(1)}, bf16[384,256]{1,0:T(8,128)(2,1)S(1)}, u32[]{:S(2)}, u32[]{:S(2)}) collective-permute-start(bf16[384,256]{1,0:T(8,128)(2,1)S(1)} %inner_act.1.i0), channel_id=1, source_target_pairs={{0,4},{2,6},{4,0},{6,2},{1,5},{3,7},{5,1},{7,3},{8,12},{10,14},{12... | collective-permute-start | bytes 589832 | tf_op jit(solution)/shard_map/experts/ppermute | solution.py:40
  158.6 7.9 %collective-permute-start.28 = (bf16[384,256]{1,0:T(8,128)(2,1)S(1)}, bf16[384,256]{1,0:T(8,128)(2,1)S(1)}, u32[]{:S(2)}, u32[]{:S(2)}) collective-permute-start(bf16[384,256]{1,0:T(8,128)(2,1)S(1)} %inner_act.1.i0), channel_id=1, source_target_pairs={{0,6},{2,0},{4,2},{6,4},{1,7},{3,1},{5,3},{7,5},{8,14},{10,8},{12,... | collective-permute-start | bytes 589832 | tf_op jit(solution)/shard_map/experts/ppermute | solution.py:40
  (6 other events, 7.7 us)

commit v5 on v3

--- a/solution.py
+++ b/solution.py
@@ -322,6 +322,28 @@
     )(*parts, gain, pick)
 
 
+def gather_kernel(*refs):
+    pieces, (held_ref, sem) = refs[:8], refs[8:]
+    n = pieces[0].shape[0]
+    copies = [pltpu.make_async_copy(p, held_ref.at[pl.ds(i * n, n)], sem.at[i]) for i, p in enumerate(pieces)]
+    for c in copies:
+        c.start()
+    for c in copies:
+        c.wait()
+
+
+def gather(pieces):
+    return call(
+        gather_kernel,
+        "down_weights",
+        pltpu.VMEM((1024, CHUNK), BF),
+        [AT] * 8,
+        [pltpu.SemaphoreType.DMA((8,))],
+        mib=16,
+        out_specs=VM,
+    )(*pieces)
+
+
 def gate_up_kernel(z_ref, x_ref, gain_ref, *refs):
     pieces, (o_ref, w, sem) = refs[:8], refs[8:]
     copies = [
@@ -376,28 +398,20 @@
     return call(inner_kernel, "inner_act", jax.ShapeDtypeStruct((EROWS, 256), BF), [VM], [], out_specs=VM)(part)
 
 
-def down_kernel(i0, i1, i2, i3, *refs):
-    pieces, (o_ref, w, sem) = refs[:8], refs[8:]
-    copies = [
-        pltpu.make_async_copy(p, w.at[pl.ds(i * 128, 128)], sem.at[i]) for i, p in enumerate(pieces)
-    ]
-    for c in copies:
-        c.start()
+def down_kernel(i0, i1, i2, i3, w, o_ref):
     inner = jnp.concatenate([i0[...], i1[...], i2[...], i3[...]], axis=1)
-    for c in copies:
-        c.wait()
     o_ref[...] = jnp.dot(inner, w[...], preferred_element_type=F32).astype(BF)
 
 
-def down(inners, pieces):
+def down(inners, held):
     return call(
         down_kernel,
         "down",
         pltpu.VMEM((EROWS, CHUNK), BF),
-        [VM] * 4 + [AT] * 8,
-        [pltpu.VMEM((1024, CHUNK), BF), pltpu.SemaphoreType.DMA((8,))],
+        [VM] * 5,
+        [],
         out_specs=VM,
-    )(*inners, *pieces)
+    )(*inners, held)
 
 
 def after(arrays, token):
@@ -524,7 +538,8 @@
         part = lax.all_to_all(part, "z", split_axis=0, concat_axis=0, tiled=True)
         inner = inner_act(part)
         inners = [inner] + [shift(inner, "z", NZ, d) for d in range(1, NZ)]
-        result = down(inners, [w for pair in zip(dn, dn_other) for w in pair])
+        held = gather([w for pair in zip(dn, dn_other) for w in pair])
+        result = down(inners, held)
 
     with jax.named_scope("return"):
         back = lax.all_to_all(

time: 210 us -> 207 us (0.986)
  waiting for transfers between devices: 53.9 us -> 51.4 us
    ppermute x33, waiting for transfers between devices: 17.8 us -> 15.4 us  [shift(): return lax.ppermute(a, axis, [(i, (i + d) % n) for i in range(n)])]
  transfers between devices with their start and end apart: 36 -> 36, of which waited for: 11 -> 11; matrix products, arithmetic and copies ran while one was open for 7% -> 7% of each run, Pallas kernels for 17% -> 18%
where the time goes in v5:
time: 207 us; the launch traced here: 204 us
  starting transfers between devices  56.1 us (27%)
  waiting for transfers between devices  51.4 us (25%)
  Pallas kernels  38.5 us (19%)
  blocking collectives  34.9 us (17%)
  local copies, waits for them, and re-layouts  15.6 us (8%)
  other arithmetic  5.83 us (3%)
    ppermute x33, starting transfers between devices, shift(): return lax.ppermute(a, axis, [(i, (i + d) % n) for i in range(n)])  37.7 us
    all_to_all x1, blocking collectives, shards(): lax.all_to_all(result.reshape(EXPERTS, SLOTS, CHUNK), ('y', 'x'), split_a...  24.4 us
    all_to_all x1, waiting for transfers between devices, shards(): part = lax.all_to_all(part, 'z', split_axis=0, concat_axis=0, tiled=True)  18.9 us
    pallas_call x1, Pallas kernels, attention(): call(attention_kernel, 'attention', (jax.ShapeDtypeStruct((64, GRP * VDIM...  16.5 us
    ppermute x33, waiting for transfers between devices, shift(): return lax.ppermute(a, axis, [(i, (i + d) % n) for i in range(n)])  15.4 us
    all_to_all x1, blocking collectives, shards(): done = lax.all_to_all(done, 'z', split_axis=0, concat_axis=0, tiled=True)  10.5 us
    all_to_all x1, waiting for transfers between devices, shards(): lax.all_to_all(q, ('y', 'core', 'z'), split_axis=0, concat_axis=0, tiled=...  8.9 us
    all_to_all x1, waiting for transfers between devices, shards(): lax.all_to_all(rows, ('y', 'x'), split_axis=0, concat_axis=0, tiled=True)  8.25 us
  transfers between devices with their start and end apart: 36, of which 11 were waited for; matrix products, arithmetic and copies ran while one was open for 7% of the time, Pallas kernels for 18%

profile of v5, /device:TPU:40, one launch (start us, length us, event | category | flops | bytes accessed | tf_op | source)
XLA Modules:
  0.0 203.6 jit_solution(17048837769309836982)
XLA Ops:
  0.0 1.5 copy.34.c0
  1.5 0.7 constant_dynamic-slice_fusion.2
  2.2 1.5 collective-permute-start
  3.7 2.7 %collective-permute-start.1 = (bf16[256,576]{1,0:T(8,128)(2,1)}, bf16[256,576]{1,0:T(8,128)(2,1)}, u32[]{:S(2)}, u32[]{:S(2)}) collective-permute-start(bf16[256,576]{1,0:T(8,128)(2,1)} %constant_dynamic-slice_fusion.2), channel_id=1, source_target_pairs={{0,16},{8,24},{16,0},{24,8},{1,17},{9,25},{17,1},{25,9},{2,18},{10... | collective-permute-start | bytes 884744 | tf_op jit(solution)/shard_map/cache_gather/ppermute | solution.py:40
  6.5 1.4 collective-permute-start.2
  8.3 3.3 %dynamic-slice_bitcast_fusion.4 = (bf16[1792,128]{1,0:T(8,128)(2,1)}, bf16[1792,128]{1,0:T(8,128)(2,1)}, bf16[1792,128]{1,0:T(8,128)(2,1)S(1)}, bf16[1792,128]{1...) fusion(bf16[4,1792,128]{2,1,0:T(8,128)(2,1)} %bitcast.69, ...), kind=kLoop, calls=%fused_computation.12 | loop fusion | bytes 7340048 | tf_op jit(solution)/shard_map/weights/jit(dynamic_index_in_dim)/squeeze | solution.py:475
  11.6 1.1 pad_maximum_fusion
  13.1 1.1 pad_maximum_fusion.1
  14.2 1.0 broadcast_in_dim.30
  15.2 8.2 %all-to-all-start = ((bf16[32,8,1664]{2,1,0:T(8,128)(2,1)}), bf16[32,8,1664]{2,1,0:T(8,128)(2,1)S(1)}, u32[]{:S(2)}, u32[]{:S(2)}) async-start(bf16[32,8,1664]{2,1,0:T(8,128)(2,1)} %bitcast.68), calls=%async_computation | async-start | bytes 1703936 | tf_op jit(solution)/shard_map/query_exchange/all_to_all | solution.py:464
  23.6 2.2 %pad_maximum_fusion.2 = bf16[1792,256]{1,0:T(8,128)(2,1)} fusion(bf16[1792,128]{1,0:T(8,128)(2,1)} %get-tuple-element.112, bf16[1792,128]{1,0:T(8,128)(2,1)} %get-tuple-element.122), kind=kLoop, calls=%fused_computation.6 | loop fusion | flops 1835008 | bytes 1835008 | tf_op jit(solution)/shard_map/weights/concatenate | solution.py:476
  26.9 8.9 %all-to-all-done = bf16[32,8,1664]{2,1,0:T(8,128)(2,1)S(1)} async-done(((bf16[32,8,1664]{2,1,0:T(8,128)(2,1)}), bf16[32,8,1664]{2,1,0:T(8,128)(2,1)S(1)}, u32[]{:S(2)}, u32[]{:S(2)}) %all-to-all-start) | async-done | bytes 852000 | tf_op jit(solution)/shard_map/query_exchange/all_to_all | solution.py:464
  35.8 2.1 %collective-permute-start.10 = (bf16[1792,256]{1,0:T(8,128)(2,1)}, bf16[1792,256]{1,0:T(8,128)(2,1)}, u32[]{:S(2)}, u32[]{:S(2)}) collective-permute-start(bf16[1792,256]{1,0:T(8,128)(2,1)} %pad_maximum_fusion.1), channel_id=1, source_target_pairs={{0,4},{2,6},{4,0},{6,2},{1,5},{3,7},{5,1},{7,3},{8,12},{10,14},{12... | collective-permute-start | bytes 2752520 | tf_op jit(solution)/shard_map/attention/ppermute | solution.py:40
  37.9 1.4 collective-permute-start.11
  41.1 1.2 copy-done.2
  42.3 1.0 copy-done.7
  43.3 16.5 %attention.1 = (bf16[64,1152]{1,0:T(8,128)(2,1)S(1)}, bf16[64,1152]{1,0:T(8,128)(2,1)S(1)}, bf16[64,1152]{1,0:T(8,128)(2,1)S(1)}, bf16[64,1152]{1,0:T(8,128)(2,1)S(1)}) custom-call(s32[8]{0:T(128)S(1)} %stack.57.pos_ref, bf16[4,64,1664]{2,1,0:T(8,128)(2,1)S(1)} %bitcast.62, s32[256,1]{1,0:T(8,128)S(1)} %copy.36.first_ref, s32[256,1]{1,0:T(8,128)S(1)} %select_n.190.last_ref, ...), custom_call_target="tpu_custom_call" | custom-call | bytes 1 | tf_op jit(solution)/shard_map/attention/attention/pallas_call | solution.py:146
  60.4 0.8 collective-permute-start.6
  61.2 2.7 %collective-permute-start.7 = (bf16[64,1152]{1,0:T(8,128)(2,1)S(1)}, bf16[64,1152]{1,0:T(8,128)(2,1)S(1)}, u32[]{:S(2)}, u32[]{:S(2)}) collective-permute-start(bf16[64,1152]{1,0:T(8,128)(2,1)S(1)} %get-tuple-element.56), channel_id=1, source_target_pairs={{0,64},{32,96},{64,0},{96,32},{1,65},{33,97},{65,1},{97,33},{2,66}... | collective-permute-start | bytes 442376 | tf_op jit(solution)/shard_map/combine/ppermute | solution.py:40
  63.9 3.0 %collective-permute-done.6.o1 = bf16[64,1152]{1,0:T(8,128)(2,1)S(1)} collective-permute-done((bf16[64,1152]{1,0:T(8,128)(2,1)S(1)}, bf16[64,1152]{1,0:T(8,128)(2,1)S(1)}, u32[]{:S(2)}, u32[]{:S(2)}) %collective-permute-start.6) | collective-permute-done | bytes 147488 | tf_op jit(solution)/shard_map/combine/ppermute | solution.py:40
  66.9 4.1 %collective-permute-start.8 = (bf16[64,1152]{1,0:T(8,128)(2,1)S(1)}, bf16[64,1152]{1,0:T(8,128)(2,1)S(1)}, u32[]{:S(2)}, u32[]{:S(2)}) collective-permute-start(bf16[64,1152]{1,0:T(8,128)(2,1)S(1)} %get-tuple-element.57), channel_id=1, source_target_pairs={{0,96},{32,0},{64,32},{96,64},{1,97},{33,1},{65,33},{97,65},{2,98}... | collective-permute-start | bytes 442376 | tf_op jit(solution)/shard_map/combine/ppermute | solution.py:40
  71.0 5.3 %stage.1.w_ref = bf16[1024,7168]{1,0:T(8,128)(2,1)S(1)} custom-call(bf16[64,1152]{1,0:T(8,128)(2,1)} %copy-done.3, bf16[1024,7168]{1,0:T(8,128)(2,1)} %w_ref.1), custom_call_target="tpu_custom_call" | custom-call | bytes 1 | tf_op jit(solution)/shard_map/combine/stage/pallas_call | solution.py:252
  77.0 2.0 project.2
  79.0 2.0 project.3
  81.6 0.8 collective-permute-done.17.refs_1_
  83.7 1.2 collective-permute-start.18
  85.0 0.9 collective-permute-start.15
  85.9 4.1 %collective-permute-start.16 = (bf16[32,1792]{1,0:T(8,128)(2,1)S(1)}, bf16[32,1792]{1,0:T(8,128)(2,1)S(1)}, u32[]{:S(2)}, u32[]{:S(2)}) collective-permute-start(bf16[32,1792]{1,0:T(8,128)(2,1)S(1)} %get-tuple-element.70), channel_id=1, source_target_pairs={{0,4},{2,6},{4,0},{6,2},{1,5},{3,7},{5,1},{7,3},{8,12},{10,14},{12... | collective-permute-start | bytes 344072 | tf_op jit(solution)/shard_map/out_projection/ppermute | solution.py:40
  90.7 0.8 broadcast_divide_fusion
  91.9 1.0 collective-permute-done.16.p2
  93.5 1.1 copy-done
  94.6 4.6 %all-to-all-start.1 = ((bf16[16,24,1792]{2,1,0:T(8,128)(2,1)}), bf16[16,24,1792]{2,1,0:T(8,128)(2,1)S(1)}, u32[]{:S(2)}, u32[]{:S(2)}) async-start(bf16[16,24,1792]{2,1,0:T(8,128)(2,1)} %bitcast.66), calls=%async_computation.1 | async-start | bytes 2752512 | tf_op jit(solution)/shard_map/dispatch/all_to_all | solution.py:529
  99.7 2.5 %dynamic-slice_bitcast_fusion = (bf16[128,1792]{1,0:T(8,128)(2,1)S(1)}, bf16[128,1792]{1,0:T(8,128)(2,1)}, bf16[128,1792]{1,0:T(8,128)(2,1)}, bf16[128,1792]{1,0:T(8,128)(2,1)}) fusion(bf16[1,128,7168]{2,1,0:T(8,128)(2,1)} %param.25, s32[]{:T(128)S(6)} %select_n.189, s32[]{:T(128)S(6)} %select_n.187, s32[]{:T(128)S(6)} %select_n.186, s32[]{:T(128)S(6)} %select_n.188), kind=kLoop, calls=%fused_computation.8 | loop fusion | bytes 3670032 | tf_op jit(solution)/shard_map/weights/dynamic_slice | solution.py:477
  102.2 2.1 %collective-permute-start.23 = (bf16[128,1792]{1,0:T(8,128)(2,1)}, bf16[128,1792]{1,0:T(8,128)(2,1)S(1)}, u32[]{:S(2)}, u32[]{:S(2)}) collective-permute-start(bf16[128,1792]{1,0:T(8,128)(2,1)} %get-tuple-element.90), channel_id=1, source_target_pairs={{0,2},{2,4},{4,6},{6,0},{1,3},{3,5},{5,7},{7,1},{8,10},{10,12},{12... | collective-permute-start | bytes 1376264 | tf_op jit(solution)/shard_map/dispatch/ppermute | solution.py:40
  104.4 3.6 %collective-permute-start.24 = (bf16[128,1792]{1,0:T(8,128)(2,1)}, bf16[128,1792]{1,0:T(8,128)(2,1)}, u32[]{:S(2)}, u32[]{:S(2)}) collective-permute-start(bf16[128,1792]{1,0:T(8,128)(2,1)} %get-tuple-element.91), channel_id=1, source_target_pairs={{0,4},{2,6},{4,0},{6,2},{1,5},{3,7},{5,1},{7,3},{8,12},{10,14},{12... | collective-permute-start | bytes 1376264 | tf_op jit(solution)/shard_map/dispatch/ppermute | solution.py:40
  108.3 8.2 %all-to-all-done.1 = bf16[16,24,1792]{2,1,0:T(8,128)(2,1)S(1)} async-done(((bf16[16,24,1792]{2,1,0:T(8,128)(2,1)}), bf16[16,24,1792]{2,1,0:T(8,128)(2,1)S(1)}, u32[]{:S(2)}, u32[]{:S(2)}) %all-to-all-start.1) | async-done | bytes 1376288 | tf_op jit(solution)/shard_map/dispatch/all_to_all | solution.py:529
  116.6 6.7 %gate_up.1 = bf16[4,400,512]{2,1,0:T(8,128)(2,1)} custom-call(s32[1]{0:T(128)} %bitcast.1.z_ref, bf16[384,1792]{1,0:T(8,128)(2,1)S(1)} %bitcast.65, f32[1,1792]{1,0:T(1,128)S(1)} %div.36.gain_ref, bf16[1792,256]{1,0:T(8,128)(2,1)S(1)} %pad_maximum_fusion.3.refs_0_, bf16[1792,256]{1,0:T(8,128)(2,1)} %collective-permute-done.19.refs_1_, ...), custom_call_target="tpu_custom_call" | custom-call | bytes 1 | tf_op jit(solution)/shard_map/experts/gate_up/pallas_call | solution.py:375
  123.3 5.3 %collective-permute-done.25.refs_6_ = bf16[128,1792]{1,0:T(8,128)(2,1)} collective-permute-done((bf16[128,1792]{1,0:T(8,128)(2,1)}, bf16[128,1792]{1,0:T(8,128)(2,1)}, u32[]{:S(2)}, u32[]{:S(2)}) %collective-permute-start.25) | collective-permute-done | bytes 458784 | tf_op jit(solution)/shard_map/dispatch/ppermute | solution.py:40
  128.6 5.5 %all-to-all-start.2 = ((bf16[4,400,512]{2,1,0:T(8,128)(2,1)}), bf16[4,400,512]{2,1,0:T(8,128)(2,1)S(1)}, u32[]{:S(2)}, u32[]{:S(2)}) async-start(bf16[4,400,512]{2,1,0:T(8,128)(2,1)} %gate_up.1), calls=%async_computation.2 | async-start | bytes 3276800 | tf_op jit(solution)/shard_map/experts/all_to_all | solution.py:538
  135.1 18.9 %all-to-all-done.2.part_ref = bf16[4,400,512]{2,1,0:T(8,128)(2,1)S(1)} async-done(((bf16[4,400,512]{2,1,0:T(8,128)(2,1)}), bf16[4,400,512]{2,1,0:T(8,128)(2,1)S(1)}, u32[]{:S(2)}, u32[]{:S(2)}) %all-to-all-start.2) | async-done | bytes 1638432 | tf_op jit(solution)/shard_map/experts/all_to_all | solution.py:538
  154.5 3.5 %collective-permute-start.27 = (bf16[384,256]{1,0:T(8,128)(2,1)S(1)}, bf16[384,256]{1,0:T(8,128)(2,1)S(1)}, u32[]{:S(2)}, u32[]{:S(2)}) collective-permute-start(bf16[384,256]{1,0:T(8,128)(2,1)S(1)} %inner_act.1.i0), channel_id=1, source_target_pairs={{0,4},{2,6},{4,0},{6,2},{1,5},{3,7},{5,1},{7,3},{8,12},{10,14},{12... | collective-permute-start | bytes 589832 | tf_op jit(solution)/shard_map/experts/ppermute | solution.py:40
  158.6 2.5 %down_weights.1.w = bf16[1024,1792]{1,0:T(8,128)(2,1)S(1)} custom-call(bf16[128,1792]{1,0:T(8,128)(2,1)S(1)} %get-tuple-element.97.refs_0_, bf16[128,1792]{1,0:T(8,128)(2,1)S(1)} %collective-permute-done.29.refs_1_, bf16[128,1792]{1,0:T(8,128)(2,1)S(1)} %collective-permute-done.23.refs_2_, bf16[128,1792]{1,0:T(8,128)(2,1)} %collective-permute-done.30.refs_3_, ...), custom_call_target="tpu_custom_call" | custom-call | bytes 1 | tf_op jit(solution)/shard_map/experts/down_weights/pallas_call | solution.py:336
  161.1 0.9 collective-permute-done.26.i1
  162.0 1.6 collective-permute-done.27.i2
  163.7 2.1 %collective-permute-done.28.i3 = bf16[384,256]{1,0:T(8,128)(2,1)S(1)} collective-permute-done((bf16[384,256]{1,0:T(8,128)(2,1)S(1)}, bf16[384,256]{1,0:T(8,128)(2,1)S(1)}, u32[]{:S(2)}, u32[]{:S(2)}) %collective-permute-start.28) | collective-permute-done | bytes 196640 | tf_op jit(solution)/shard_map/experts/ppermute | solution.py:40
  165.7 1.6 down.1
  167.3 24.4 %all_to_all.25 = bf16[16,24,1792]{2,1,0:T(8,128)(2,1)S(1)} all-to-all(bf16[16,24,1792]{2,1,0:T(8,128)(2,1)S(1)} %bitcast.64), channel_id=1, replica_groups=mesh['y'=4,'x'=4,'z'=4,'core'=2] {'y','x'}, dimensions={0} | all-to-all | bytes 2752512 | tf_op jit(solution)/shard_map/return/all_to_all | solution.py:545
  192.4 10.5 %all_to_all.26 = bf16[4,8,1792]{2,1,0:T(8,128)(2,1)S(1)} all-to-all(bf16[4,8,1792]{2,1,0:T(8,128)(2,1)S(1)} %fusion.1), channel_id=1, replica_groups=mesh['y'=4,'x'=4,'z'=4,'core'=2] {'z'}, dimensions={0} | all-to-all | bytes 229376 | tf_op jit(solution)/shard_map/return/all_to_all | solution.py:550
  (115 shorter events, 12.9 us)
Async XLA Ops:
  0.0 8.1 %slice-start = ((bf16[8,64,192]{2,1,0:T(8,128)(2,1)}), bf16[8,64,128]{2,1,0:T(8,128)(2,1)S(1)}, s32[]{:S(2)}) async-start(bf16[8,64,192]{2,1,0:T(8,128)(2,1)} %param.13), calls=%async_computation.5 | async-start | bytes 262144 | tf_op jit(solution)/shard_map/query_exchange/slice | solution.py:458
  0.0 8.1 %slice-start.1 = ((bf16[8,64,192]{2,1,0:T(8,128)(2,1)}), bf16[8,64,64]{2,1,0:T(8,128)(2,1)S(1)}, s32[]{:S(2)}) async-start(bf16[8,64,192]{2,1,0:T(8,128)(2,1)} %param.13), calls=%async_computation.6 | async-start | bytes 262144 | tf_op jit(solution)/shard_map/query_exchange/slice | solution.py:459
  0.0 7.9 %copy-start.10 = (s32[1024]{0:T(1024)S(1)}, s32[1024]{0:T(1024)}, u32[]{:S(2)}) copy-start(s32[1024]{0:T(1024)} %param.22) | copy-start | bytes 12292
  0.0 8.0 %copy-start.12 = (f32[8,8]{1,0:T(8,128)S(1)}, f32[8,8]{1,0:T(8,128)}, u32[]{:S(2)}) copy-start(f32[8,8]{1,0:T(8,128)} %param.21) | copy-start | bytes 772
  0.0 8.1 %copy-start.11 = (s32[8,8]{1,0:T(8,128)S(1)}, s32[8,8]{1,0:T(8,128)}, u32[]{:S(2)}) copy-start(s32[8,8]{1,0:T(8,128)} %param.20) | copy-start | bytes 772
  2.2 12.0 %collective-permute-start = (bf16[256,576]{1,0:T(8,128)(2,1)}, bf16[256,576]{1,0:T(8,128)(2,1)S(1)}, u32[]{:S(2)}, u32[]{:S(2)}) collective-permute-start(bf16[256,576]{1,0:T(8,128)(2,1)} %constant_dynamic-slice_fusion.2), channel_id=1, source_target_pairs={{0,8},{8,16},{16,24},{24,0},{1,9},{9,17},{17,25},{25,1},{2,10},{10... | collective-permute-start | bytes 884744 | tf_op jit(solution)/shard_map/cache_gather/ppermute | solution.py:40
  3.7 22.5 %collective-permute-start.1 = (bf16[256,576]{1,0:T(8,128)(2,1)}, bf16[256,576]{1,0:T(8,128)(2,1)}, u32[]{:S(2)}, u32[]{:S(2)}) collective-permute-start(bf16[256,576]{1,0:T(8,128)(2,1)} %constant_dynamic-slice_fusion.2), channel_id=1, source_target_pairs={{0,16},{8,24},{16,0},{24,8},{1,17},{9,25},{17,1},{25,9},{2,18},{10... | collective-permute-start | bytes 884744 | tf_op jit(solution)/shard_map/cache_gather/ppermute | solution.py:40
  6.5 20.2 %collective-permute-start.2 = (bf16[256,576]{1,0:T(8,128)(2,1)}, bf16[256,576]{1,0:T(8,128)(2,1)}, u32[]{:S(2)}, u32[]{:S(2)}) collective-permute-start(bf16[256,576]{1,0:T(8,128)(2,1)} %constant_dynamic-slice_fusion.2), channel_id=1, source_target_pairs={{0,24},{8,0},{16,8},{24,16},{1,25},{9,1},{17,9},{25,17},{2,26},{10... | collective-permute-start | bytes 884744 | tf_op jit(solution)/shard_map/cache_gather/ppermute | solution.py:40
  15.2 25.9 %copy-start.1 = (bf16[8,128,512]{2,1,0:T(8,128)(2,1)S(1)}, bf16[8,128,512]{2,1,0:T(8,128)(2,1)}, u32[]{:S(2)}) copy-start(bf16[8,128,512]{2,1,0:T(8,128)(2,1)} %ak_ref.1) | copy-start | bytes 3145732
  15.2 20.6 %all-to-all-start = ((bf16[32,8,1664]{2,1,0:T(8,128)(2,1)}), bf16[32,8,1664]{2,1,0:T(8,128)(2,1)S(1)}, u32[]{:S(2)}, u32[]{:S(2)}) async-start(bf16[32,8,1664]{2,1,0:T(8,128)(2,1)} %bitcast.68), calls=%async_computation | async-start | bytes 1703936 | tf_op jit(solution)/shard_map/query_exchange/all_to_all | solution.py:464
  26.0 13.3 %collective-permute-start.3 = (bf16[256,576]{1,0:T(8,128)(2,1)S(1)}, bf16[256,576]{1,0:T(8,128)(2,1)S(1)}, u32[]{:S(2)}, u32[]{:S(2)}) collective-permute-start(bf16[256,576]{1,0:T(8,128)(2,1)S(1)} %collective-permute-done.c1), channel_id=1, source_target_pairs={{0,1},{1,0},{2,3},{3,2},{4,5},{5,4},{6,7},{7,6},{8,9},{9,8},{10,11... | collective-permute-start | bytes 884744 | tf_op jit(solution)/shard_map/cache_share/ppermute | solution.py:40
  26.3 14.8 %collective-permute-start.4 = (bf16[256,576]{1,0:T(8,128)(2,1)}, bf16[256,576]{1,0:T(8,128)(2,1)}, u32[]{:S(2)}, u32[]{:S(2)}) collective-permute-start(bf16[256,576]{1,0:T(8,128)(2,1)} %collective-permute-done.1.c2), channel_id=1, source_target_pairs={{0,1},{1,0},{2,3},{3,2},{4,5},{5,4},{6,7},{7,6},{8,9},{9,8},{10,11... | collective-permute-start | bytes 884744 | tf_op jit(solution)/shard_map/cache_share/ppermute | solution.py:40
  26.6 14.5 %collective-permute-start.5 = (bf16[256,576]{1,0:T(8,128)(2,1)}, bf16[256,576]{1,0:T(8,128)(2,1)}, u32[]{:S(2)}, u32[]{:S(2)}) collective-permute-start(bf16[256,576]{1,0:T(8,128)(2,1)} %collective-permute-done.2.c3), channel_id=1, source_target_pairs={{0,1},{1,0},{2,3},{3,2},{4,5},{5,4},{6,7},{7,6},{8,9},{9,8},{10,11... | collective-permute-start | bytes 884744 | tf_op jit(solution)/shard_map/cache_share/ppermute | solution.py:40
  35.8 49.2 %collective-permute-start.10 = (bf16[1792,256]{1,0:T(8,128)(2,1)}, bf16[1792,256]{1,0:T(8,128)(2,1)}, u32[]{:S(2)}, u32[]{:S(2)}) collective-permute-start(bf16[1792,256]{1,0:T(8,128)(2,1)} %pad_maximum_fusion.1), channel_id=1, source_target_pairs={{0,4},{2,6},{4,0},{6,2},{1,5},{3,7},{5,1},{7,3},{8,12},{10,14},{12... | collective-permute-start | bytes 2752520 | tf_op jit(solution)/shard_map/attention/ppermute | solution.py:40
  37.9 48.0 %collective-permute-start.11 = (bf16[1792,256]{1,0:T(8,128)(2,1)}, bf16[1792,256]{1,0:T(8,128)(2,1)}, u32[]{:S(2)}, u32[]{:S(2)}) collective-permute-start(bf16[1792,256]{1,0:T(8,128)(2,1)} %pad_maximum_fusion.2), channel_id=1, source_target_pairs={{0,6},{2,0},{4,2},{6,4},{1,7},{3,1},{5,3},{7,5},{8,14},{10,8},{12,... | collective-permute-start | bytes 2752520 | tf_op jit(solution)/shard_map/attention/ppermute | solution.py:40
  40.1 50.0 %collective-permute-start.9 = (bf16[1792,256]{1,0:T(8,128)(2,1)}, bf16[1792,256]{1,0:T(8,128)(2,1)}, u32[]{:S(2)}, u32[]{:S(2)}) collective-permute-start(bf16[1792,256]{1,0:T(8,128)(2,1)} %pad_maximum_fusion), channel_id=1, source_target_pairs={{0,2},{2,4},{4,6},{6,0},{1,3},{3,5},{5,7},{7,1},{8,10},{10,12},{12... | collective-permute-start | bytes 2752520 | tf_op jit(solution)/shard_map/attention/ppermute | solution.py:40
  41.1 1.2 copy-start.2
  60.4 6.4 %collective-permute-start.6 = (bf16[64,1152]{1,0:T(8,128)(2,1)S(1)}, bf16[64,1152]{1,0:T(8,128)(2,1)S(1)}, u32[]{:S(2)}, u32[]{:S(2)}) collective-permute-start(bf16[64,1152]{1,0:T(8,128)(2,1)S(1)} %get-tuple-element.55), channel_id=1, source_target_pairs={{0,32},{32,64},{64,96},{96,0},{1,33},{33,65},{65,97},{97,1},{2,34}... | collective-permute-start | bytes 442376 | tf_op jit(solution)/shard_map/combine/ppermute | solution.py:40
  61.2 15.2 %collective-permute-start.7 = (bf16[64,1152]{1,0:T(8,128)(2,1)S(1)}, bf16[64,1152]{1,0:T(8,128)(2,1)S(1)}, u32[]{:S(2)}, u32[]{:S(2)}) collective-permute-start(bf16[64,1152]{1,0:T(8,128)(2,1)S(1)} %get-tuple-element.56), channel_id=1, source_target_pairs={{0,64},{32,96},{64,0},{96,32},{1,65},{33,97},{65,1},{97,33},{2,66}... | collective-permute-start | bytes 442376 | tf_op jit(solution)/shard_map/combine/ppermute | solution.py:40
  66.9 9.5 %collective-permute-start.8 = (bf16[64,1152]{1,0:T(8,128)(2,1)S(1)}, bf16[64,1152]{1,0:T(8,128)(2,1)S(1)}, u32[]{:S(2)}, u32[]{:S(2)}) collective-permute-start(bf16[64,1152]{1,0:T(8,128)(2,1)S(1)} %get-tuple-element.57), channel_id=1, source_target_pairs={{0,96},{32,0},{64,32},{96,64},{1,97},{33,1},{65,33},{97,65},{2,98}... | collective-permute-start | bytes 442376 | tf_op jit(solution)/shard_map/combine/ppermute | solution.py:40
  71.0 5.4 %copy-start.4 = (bf16[64,1152]{1,0:T(8,128)(2,1)S(1)}, bf16[64,1152]{1,0:T(8,128)(2,1)}, u32[]{:S(2)}) copy-start(bf16[64,1152]{1,0:T(8,128)(2,1)} %copy-done.3) | copy-start | bytes 442372
  71.0 6.0 %copy-start.5 = (bf16[8,7168]{1,0:T(8,128)(2,1)S(1)}, bf16[8,7168]{1,0:T(8,128)(2,1)}, u32[]{:S(2)}) copy-start(bf16[8,7168]{1,0:T(8,128)(2,1)} %res_ref.3) | copy-start | bytes 344068
  79.0 3.6 %copy-start.8 = (bf16[1792,128]{1,0:T(8,128)(2,1)S(1)}, bf16[1792,128]{1,0:T(8,128)(2,1)}, u32[]{:S(2)}) copy-start(bf16[1792,128]{1,0:T(8,128)(2,1)} %get-tuple-element.111) | copy-start | bytes 1376260
  79.0 3.6 %copy-start.9 = (bf16[1792,128]{1,0:T(8,128)(2,1)S(1)}, bf16[1792,128]{1,0:T(8,128)(2,1)}, u32[]{:S(2)}) copy-start(bf16[1792,128]{1,0:T(8,128)(2,1)} %get-tuple-element.123) | copy-start | bytes 1376260
  81.0 1.4 collective-permute-start.17
  81.1 1.6 collective-permute-start.13
  82.4 1.3 collective-permute-start.14
  82.6 7.5 %collective-permute-start.12 = (bf16[32,1792]{1,0:T(8,128)(2,1)S(1)}, bf16[32,1792]{1,0:T(8,128)(2,1)S(1)}, u32[]{:S(2)}, u32[]{:S(2)}) collective-permute-start(bf16[32,1792]{1,0:T(8,128)(2,1)S(1)} %get-tuple-element.65), channel_id=1, source_target_pairs={{0,1},{1,0},{2,3},{3,2},{4,5},{5,4},{6,7},{7,6},{8,9},{9,8},{10,11... | collective-permute-start | bytes 344072 | tf_op jit(solution)/shard_map/out_projection/ppermute | solution.py:40
  83.7 8.2 %collective-permute-start.18 = (bf16[32,1792]{1,0:T(8,128)(2,1)S(1)}, bf16[32,1792]{1,0:T(8,128)(2,1)S(1)}, u32[]{:S(2)}, u32[]{:S(2)}) collective-permute-start(bf16[32,1792]{1,0:T(8,128)(2,1)S(1)} %fold.3), channel_id=1, source_target_pairs={{0,6},{2,0},{4,2},{6,4},{1,7},{3,1},{5,3},{7,5},{8,14},{10,8},{12,... | collective-permute-start | bytes 344072 | tf_op jit(solution)/shard_map/out_projection/ppermute | solution.py:40
  85.0 6.9 %collective-permute-start.15 = (bf16[32,1792]{1,0:T(8,128)(2,1)S(1)}, bf16[32,1792]{1,0:T(8,128)(2,1)S(1)}, u32[]{:S(2)}, u32[]{:S(2)}) collective-permute-start(bf16[32,1792]{1,0:T(8,128)(2,1)S(1)} %get-tuple-element.69), channel_id=1, source_target_pairs={{0,2},{2,4},{4,6},{6,0},{1,3},{3,5},{5,7},{7,1},{8,10},{10,12},{12... | collective-permute-start | bytes 344072 | tf_op jit(solution)/shard_map/out_projection/ppermute | solution.py:40
  85.9 7.0 %collective-permute-start.16 = (bf16[32,1792]{1,0:T(8,128)(2,1)S(1)}, bf16[32,1792]{1,0:T(8,128)(2,1)S(1)}, u32[]{:S(2)}, u32[]{:S(2)}) collective-permute-start(bf16[32,1792]{1,0:T(8,128)(2,1)S(1)} %get-tuple-element.70), channel_id=1, source_target_pairs={{0,4},{2,6},{4,0},{6,2},{1,5},{3,7},{5,1},{7,3},{8,12},{10,14},{12... | collective-permute-start | bytes 344072 | tf_op jit(solution)/shard_map/out_projection/ppermute | solution.py:40
  90.1 14.3 %collective-permute-start.19 = (bf16[1792,256]{1,0:T(8,128)(2,1)S(1)}, bf16[1792,256]{1,0:T(8,128)(2,1)}, u32[]{:S(2)}, u32[]{:S(2)}) collective-permute-start(bf16[1792,256]{1,0:T(8,128)(2,1)S(1)} %pad_maximum_fusion.3.refs_0_), channel_id=1, source_target_pairs={{0,1},{1,0},{2,3},{3,2},{4,5},{5,4},{6,7},{7,6},{8,9},{9,8},{10,11... | collective-permute-start | bytes 2752520 | tf_op jit(solution)/shard_map/dispatch/ppermute | solution.py:40
  90.2 17.7 %collective-permute-start.20 = (bf16[1792,256]{1,0:T(8,128)(2,1)}, bf16[1792,256]{1,0:T(8,128)(2,1)}, u32[]{:S(2)}, u32[]{:S(2)}) collective-permute-start(bf16[1792,256]{1,0:T(8,128)(2,1)} %collective-permute-done.9.refs_2_), channel_id=1, source_target_pairs={{0,1},{1,0},{2,3},{3,2},{4,5},{5,4},{6,7},{7,6},{8,9},{9,8},{10,11... | collective-permute-start | bytes 2752520 | tf_op jit(solution)/shard_map/dispatch/ppermute | solution.py:40
  93.5 1.1 copy-start
  94.6 22.0 %all-to-all-start.1 = ((bf16[16,24,1792]{2,1,0:T(8,128)(2,1)}), bf16[16,24,1792]{2,1,0:T(8,128)(2,1)S(1)}, u32[]{:S(2)}, u32[]{:S(2)}) async-start(bf16[16,24,1792]{2,1,0:T(8,128)(2,1)} %bitcast.66), calls=%async_computation.1 | async-start | bytes 2752512 | tf_op jit(solution)/shard_map/dispatch/all_to_all | solution.py:529
  99.2 9.1 %collective-permute-start.21 = (bf16[1792,256]{1,0:T(8,128)(2,1)}, bf16[1792,256]{1,0:T(8,128)(2,1)}, u32[]{:S(2)}, u32[]{:S(2)}) collective-permute-start(bf16[1792,256]{1,0:T(8,128)(2,1)} %collective-permute-done.10.refs_4_), channel_id=1, source_target_pairs={{0,1},{1,0},{2,3},{3,2},{4,5},{5,4},{6,7},{7,6},{8,9},{9,8},{10,11... | collective-permute-start | bytes 2752520 | tf_op jit(solution)/shard_map/dispatch/ppermute | solution.py:40
  99.2 9.1 %collective-permute-start.22 = (bf16[1792,256]{1,0:T(8,128)(2,1)}, bf16[1792,256]{1,0:T(8,128)(2,1)}, u32[]{:S(2)}, u32[]{:S(2)}) collective-permute-start(bf16[1792,256]{1,0:T(8,128)(2,1)} %collective-permute-done.11.refs_6_), channel_id=1, source_target_pairs={{0,1},{1,0},{2,3},{3,2},{4,5},{5,4},{6,7},{7,6},{8,9},{9,8},{10,11... | collective-permute-start | bytes 2752520 | tf_op jit(solution)/shard_map/dispatch/ppermute | solution.py:40
  102.2 21.0 %collective-permute-start.23 = (bf16[128,1792]{1,0:T(8,128)(2,1)}, bf16[128,1792]{1,0:T(8,128)(2,1)S(1)}, u32[]{:S(2)}, u32[]{:S(2)}) collective-permute-start(bf16[128,1792]{1,0:T(8,128)(2,1)} %get-tuple-element.90), channel_id=1, source_target_pairs={{0,2},{2,4},{4,6},{6,0},{1,3},{3,5},{5,7},{7,1},{8,10},{10,12},{12... | collective-permute-start | bytes 1376264 | tf_op jit(solution)/shard_map/dispatch/ppermute | solution.py:40
  104.4 18.9 %collective-permute-start.24 = (bf16[128,1792]{1,0:T(8,128)(2,1)}, bf16[128,1792]{1,0:T(8,128)(2,1)}, u32[]{:S(2)}, u32[]{:S(2)}) collective-permute-start(bf16[128,1792]{1,0:T(8,128)(2,1)} %get-tuple-element.91), channel_id=1, source_target_pairs={{0,4},{2,6},{4,0},{6,2},{1,5},{3,7},{5,1},{7,3},{8,12},{10,14},{12... | collective-permute-start | bytes 1376264 | tf_op jit(solution)/shard_map/dispatch/ppermute | solution.py:40
  107.9 20.6 %collective-permute-start.25 = (bf16[128,1792]{1,0:T(8,128)(2,1)}, bf16[128,1792]{1,0:T(8,128)(2,1)}, u32[]{:S(2)}, u32[]{:S(2)}) collective-permute-start(bf16[128,1792]{1,0:T(8,128)(2,1)} %get-tuple-element.92), channel_id=1, source_target_pairs={{0,6},{2,0},{4,2},{6,4},{1,7},{3,1},{5,3},{7,5},{8,14},{10,8},{12,... | collective-permute-start | bytes 1376264 | tf_op jit(solution)/shard_map/dispatch/ppermute | solution.py:40
  128.6 25.4 %all-to-all-start.2 = ((bf16[4,400,512]{2,1,0:T(8,128)(2,1)}), bf16[4,400,512]{2,1,0:T(8,128)(2,1)S(1)}, u32[]{:S(2)}, u32[]{:S(2)}) async-start(bf16[4,400,512]{2,1,0:T(8,128)(2,1)} %gate_up.1), calls=%async_computation.2 | async-start | bytes 3276800 | tf_op jit(solution)/shard_map/experts/all_to_all | solution.py:538
  134.0 20.5 %collective-permute-start.29 = (bf16[128,1792]{1,0:T(8,128)(2,1)S(1)}, bf16[128,1792]{1,0:T(8,128)(2,1)S(1)}, u32[]{:S(2)}, u32[]{:S(2)}) collective-permute-start(bf16[128,1792]{1,0:T(8,128)(2,1)S(1)} %get-tuple-element.97.refs_0_), channel_id=1, source_target_pairs={{0,1},{1,0},{2,3},{3,2},{4,5},{5,4},{6,7},{7,6},{8,9},{9,8},{10,11... | collective-permute-start | bytes 1376264 | tf_op jit(solution)/shard_map/experts/ppermute | solution.py:40
  134.0 24.0 %collective-permute-start.30 = (bf16[128,1792]{1,0:T(8,128)(2,1)S(1)}, bf16[128,1792]{1,0:T(8,128)(2,1)}, u32[]{:S(2)}, u32[]{:S(2)}) collective-permute-start(bf16[128,1792]{1,0:T(8,128)(2,1)S(1)} %collective-permute-done.23.refs_2_), channel_id=1, source_target_pairs={{0,1},{1,0},{2,3},{3,2},{4,5},{5,4},{6,7},{7,6},{8,9},{9,8},{10,11... | collective-permute-start | bytes 1376264 | tf_op jit(solution)/shard_map/experts/ppermute | solution.py:40
  134.6 24.0 %collective-permute-start.31 = (bf16[128,1792]{1,0:T(8,128)(2,1)}, bf16[128,1792]{1,0:T(8,128)(2,1)}, u32[]{:S(2)}, u32[]{:S(2)}) collective-permute-start(bf16[128,1792]{1,0:T(8,128)(2,1)} %collective-permute-done.24.refs_4_), channel_id=1, source_target_pairs={{0,1},{1,0},{2,3},{3,2},{4,5},{5,4},{6,7},{7,6},{8,9},{9,8},{10,11... | collective-permute-start | bytes 1376264 | tf_op jit(solution)/shard_map/experts/ppermute | solution.py:40
  134.6 24.0 %collective-permute-start.32 = (bf16[128,1792]{1,0:T(8,128)(2,1)}, bf16[128,1792]{1,0:T(8,128)(2,1)}, u32[]{:S(2)}, u32[]{:S(2)}) collective-permute-start(bf16[128,1792]{1,0:T(8,128)(2,1)} %collective-permute-done.25.refs_6_), channel_id=1, source_target_pairs={{0,1},{1,0},{2,3},{3,2},{4,5},{5,4},{6,7},{7,6},{8,9},{9,8},{10,11... | collective-permute-start | bytes 1376264 | tf_op jit(solution)/shard_map/experts/ppermute | solution.py:40
  154.4 7.6 %collective-permute-start.26 = (bf16[384,256]{1,0:T(8,128)(2,1)S(1)}, bf16[384,256]{1,0:T(8,128)(2,1)S(1)}, u32[]{:S(2)}, u32[]{:S(2)}) collective-permute-start(bf16[384,256]{1,0:T(8,128)(2,1)S(1)} %inner_act.1.i0), channel_id=1, source_target_pairs={{0,2},{2,4},{4,6},{6,0},{1,3},{3,5},{5,7},{7,1},{8,10},{10,12},{12... | collective-permute-start | bytes 589832 | tf_op jit(solution)/shard_map/experts/ppermute | solution.py:40
  154.5 9.1 %collective-permute-start.27 = (bf16[384,256]{1,0:T(8,128)(2,1)S(1)}, bf16[384,256]{1,0:T(8,128)(2,1)S(1)}, u32[]{:S(2)}, u32[]{:S(2)}) collective-permute-start(bf16[384,256]{1,0:T(8,128)(2,1)S(1)} %inner_act.1.i0), channel_id=1, source_target_pairs={{0,4},{2,6},{4,0},{6,2},{1,5},{3,7},{5,1},{7,3},{8,12},{10,14},{12... | collective-permute-start | bytes 589832 | tf_op jit(solution)/shard_map/experts/ppermute | solution.py:40
  158.0 7.7 %collective-permute-start.28 = (bf16[384,256]{1,0:T(8,128)(2,1)S(1)}, bf16[384,256]{1,0:T(8,128)(2,1)S(1)}, u32[]{:S(2)}, u32[]{:S(2)}) collective-permute-start(bf16[384,256]{1,0:T(8,128)(2,1)S(1)} %inner_act.1.i0), channel_id=1, source_target_pairs={{0,6},{2,0},{4,2},{6,4},{1,7},{3,1},{5,3},{7,5},{8,14},{10,8},{12,... | collective-permute-start | bytes 589832 | tf_op jit(solution)/shard_map/experts/ppermute | solution.py:40
  (3 other events, 2.4 us)

commit v6 on v5

--- a/solution.py
+++ b/solution.py
@@ -378,6 +378,7 @@
         pltpu.VMEM((NZ, EROWS + 16, 512), BF),
         [SM, VM, VM] + [AT] * 8,
         [pltpu.VMEM((CHUNK, 2048), BF), pltpu.SemaphoreType.DMA((8,))],
+        mib=56,
         out_specs=VM,
     )(z, x, gain, *pieces)
 
@@ -494,6 +495,7 @@
         place_of = jnp.stack(at + [y]).astype(jnp.int32)
 
         ahead = after(gu[1:], q)
+        q, *dn = lax.optimization_barrier((q, *dn))
         gu = gu[:1] + [shift(w, "z", NZ, d + 1) for d, w in enumerate(ahead)]
         outs = attention(place_of, q.reshape(NY, 64, QCOLS), first, last, [latent_cache] + mine + other, absorb_key, absorb_value)
 
@@ -516,6 +518,7 @@
         gu = gu[:1] + list(moved)
         part1, part2 = fold([keep1, keep2], swap1)
         (part3,) = fold([keep3], swap2[:1])
+        sums = part3
         parts = [shift(p, "z", NZ, d + 1) for d, p in enumerate((part1, part2, part3))]
         parts = [keep, swap2[1]] + parts
 
@@ -523,7 +526,7 @@
         gain = lax.dynamic_slice_in_dim(norm_gain, z * CHUNK, CHUNK)[None]
         gu_other = [shift(w, "core", 2, 1) for w in after(gu, keep)]
         hidden, rows = spread(parts, gain, pick)
-        ahead = after(dn[1:], hidden)
+        ahead = after(dn[1:], sums)
         dn = dn[:1] + [shift(w, "z", NZ, d + 1) for d, w in enumerate(ahead)]
         rows = rows.reshape(EXPERTS, SLOTS, CHUNK)
         rows = lax.all_to_all(rows, ("y", "x"), split_axis=0, concat_axis=0, tiled=True)

time: 207 us -> 207 us (level)
  waiting for transfers between devices: 51.4 us -> 48 us
  Pallas kernels: 38.5 us -> 40.6 us
    ppermute x33, waiting for transfers between devices: 15.4 us -> 10.7 us  [shift(): return lax.ppermute(a, axis, [(i, (i + d) % n) for i in range(n)])]
    all_to_all x1, blocking collectives: 24.4 us -> 26.5 us  [shards(): lax.all_to_all(result.reshape(EXPERTS, SLOTS, CHUNK), ('y', 'x'), split_a...]
    all_to_all x1, waiting for transfers between devices: 8.25 us -> 10.4 us  [shards(): lax.all_to_all(rows, ('y', 'x'), split_axis=0, concat_axis=0, tiled=True)]
    unnamed x28 -> x32, local copies, waits for them, and re-layouts: 6.81 us -> 5.74 us
  transfers between devices with their start and end apart: 36 -> 36, of which waited for: 11 -> 10; matrix products, arithmetic and copies ran while one was open for 7% -> 7% of each run, Pallas kernels for 18% -> 19%
where the time goes in v6:
time: 207 us; the launch traced here: 203 us
  starting transfers between devices  56.2 us (27%)
  waiting for transfers between devices  48 us (23%)
  Pallas kernels  40.6 us (20%)
  blocking collectives  36.8 us (18%)
  local copies, waits for them, and re-layouts  15.1 us (7%)
  other arithmetic  5.61 us (3%)
    ppermute x33, starting transfers between devices, shift(): return lax.ppermute(a, axis, [(i, (i + d) % n) for i in range(n)])  37.9 us
    all_to_all x1, blocking collectives, shards(): lax.all_to_all(result.reshape(EXPERTS, SLOTS, CHUNK), ('y', 'x'), split_a...  26.5 us
    all_to_all x1, waiting for transfers between devices, shards(): part = lax.all_to_all(part, 'z', split_axis=0, concat_axis=0, tiled=True)  18.4 us
    pallas_call x1, Pallas kernels, attention(): call(attention_kernel, 'attention', (jax.ShapeDtypeStruct((64, GRP * VDIM...  16.5 us
    ppermute x33, waiting for transfers between devices, shift(): return lax.ppermute(a, axis, [(i, (i + d) % n) for i in range(n)])  10.7 us
    all_to_all x1, waiting for transfers between devices, shards(): lax.all_to_all(rows, ('y', 'x'), split_axis=0, concat_axis=0, tiled=True)  10.4 us
    all_to_all x1, blocking collectives, shards(): done = lax.all_to_all(done, 'z', split_axis=0, concat_axis=0, tiled=True)  10.3 us
    all_to_all x1, waiting for transfers between devices, shards(): lax.all_to_all(q, ('y', 'core', 'z'), split_axis=0, concat_axis=0, tiled=...  8.48 us
  transfers between devices with their start and end apart: 36, of which 10 were waited for; matrix products, arithmetic and copies ran while one was open for 7% of the time, Pallas kernels for 19%

profile of v6, /device:TPU:40, one launch (start us, length us, event | category | flops | bytes accessed | tf_op | source)
XLA Modules:
  0.0 203.4 jit_solution(11272566053108312380)
XLA Ops:
  0.0 1.4 copy.34.c0
  2.2 1.5 collective-permute-start
  3.7 2.7 %collective-permute-start.1 = (bf16[256,576]{1,0:T(8,128)(2,1)}, bf16[256,576]{1,0:T(8,128)(2,1)}, u32[]{:S(2)}, u32[]{:S(2)}) collective-permute-start(bf16[256,576]{1,0:T(8,128)(2,1)} %constant_dynamic-slice_fusion.2), channel_id=1, source_target_pairs={{0,16},{8,24},{16,0},{24,8},{1,17},{9,25},{17,1},{25,9},{2,18},{10... | collective-permute-start | bytes 884744 | tf_op jit(solution)/shard_map/cache_gather/ppermute | solution.py:40
  6.5 1.4 collective-permute-start.2
  8.4 3.2 %dynamic-slice_bitcast_fusion = (bf16[1792,128]{1,0:T(8,128)(2,1)}, bf16[1792,128]{1,0:T(8,128)(2,1)S(1)}, bf16[1792,128]{1,0:T(8,128)(2,1)S(1)}, bf16[1792,128]...) fusion(bf16[4,1792,128]{2,1,0:T(8,128)(2,1)} %bitcast.66, ...), kind=kLoop, calls=%fused_computation.5 | loop fusion | bytes 7340048 | tf_op jit(solution)/shard_map/weights/jit(dynamic_index_in_dim)/squeeze | solution.py:476
  11.6 1.1 pad_maximum_fusion
  12.6 1.1 pad_maximum_fusion.1
  14.1 1.0 pad_maximum_fusion.2
  15.1 1.0 broadcast_in_dim.30
  16.2 8.1 %all-to-all-start = ((bf16[32,8,1664]{2,1,0:T(8,128)(2,1)}), bf16[32,8,1664]{2,1,0:T(8,128)(2,1)S(1)}, u32[]{:S(2)}, u32[]{:S(2)}) async-start(bf16[32,8,1664]{2,1,0:T(8,128)(2,1)} %bitcast.11), calls=%async_computation | async-start | bytes 1703936 | tf_op jit(solution)/shard_map/query_exchange/all_to_all | solution.py:465
  24.4 2.6 %dynamic-slice_bitcast_fusion.8 = (bf16[128,1792]{1,0:T(8,128)(2,1)}, bf16[128,1792]{1,0:T(8,128)(2,1)}, bf16[128,1792]{1,0:T(8,128)(2,1)S(1)}, bf16[128,1792]{1,0:T(8,128)(2,1)}) fusion(bf16[1,128,7168]{2,1,0:T(8,128)(2,1)} %param.25, s32[]{:T(128)S(6)} %select_n.172, s32[]{:T(128)S(6)} %select_n.168, s32[]{:T(128)S(6)} %select_n.166, s32[]{:T(128)S(6)} %select_n.170), kind=kLoop, calls=%fused_computation.13 | loop fusion | bytes 3670032 | tf_op jit(solution)/shard_map/weights/dynamic_slice | solution.py:478
  28.1 8.5 %all-to-all-done = bf16[32,8,1664]{2,1,0:T(8,128)(2,1)S(1)} async-done(((bf16[32,8,1664]{2,1,0:T(8,128)(2,1)}), bf16[32,8,1664]{2,1,0:T(8,128)(2,1)S(1)}, u32[]{:S(2)}, u32[]{:S(2)}) %all-to-all-start) | async-done | bytes 852000 | tf_op jit(solution)/shard_map/query_exchange/all_to_all | solution.py:465
  36.6 2.1 %collective-permute-start.10 = (bf16[1792,256]{1,0:T(8,128)(2,1)}, bf16[1792,256]{1,0:T(8,128)(2,1)}, u32[]{:S(2)}, u32[]{:S(2)}) collective-permute-start(bf16[1792,256]{1,0:T(8,128)(2,1)} %pad_maximum_fusion.1), channel_id=1, source_target_pairs={{0,4},{2,6},{4,0},{6,2},{1,5},{3,7},{5,1},{7,3},{8,12},{10,14},{12... | collective-permute-start | bytes 2752520 | tf_op jit(solution)/shard_map/attention/ppermute | solution.py:40
  38.7 1.4 collective-permute-start.11
  41.2 1.2 copy-done.1
  42.5 1.0 copy-done.8
  43.4 16.5 %attention.1 = (bf16[64,1152]{1,0:T(8,128)(2,1)S(1)}, bf16[64,1152]{1,0:T(8,128)(2,1)S(1)}, bf16[64,1152]{1,0:T(8,128)(2,1)S(1)}, bf16[64,1152]{1,0:T(8,128)(2,1)S(1)}) custom-call(s32[8]{0:T(128)S(1)} %stack.57.pos_ref, bf16[4,64,1664]{2,1,0:T(8,128)(2,1)S(1)} %bitcast.62, s32[256,1]{1,0:T(8,128)S(1)} %copy.36.first_ref, s32[256,1]{1,0:T(8,128)S(1)} %select_n.190.last_ref, ...), custom_call_target="tpu_custom_call" | custom-call | bytes 1 | tf_op jit(solution)/shard_map/attention/attention/pallas_call | solution.py:146
  60.6 0.8 collective-permute-start.6
  61.3 2.7 %collective-permute-start.7 = (bf16[64,1152]{1,0:T(8,128)(2,1)S(1)}, bf16[64,1152]{1,0:T(8,128)(2,1)S(1)}, u32[]{:S(2)}, u32[]{:S(2)}) collective-permute-start(bf16[64,1152]{1,0:T(8,128)(2,1)S(1)} %get-tuple-element.62), channel_id=1, source_target_pairs={{0,64},{32,96},{64,0},{96,32},{1,65},{33,97},{65,1},{97,33},{2,66}... | collective-permute-start | bytes 442376 | tf_op jit(solution)/shard_map/combine/ppermute | solution.py:40
  64.0 3.0 %collective-permute-done.6.o1 = bf16[64,1152]{1,0:T(8,128)(2,1)S(1)} collective-permute-done((bf16[64,1152]{1,0:T(8,128)(2,1)S(1)}, bf16[64,1152]{1,0:T(8,128)(2,1)S(1)}, u32[]{:S(2)}, u32[]{:S(2)}) %collective-permute-start.6) | collective-permute-done | bytes 147488 | tf_op jit(solution)/shard_map/combine/ppermute | solution.py:40
  67.0 4.0 %collective-permute-start.8 = (bf16[64,1152]{1,0:T(8,128)(2,1)S(1)}, bf16[64,1152]{1,0:T(8,128)(2,1)S(1)}, u32[]{:S(2)}, u32[]{:S(2)}) collective-permute-start(bf16[64,1152]{1,0:T(8,128)(2,1)S(1)} %get-tuple-element.63), channel_id=1, source_target_pairs={{0,96},{32,0},{64,32},{96,64},{1,97},{33,1},{65,33},{97,65},{2,98}... | collective-permute-start | bytes 442376 | tf_op jit(solution)/shard_map/combine/ppermute | solution.py:40
  71.2 5.3 %stage.1.w_ref = bf16[1024,7168]{1,0:T(8,128)(2,1)S(1)} custom-call(bf16[64,1152]{1,0:T(8,128)(2,1)} %copy-done.2, bf16[1024,7168]{1,0:T(8,128)(2,1)} %w_ref.1), custom_call_target="tpu_custom_call" | custom-call | bytes 1 | tf_op jit(solution)/shard_map/combine/stage/pallas_call | solution.py:252
  77.1 2.0 project.2
  79.1 2.0 project.3
  81.7 0.8 collective-permute-done.17.refs_1_
  82.7 1.0 pad_maximum_fusion.3.refs_0_
  84.2 1.3 collective-permute-start.18
  85.5 0.9 collective-permute-start.15
  86.4 4.2 %collective-permute-start.16 = (bf16[32,1792]{1,0:T(8,128)(2,1)S(1)}, bf16[32,1792]{1,0:T(8,128)(2,1)S(1)}, u32[]{:S(2)}, u32[]{:S(2)}) collective-permute-start(bf16[32,1792]{1,0:T(8,128)(2,1)S(1)} %get-tuple-element.76), channel_id=1, source_target_pairs={{0,4},{2,6},{4,0},{6,2},{1,5},{3,7},{5,1},{7,3},{8,12},{10,14},{12... | collective-permute-start | bytes 344072 | tf_op jit(solution)/shard_map/out_projection/ppermute | solution.py:40
  91.2 0.8 broadcast_divide_fusion
  92.4 1.0 collective-permute-done.16.p2
  93.4 1.6 spread.1
  95.1 4.3 %all-to-all-start.1 = ((bf16[16,24,1792]{2,1,0:T(8,128)(2,1)}), bf16[16,24,1792]{2,1,0:T(8,128)(2,1)}, u32[]{:S(2)}, u32[]{:S(2)}) async-start(bf16[16,24,1792]{2,1,0:T(8,128)(2,1)} %bitcast.32), calls=%async_computation.1 | async-start | bytes 2752512 | tf_op jit(solution)/shard_map/dispatch/all_to_all | solution.py:532
  100.0 2.1 %collective-permute-start.23 = (bf16[128,1792]{1,0:T(8,128)(2,1)}, bf16[128,1792]{1,0:T(8,128)(2,1)S(1)}, u32[]{:S(2)}, u32[]{:S(2)}) collective-permute-start(bf16[128,1792]{1,0:T(8,128)(2,1)} %get-tuple-element.99), channel_id=1, source_target_pairs={{0,2},{2,4},{4,6},{6,0},{1,3},{3,5},{5,7},{7,1},{8,10},{10,12},{12... | collective-permute-start | bytes 1376264 | tf_op jit(solution)/shard_map/dispatch/ppermute | solution.py:40
  102.1 3.6 %collective-permute-start.24 = (bf16[128,1792]{1,0:T(8,128)(2,1)}, bf16[128,1792]{1,0:T(8,128)(2,1)S(1)}, u32[]{:S(2)}, u32[]{:S(2)}) collective-permute-start(bf16[128,1792]{1,0:T(8,128)(2,1)} %get-tuple-element.100), channel_id=1, source_target_pairs={{0,4},{2,6},{4,0},{6,2},{1,5},{3,7},{5,1},{7,3},{8,12},{10,14},{12... | collective-permute-start | bytes 1376264 | tf_op jit(solution)/shard_map/dispatch/ppermute | solution.py:40
  106.6 10.4 %all-to-all-done.1 = bf16[16,24,1792]{2,1,0:T(8,128)(2,1)} async-done(((bf16[16,24,1792]{2,1,0:T(8,128)(2,1)}), bf16[16,24,1792]{2,1,0:T(8,128)(2,1)}, u32[]{:S(2)}, u32[]{:S(2)}) %all-to-all-start.1) | async-done | bytes 1376288 | tf_op jit(solution)/shard_map/dispatch/all_to_all | solution.py:532
  117.0 7.7 %gate_up.1 = bf16[4,400,512]{2,1,0:T(8,128)(2,1)} custom-call(s32[1]{0:T(128)} %bitcast.1.z_ref, bf16[384,1792]{1,0:T(8,128)(2,1)} %bitcast.33.x_ref, f32[1,1792]{1,0:T(1,128)} %div.36.gain_ref, bf16[1792,256]{1,0:T(8,128)(2,1)} %pad_maximum_fusion.3.refs_0_, bf16[1792,256]{1,0:T(8,128)(2,1)} %collective-permute-done.19.refs_1_, ...), custom_call_target="tpu_custom_call" | custom-call | bytes 1 | tf_op jit(solution)/shard_map/experts/gate_up/pallas_call | solution.py:375
  124.7 1.5 collective-permute-done.25.refs_6_
  126.2 0.8 copy-done.4
  127.0 5.9 %all-to-all-start.2 = ((bf16[4,400,512]{2,1,0:T(8,128)(2,1)}), bf16[4,400,512]{2,1,0:T(8,128)(2,1)S(1)}, u32[]{:S(2)}, u32[]{:S(2)}) async-start(bf16[4,400,512]{2,1,0:T(8,128)(2,1)} %gate_up.1), calls=%async_computation.2 | async-start | bytes 3276800 | tf_op jit(solution)/shard_map/experts/all_to_all | solution.py:541
  133.9 18.4 %all-to-all-done.2.part_ref = bf16[4,400,512]{2,1,0:T(8,128)(2,1)S(1)} async-done(((bf16[4,400,512]{2,1,0:T(8,128)(2,1)}), bf16[4,400,512]{2,1,0:T(8,128)(2,1)S(1)}, u32[]{:S(2)}, u32[]{:S(2)}) %all-to-all-start.2) | async-done | bytes 1638432 | tf_op jit(solution)/shard_map/experts/all_to_all | solution.py:541
  152.9 3.5 %collective-permute-start.27 = (bf16[384,256]{1,0:T(8,128)(2,1)S(1)}, bf16[384,256]{1,0:T(8,128)(2,1)S(1)}, u32[]{:S(2)}, u32[]{:S(2)}) collective-permute-start(bf16[384,256]{1,0:T(8,128)(2,1)S(1)} %inner_act.1.i0), channel_id=1, source_target_pairs={{0,4},{2,6},{4,0},{6,2},{1,5},{3,7},{5,1},{7,3},{8,12},{10,14},{12... | collective-permute-start | bytes 589832 | tf_op jit(solution)/shard_map/experts/ppermute | solution.py:40
  157.0 2.3 %down_weights.1.w = bf16[1024,1792]{1,0:T(8,128)(2,1)S(1)} custom-call(bf16[128,1792]{1,0:T(8,128)(2,1)S(1)} %get-tuple-element.107.refs_0_, bf16[128,1792]{1,0:T(8,128)(2,1)} %collective-permute-done.29.refs_1_, bf16[128,1792]{1,0:T(8,128)(2,1)S(1)} %collective-permute-done.23.refs_2_, bf16[128,1792]{1,0:T(8,128)(2,1)} %collective-permute-done.30.refs_3_, ...), custom_call_target="tpu_custom_call" | custom-call | bytes 1 | tf_op jit(solution)/shard_map/experts/down_weights/pallas_call | solution.py:336
  160.0 1.7 collective-permute-done.27.i2
  161.7 2.0 collective-permute-done.28.i3
  163.7 1.6 down.1
  165.3 26.5 %all_to_all.25 = bf16[16,24,1792]{2,1,0:T(8,128)(2,1)S(1)} all-to-all(bf16[16,24,1792]{2,1,0:T(8,128)(2,1)S(1)} %bitcast.64), channel_id=1, replica_groups=mesh['y'=4,'x'=4,'z'=4,'core'=2] {'y','x'}, dimensions={0} | all-to-all | bytes 2752512 | tf_op jit(solution)/shard_map/return/all_to_all | solution.py:548
  192.5 10.3 %all_to_all.26 = bf16[4,8,1792]{2,1,0:T(8,128)(2,1)S(1)} all-to-all(bf16[4,8,1792]{2,1,0:T(8,128)(2,1)S(1)} %fusion), channel_id=1, replica_groups=mesh['y'=4,'x'=4,'z'=4,'core'=2] {'z'}, dimensions={0} | all-to-all | bytes 229376 | tf_op jit(solution)/shard_map/return/all_to_all | solution.py:553
  (120 shorter events, 13.0 us)
Async XLA Ops:
  0.0 7.9 %slice-start = ((bf16[8,64,192]{2,1,0:T(8,128)(2,1)}), bf16[8,64,128]{2,1,0:T(8,128)(2,1)S(1)}, s32[]{:S(2)}) async-start(bf16[8,64,192]{2,1,0:T(8,128)(2,1)} %param.13), calls=%async_computation.5 | async-start | bytes 262144 | tf_op jit(solution)/shard_map/query_exchange/slice | solution.py:459
  0.0 8.0 %slice-start.1 = ((bf16[8,64,192]{2,1,0:T(8,128)(2,1)}), bf16[8,64,64]{2,1,0:T(8,128)(2,1)S(1)}, s32[]{:S(2)}) async-start(bf16[8,64,192]{2,1,0:T(8,128)(2,1)} %param.13), calls=%async_computation.6 | async-start | bytes 262144 | tf_op jit(solution)/shard_map/query_exchange/slice | solution.py:460
  0.0 7.9 %copy-start.14 = (f32[8,8]{1,0:T(8,128)S(1)}, f32[8,8]{1,0:T(8,128)}, u32[]{:S(2)}) copy-start(f32[8,8]{1,0:T(8,128)} %param.21) | copy-start | bytes 772
  0.0 7.9 %copy-start.13 = (s32[8,8]{1,0:T(8,128)S(1)}, s32[8,8]{1,0:T(8,128)}, u32[]{:S(2)}) copy-start(s32[8,8]{1,0:T(8,128)} %param.20) | copy-start | bytes 772
  0.0 8.1 %copy-start.12 = (s32[1024]{0:T(1024)S(1)}, s32[1024]{0:T(1024)}, u32[]{:S(2)}) copy-start(s32[1024]{0:T(1024)} %param.22) | copy-start | bytes 12292
  2.2 12.9 %collective-permute-start = (bf16[256,576]{1,0:T(8,128)(2,1)}, bf16[256,576]{1,0:T(8,128)(2,1)S(1)}, u32[]{:S(2)}, u32[]{:S(2)}) collective-permute-start(bf16[256,576]{1,0:T(8,128)(2,1)} %constant_dynamic-slice_fusion.2), channel_id=1, source_target_pairs={{0,8},{8,16},{16,24},{24,0},{1,9},{9,17},{17,25},{25,1},{2,10},{10... | collective-permute-start | bytes 884744 | tf_op jit(solution)/shard_map/cache_gather/ppermute | solution.py:40
  3.7 23.8 %collective-permute-start.1 = (bf16[256,576]{1,0:T(8,128)(2,1)}, bf16[256,576]{1,0:T(8,128)(2,1)}, u32[]{:S(2)}, u32[]{:S(2)}) collective-permute-start(bf16[256,576]{1,0:T(8,128)(2,1)} %constant_dynamic-slice_fusion.2), channel_id=1, source_target_pairs={{0,16},{8,24},{16,0},{24,8},{1,17},{9,25},{17,1},{25,9},{2,18},{10... | collective-permute-start | bytes 884744 | tf_op jit(solution)/shard_map/cache_gather/ppermute | solution.py:40
  6.5 21.4 %collective-permute-start.2 = (bf16[256,576]{1,0:T(8,128)(2,1)}, bf16[256,576]{1,0:T(8,128)(2,1)}, u32[]{:S(2)}, u32[]{:S(2)}) collective-permute-start(bf16[256,576]{1,0:T(8,128)(2,1)} %constant_dynamic-slice_fusion.2), channel_id=1, source_target_pairs={{0,24},{8,0},{16,8},{24,16},{1,25},{9,1},{17,9},{25,17},{2,26},{10... | collective-permute-start | bytes 884744 | tf_op jit(solution)/shard_map/cache_gather/ppermute | solution.py:40
  15.1 12.1 %copy-start.7 = (bf16[256,576]{1,0:T(8,128)(2,1)}, bf16[256,576]{1,0:T(8,128)(2,1)S(1)}, u32[]{:S(2)}) copy-start(bf16[256,576]{1,0:T(8,128)(2,1)S(1)} %collective-permute-done.c1) | copy-start | bytes 884740
  16.2 20.4 %all-to-all-start = ((bf16[32,8,1664]{2,1,0:T(8,128)(2,1)}), bf16[32,8,1664]{2,1,0:T(8,128)(2,1)S(1)}, u32[]{:S(2)}, u32[]{:S(2)}) async-start(bf16[32,8,1664]{2,1,0:T(8,128)(2,1)} %bitcast.11), calls=%async_computation | async-start | bytes 1703936 | tf_op jit(solution)/shard_map/query_exchange/all_to_all | solution.py:465
  24.4 16.9 %copy-start = (bf16[8,128,512]{2,1,0:T(8,128)(2,1)S(1)}, bf16[8,128,512]{2,1,0:T(8,128)(2,1)}, u32[]{:S(2)}) copy-start(bf16[8,128,512]{2,1,0:T(8,128)(2,1)} %ak_ref.1) | copy-start | bytes 3145732
  27.3 12.9 %collective-permute-start.3 = (bf16[256,576]{1,0:T(8,128)(2,1)S(1)}, bf16[256,576]{1,0:T(8,128)(2,1)}, u32[]{:S(2)}, u32[]{:S(2)}) collective-permute-start(bf16[256,576]{1,0:T(8,128)(2,1)S(1)} %collective-permute-done.c1), channel_id=1, source_target_pairs={{0,1},{1,0},{2,3},{3,2},{4,5},{5,4},{6,7},{7,6},{8,9},{9,8},{10,11... | collective-permute-start | bytes 884744 | tf_op jit(solution)/shard_map/cache_share/ppermute | solution.py:40
  27.5 13.7 %collective-permute-start.4 = (bf16[256,576]{1,0:T(8,128)(2,1)}, bf16[256,576]{1,0:T(8,128)(2,1)}, u32[]{:S(2)}, u32[]{:S(2)}) collective-permute-start(bf16[256,576]{1,0:T(8,128)(2,1)} %collective-permute-done.1.c2), channel_id=1, source_target_pairs={{0,1},{1,0},{2,3},{3,2},{4,5},{5,4},{6,7},{7,6},{8,9},{9,8},{10,11... | collective-permute-start | bytes 884744 | tf_op jit(solution)/shard_map/cache_share/ppermute | solution.py:40
  27.9 13.3 %collective-permute-start.5 = (bf16[256,576]{1,0:T(8,128)(2,1)}, bf16[256,576]{1,0:T(8,128)(2,1)}, u32[]{:S(2)}, u32[]{:S(2)}) collective-permute-start(bf16[256,576]{1,0:T(8,128)(2,1)} %collective-permute-done.2.c3), channel_id=1, source_target_pairs={{0,1},{1,0},{2,3},{3,2},{4,5},{5,4},{6,7},{7,6},{8,9},{9,8},{10,11... | collective-permute-start | bytes 884744 | tf_op jit(solution)/shard_map/cache_share/ppermute | solution.py:40
  36.6 48.9 %collective-permute-start.10 = (bf16[1792,256]{1,0:T(8,128)(2,1)}, bf16[1792,256]{1,0:T(8,128)(2,1)}, u32[]{:S(2)}, u32[]{:S(2)}) collective-permute-start(bf16[1792,256]{1,0:T(8,128)(2,1)} %pad_maximum_fusion.1), channel_id=1, source_target_pairs={{0,4},{2,6},{4,0},{6,2},{1,5},{3,7},{5,1},{7,3},{8,12},{10,14},{12... | collective-permute-start | bytes 2752520 | tf_op jit(solution)/shard_map/attention/ppermute | solution.py:40
  38.7 47.7 %collective-permute-start.11 = (bf16[1792,256]{1,0:T(8,128)(2,1)}, bf16[1792,256]{1,0:T(8,128)(2,1)}, u32[]{:S(2)}, u32[]{:S(2)}) collective-permute-start(bf16[1792,256]{1,0:T(8,128)(2,1)} %pad_maximum_fusion.2), channel_id=1, source_target_pairs={{0,6},{2,0},{4,2},{6,4},{1,7},{3,1},{5,3},{7,5},{8,14},{10,8},{12,... | collective-permute-start | bytes 2752520 | tf_op jit(solution)/shard_map/attention/ppermute | solution.py:40
  40.2 50.5 %collective-permute-start.9 = (bf16[1792,256]{1,0:T(8,128)(2,1)}, bf16[1792,256]{1,0:T(8,128)(2,1)}, u32[]{:S(2)}, u32[]{:S(2)}) collective-permute-start(bf16[1792,256]{1,0:T(8,128)(2,1)} %pad_maximum_fusion), channel_id=1, source_target_pairs={{0,2},{2,4},{4,6},{6,0},{1,3},{3,5},{5,7},{7,1},{8,10},{10,12},{12... | collective-permute-start | bytes 2752520 | tf_op jit(solution)/shard_map/attention/ppermute | solution.py:40
  60.6 6.5 %collective-permute-start.6 = (bf16[64,1152]{1,0:T(8,128)(2,1)S(1)}, bf16[64,1152]{1,0:T(8,128)(2,1)S(1)}, u32[]{:S(2)}, u32[]{:S(2)}) collective-permute-start(bf16[64,1152]{1,0:T(8,128)(2,1)S(1)} %get-tuple-element.61), channel_id=1, source_target_pairs={{0,32},{32,64},{64,96},{96,0},{1,33},{33,65},{65,97},{97,1},{2,34}... | collective-permute-start | bytes 442376 | tf_op jit(solution)/shard_map/combine/ppermute | solution.py:40
  61.3 15.2 %collective-permute-start.7 = (bf16[64,1152]{1,0:T(8,128)(2,1)S(1)}, bf16[64,1152]{1,0:T(8,128)(2,1)S(1)}, u32[]{:S(2)}, u32[]{:S(2)}) collective-permute-start(bf16[64,1152]{1,0:T(8,128)(2,1)S(1)} %get-tuple-element.62), channel_id=1, source_target_pairs={{0,64},{32,96},{64,0},{96,32},{1,65},{33,97},{65,1},{97,33},{2,66}... | collective-permute-start | bytes 442376 | tf_op jit(solution)/shard_map/combine/ppermute | solution.py:40
  67.0 9.5 %collective-permute-start.8 = (bf16[64,1152]{1,0:T(8,128)(2,1)S(1)}, bf16[64,1152]{1,0:T(8,128)(2,1)S(1)}, u32[]{:S(2)}, u32[]{:S(2)}) collective-permute-start(bf16[64,1152]{1,0:T(8,128)(2,1)S(1)} %get-tuple-element.63), channel_id=1, source_target_pairs={{0,96},{32,0},{64,32},{96,64},{1,97},{33,1},{65,33},{97,65},{2,98}... | collective-permute-start | bytes 442376 | tf_op jit(solution)/shard_map/combine/ppermute | solution.py:40
  71.2 5.4 %copy-start.3 = (bf16[64,1152]{1,0:T(8,128)(2,1)S(1)}, bf16[64,1152]{1,0:T(8,128)(2,1)}, u32[]{:S(2)}) copy-start(bf16[64,1152]{1,0:T(8,128)(2,1)} %copy-done.2) | copy-start | bytes 442372
  71.2 6.0 %copy-start.6 = (bf16[8,7168]{1,0:T(8,128)(2,1)S(1)}, bf16[8,7168]{1,0:T(8,128)(2,1)}, u32[]{:S(2)}) copy-start(bf16[8,7168]{1,0:T(8,128)(2,1)} %res_ref.3) | copy-start | bytes 344068
  79.1 3.6 %copy-start.9 = (bf16[1792,128]{1,0:T(8,128)(2,1)S(1)}, bf16[1792,128]{1,0:T(8,128)(2,1)}, u32[]{:S(2)}) copy-start(bf16[1792,128]{1,0:T(8,128)(2,1)} %get-tuple-element.117) | copy-start | bytes 1376260
  81.1 1.4 collective-permute-start.17
  81.2 2.5 %collective-permute-start.13 = (bf16[32,1792]{1,0:T(8,128)(2,1)S(1)}, bf16[32,1792]{1,0:T(8,128)(2,1)S(1)}, u32[]{:S(2)}, u32[]{:S(2)}) collective-permute-start(bf16[32,1792]{1,0:T(8,128)(2,1)S(1)} %get-tuple-element.64), channel_id=1, source_target_pairs={{0,1},{1,0},{2,3},{3,2},{4,5},{5,4},{6,7},{7,6},{8,9},{9,8},{10,11... | collective-permute-start | bytes 344072 | tf_op jit(solution)/shard_map/out_projection/ppermute | solution.py:40
  82.5 1.6 collective-permute-start.14
  83.7 7.0 %collective-permute-start.12 = (bf16[32,1792]{1,0:T(8,128)(2,1)S(1)}, bf16[32,1792]{1,0:T(8,128)(2,1)S(1)}, u32[]{:S(2)}, u32[]{:S(2)}) collective-permute-start(bf16[32,1792]{1,0:T(8,128)(2,1)S(1)} %get-tuple-element.71), channel_id=1, source_target_pairs={{0,1},{1,0},{2,3},{3,2},{4,5},{5,4},{6,7},{7,6},{8,9},{9,8},{10,11... | collective-permute-start | bytes 344072 | tf_op jit(solution)/shard_map/out_projection/ppermute | solution.py:40
  84.2 8.3 %collective-permute-start.18 = (bf16[32,1792]{1,0:T(8,128)(2,1)S(1)}, bf16[32,1792]{1,0:T(8,128)(2,1)S(1)}, u32[]{:S(2)}, u32[]{:S(2)}) collective-permute-start(bf16[32,1792]{1,0:T(8,128)(2,1)S(1)} %fold.3), channel_id=1, source_target_pairs={{0,6},{2,0},{4,2},{6,4},{1,7},{3,1},{5,3},{7,5},{8,14},{10,8},{12,... | collective-permute-start | bytes 344072 | tf_op jit(solution)/shard_map/out_projection/ppermute | solution.py:40
  85.5 6.9 %collective-permute-start.15 = (bf16[32,1792]{1,0:T(8,128)(2,1)S(1)}, bf16[32,1792]{1,0:T(8,128)(2,1)S(1)}, u32[]{:S(2)}, u32[]{:S(2)}) collective-permute-start(bf16[32,1792]{1,0:T(8,128)(2,1)S(1)} %get-tuple-element.75), channel_id=1, source_target_pairs={{0,2},{2,4},{4,6},{6,0},{1,3},{3,5},{5,7},{7,1},{8,10},{10,12},{12... | collective-permute-start | bytes 344072 | tf_op jit(solution)/shard_map/out_projection/ppermute | solution.py:40
  86.4 7.1 %collective-permute-start.16 = (bf16[32,1792]{1,0:T(8,128)(2,1)S(1)}, bf16[32,1792]{1,0:T(8,128)(2,1)S(1)}, u32[]{:S(2)}, u32[]{:S(2)}) collective-permute-start(bf16[32,1792]{1,0:T(8,128)(2,1)S(1)} %get-tuple-element.76), channel_id=1, source_target_pairs={{0,4},{2,6},{4,0},{6,2},{1,5},{3,7},{5,1},{7,3},{8,12},{10,14},{12... | collective-permute-start | bytes 344072 | tf_op jit(solution)/shard_map/out_projection/ppermute | solution.py:40
  90.6 11.5 %collective-permute-start.19 = (bf16[1792,256]{1,0:T(8,128)(2,1)}, bf16[1792,256]{1,0:T(8,128)(2,1)}, u32[]{:S(2)}, u32[]{:S(2)}) collective-permute-start(bf16[1792,256]{1,0:T(8,128)(2,1)} %pad_maximum_fusion.3.refs_0_), channel_id=1, source_target_pairs={{0,1},{1,0},{2,3},{3,2},{4,5},{5,4},{6,7},{7,6},{8,9},{9,8},{10,11... | collective-permute-start | bytes 2752520 | tf_op jit(solution)/shard_map/dispatch/ppermute | solution.py:40
  90.7 14.9 %collective-permute-start.20 = (bf16[1792,256]{1,0:T(8,128)(2,1)}, bf16[1792,256]{1,0:T(8,128)(2,1)}, u32[]{:S(2)}, u32[]{:S(2)}) collective-permute-start(bf16[1792,256]{1,0:T(8,128)(2,1)} %collective-permute-done.9.refs_2_), channel_id=1, source_target_pairs={{0,1},{1,0},{2,3},{3,2},{4,5},{5,4},{6,7},{7,6},{8,9},{9,8},{10,11... | collective-permute-start | bytes 2752520 | tf_op jit(solution)/shard_map/dispatch/ppermute | solution.py:40
  95.1 21.9 %all-to-all-start.1 = ((bf16[16,24,1792]{2,1,0:T(8,128)(2,1)}), bf16[16,24,1792]{2,1,0:T(8,128)(2,1)}, u32[]{:S(2)}, u32[]{:S(2)}) async-start(bf16[16,24,1792]{2,1,0:T(8,128)(2,1)} %bitcast.32), calls=%async_computation.1 | async-start | bytes 2752512 | tf_op jit(solution)/shard_map/dispatch/all_to_all | solution.py:532
  99.4 7.2 %collective-permute-start.21 = (bf16[1792,256]{1,0:T(8,128)(2,1)}, bf16[1792,256]{1,0:T(8,128)(2,1)S(1)}, u32[]{:S(2)}, u32[]{:S(2)}) collective-permute-start(bf16[1792,256]{1,0:T(8,128)(2,1)} %collective-permute-done.10.refs_4_), channel_id=1, source_target_pairs={{0,1},{1,0},{2,3},{3,2},{4,5},{5,4},{6,7},{7,6},{8,9},{9,8},{10,11... | collective-permute-start | bytes 2752520 | tf_op jit(solution)/shard_map/dispatch/ppermute | solution.py:40
  99.5 7.1 %collective-permute-start.22 = (bf16[1792,256]{1,0:T(8,128)(2,1)}, bf16[1792,256]{1,0:T(8,128)(2,1)}, u32[]{:S(2)}, u32[]{:S(2)}) collective-permute-start(bf16[1792,256]{1,0:T(8,128)(2,1)} %collective-permute-done.11.refs_6_), channel_id=1, source_target_pairs={{0,1},{1,0},{2,3},{3,2},{4,5},{5,4},{6,7},{7,6},{8,9},{9,8},{10,11... | collective-permute-start | bytes 2752520 | tf_op jit(solution)/shard_map/dispatch/ppermute | solution.py:40
  100.0 24.7 %collective-permute-start.23 = (bf16[128,1792]{1,0:T(8,128)(2,1)}, bf16[128,1792]{1,0:T(8,128)(2,1)S(1)}, u32[]{:S(2)}, u32[]{:S(2)}) collective-permute-start(bf16[128,1792]{1,0:T(8,128)(2,1)} %get-tuple-element.99), channel_id=1, source_target_pairs={{0,2},{2,4},{4,6},{6,0},{1,3},{3,5},{5,7},{7,1},{8,10},{10,12},{12... | collective-permute-start | bytes 1376264 | tf_op jit(solution)/shard_map/dispatch/ppermute | solution.py:40
  102.1 22.6 %collective-permute-start.24 = (bf16[128,1792]{1,0:T(8,128)(2,1)}, bf16[128,1792]{1,0:T(8,128)(2,1)S(1)}, u32[]{:S(2)}, u32[]{:S(2)}) collective-permute-start(bf16[128,1792]{1,0:T(8,128)(2,1)} %get-tuple-element.100), channel_id=1, source_target_pairs={{0,4},{2,6},{4,0},{6,2},{1,5},{3,7},{5,1},{7,3},{8,12},{10,14},{12... | collective-permute-start | bytes 1376264 | tf_op jit(solution)/shard_map/dispatch/ppermute | solution.py:40
  105.7 20.5 %collective-permute-start.25 = (bf16[128,1792]{1,0:T(8,128)(2,1)}, bf16[128,1792]{1,0:T(8,128)(2,1)S(1)}, u32[]{:S(2)}, u32[]{:S(2)}) collective-permute-start(bf16[128,1792]{1,0:T(8,128)(2,1)} %get-tuple-element.101), channel_id=1, source_target_pairs={{0,6},{2,0},{4,2},{6,4},{1,7},{3,1},{5,3},{7,5},{8,14},{10,8},{12,... | collective-permute-start | bytes 1376264 | tf_op jit(solution)/shard_map/dispatch/ppermute | solution.py:40
  106.6 10.4 %copy-start.11 = (bf16[1792,256]{1,0:T(8,128)(2,1)}, bf16[1792,256]{1,0:T(8,128)(2,1)S(1)}, u32[]{:S(2)}) copy-start(bf16[1792,256]{1,0:T(8,128)(2,1)S(1)} %collective-permute-done.21.refs_5_) | copy-start | bytes 2752516
  127.0 25.4 %all-to-all-start.2 = ((bf16[4,400,512]{2,1,0:T(8,128)(2,1)}), bf16[4,400,512]{2,1,0:T(8,128)(2,1)S(1)}, u32[]{:S(2)}, u32[]{:S(2)}) async-start(bf16[4,400,512]{2,1,0:T(8,128)(2,1)} %gate_up.1), calls=%async_computation.2 | async-start | bytes 3276800 | tf_op jit(solution)/shard_map/experts/all_to_all | solution.py:541
  132.9 20.0 %collective-permute-start.29 = (bf16[128,1792]{1,0:T(8,128)(2,1)S(1)}, bf16[128,1792]{1,0:T(8,128)(2,1)}, u32[]{:S(2)}, u32[]{:S(2)}) collective-permute-start(bf16[128,1792]{1,0:T(8,128)(2,1)S(1)} %get-tuple-element.107.refs_0_), channel_id=1, source_target_pairs={{0,1},{1,0},{2,3},{3,2},{4,5},{5,4},{6,7},{7,6},{8,9},{9,8},{10,11... | collective-permute-start | bytes 1376264 | tf_op jit(solution)/shard_map/experts/ppermute | solution.py:40
  132.9 23.5 %collective-permute-start.30 = (bf16[128,1792]{1,0:T(8,128)(2,1)S(1)}, bf16[128,1792]{1,0:T(8,128)(2,1)}, u32[]{:S(2)}, u32[]{:S(2)}) collective-permute-start(bf16[128,1792]{1,0:T(8,128)(2,1)S(1)} %collective-permute-done.23.refs_2_), channel_id=1, source_target_pairs={{0,1},{1,0},{2,3},{3,2},{4,5},{5,4},{6,7},{7,6},{8,9},{9,8},{10,11... | collective-permute-start | bytes 1376264 | tf_op jit(solution)/shard_map/experts/ppermute | solution.py:40
  133.4 23.6 %collective-permute-start.31 = (bf16[128,1792]{1,0:T(8,128)(2,1)S(1)}, bf16[128,1792]{1,0:T(8,128)(2,1)}, u32[]{:S(2)}, u32[]{:S(2)}) collective-permute-start(bf16[128,1792]{1,0:T(8,128)(2,1)S(1)} %collective-permute-done.24.refs_4_), channel_id=1, source_target_pairs={{0,1},{1,0},{2,3},{3,2},{4,5},{5,4},{6,7},{7,6},{8,9},{9,8},{10,11... | collective-permute-start | bytes 1376264 | tf_op jit(solution)/shard_map/experts/ppermute | solution.py:40
  133.4 23.6 %collective-permute-start.32 = (bf16[128,1792]{1,0:T(8,128)(2,1)}, bf16[128,1792]{1,0:T(8,128)(2,1)}, u32[]{:S(2)}, u32[]{:S(2)}) collective-permute-start(bf16[128,1792]{1,0:T(8,128)(2,1)} %copy-done.4), channel_id=1, source_target_pairs={{0,1},{1,0},{2,3},{3,2},{4,5},{5,4},{6,7},{7,6},{8,9},{9,8},{10,11... | collective-permute-start | bytes 1376264 | tf_op jit(solution)/shard_map/experts/ppermute | solution.py:40
  152.4 4.6 %copy-start.5 = (bf16[128,1792]{1,0:T(8,128)(2,1)S(1)}, bf16[128,1792]{1,0:T(8,128)(2,1)}, u32[]{:S(2)}) copy-start(bf16[128,1792]{1,0:T(8,128)(2,1)} %copy-done.4) | copy-start | bytes 1376260
  152.8 7.1 %collective-permute-start.26 = (bf16[384,256]{1,0:T(8,128)(2,1)S(1)}, bf16[384,256]{1,0:T(8,128)(2,1)S(1)}, u32[]{:S(2)}, u32[]{:S(2)}) collective-permute-start(bf16[384,256]{1,0:T(8,128)(2,1)S(1)} %inner_act.1.i0), channel_id=1, source_target_pairs={{0,2},{2,4},{4,6},{6,0},{1,3},{3,5},{5,7},{7,1},{8,10},{10,12},{12... | collective-permute-start | bytes 589832 | tf_op jit(solution)/shard_map/experts/ppermute | solution.py:40
  152.9 8.7 %collective-permute-start.27 = (bf16[384,256]{1,0:T(8,128)(2,1)S(1)}, bf16[384,256]{1,0:T(8,128)(2,1)S(1)}, u32[]{:S(2)}, u32[]{:S(2)}) collective-permute-start(bf16[384,256]{1,0:T(8,128)(2,1)S(1)} %inner_act.1.i0), channel_id=1, source_target_pairs={{0,4},{2,6},{4,0},{6,2},{1,5},{3,7},{5,1},{7,3},{8,12},{10,14},{12... | collective-permute-start | bytes 589832 | tf_op jit(solution)/shard_map/experts/ppermute | solution.py:40
  156.5 7.2 %collective-permute-start.28 = (bf16[384,256]{1,0:T(8,128)(2,1)S(1)}, bf16[384,256]{1,0:T(8,128)(2,1)S(1)}, u32[]{:S(2)}, u32[]{:S(2)}) collective-permute-start(bf16[384,256]{1,0:T(8,128)(2,1)S(1)} %inner_act.1.i0), channel_id=1, source_target_pairs={{0,6},{2,0},{4,2},{6,4},{1,7},{3,1},{5,3},{7,5},{8,14},{10,8},{12,... | collective-permute-start | bytes 589832 | tf_op jit(solution)/shard_map/experts/ppermute | solution.py:40
  (5 other events, 7.2 us)
